TPU v7x, 32 devices: a whole 2x2x4 slice. The times are simulated.
32 devices in a mesh: dp: 8 (over y, x, core), tensor: 4 (over z).
Axes of the slice: x: 2, y: 2, z: 4, core: 2. Of those that a mesh axis runs over, the one named last changes fastest.
Arguments:
- tokens: bfloat16 [36864, 512], P('dp'), may hold values from -6 to 6
- first_gain: float32 [512], replicated, may hold values from 0.5 to 1.5
- second_gain: float32 [512], replicated, may hold values from 0.5 to 1.5
- query_weight: bfloat16 [512, 512], P(None, 'tensor'), may hold values from -0.25 to 0.25
- key_weight: bfloat16 [512, 512], P(None, 'tensor'), may hold values from -0.25 to 0.25
- value_weight: bfloat16 [512, 512], P(None, 'tensor'), may hold values from -0.25 to 0.25
- out_weight: bfloat16 [512, 512], P('tensor'), may hold values from -1.5 to 1.5
- key_conv: bfloat16 [8, 192, 64], P('tensor'), may hold values from -0.4375 to 0.4375
- value_conv: bfloat16 [8, 192, 64], P('tensor'), may hold values from -0.4375 to 0.4375
- up_weight: bfloat16 [512, 2048], P(None, 'tensor'), may hold values from -0.25 to 0.25
- down_weight: bfloat16 [2048, 512], P('tensor'), may hold values from -0.125 to 0.125
- pad_mask: int32 [36864], P('dp'), may hold values 0 or 1
- item_lengths: int32 [8, 6], P('dp'), may hold values from 1 to 768, 1536 in all within a row
- cotangent: bfloat16 [36864, 512], P('dp'), may hold values from -6 to 6
Outputs:
- mixed_out: bfloat16 [36864, 512], P('dp')
- grad_tokens: bfloat16 [36864, 512], P('dp')
- grad_first_gain: float32 [512], P('dp')
- grad_second_gain: float32 [512], P('dp')
- grad_query: float32 [512, 512], P('dp', 'tensor')
- grad_key: float32 [512, 512], P('dp', 'tensor')
- grad_value: float32 [512, 512], P('dp', 'tensor')
- grad_out: float32 [512, 512], P('tensor', 'dp')
- grad_key_conv: float32 [8, 192, 64], P('tensor', 'dp')
- grad_value_conv: float32 [8, 192, 64], P('tensor', 'dp')
- grad_up: float32 [512, 2048], P('dp', 'tensor')
- grad_down: float32 [2048, 512], P('tensor', 'dp')
Inputs may be any that keep to these rules, and one draw needn't show every extreme that they name: `item_lengths`: each row sums to 1536 and its largest entry is 768.
All inputs are finite; a program needn't handle non-finite values. No bound on the sum of `pad_mask` on one device may be relied on, other than what follows from the above.
Results may differ from a plain program's by a relative error of at most 0.019.
Values may be sent and summed in bfloat16 or wider, within the bound.
A program may use at most 256 MiB of HBM per device.

v0:
```python
import math

import jax
import jax.numpy as jnp
from jax import lax
from jax.sharding import PartitionSpec as P


def in_blocks(shard, dim, count):
    dims = shard.shape
    parts = shard.reshape(*dims[:dim], count, dims[dim] // count, *dims[dim + 1 :])
    return jnp.moveaxis(parts, dim, 0)


def sent_and_summed(shard, axis, dim):
    count = lax.axis_size(axis)
    parts = lax.all_to_all(in_blocks(shard, dim, count), axis, 0, 0, tiled=True)
    return jnp.sum(parts.astype(jnp.float32), axis=0)


def side_by_side(arrays, axis, dim, along):
    widths = [math.prod(a.shape[along:]) for a in arrays]
    both = jnp.concatenate(
        [a.reshape(*a.shape[:along], w) for a, w in zip(arrays, widths)], axis=along
    )
    whole = sent_and_summed(both, axis, dim)
    parts = jnp.split(whole, [sum(widths[:k]) for k in range(1, len(widths))], axis=along)
    return tuple((b.reshape(*whole.shape[:along], *a.shape[along:]) for a, b in zip(arrays, parts)))


def sent_together(arrays, axis, dim, along):
    widths = [a.shape[along] for a in arrays]
    both = jnp.concatenate(arrays, axis=along)
    whole = sent_and_summed(both, axis, dim)
    return tuple(jnp.split(whole, [sum(widths[:k]) for k in range(1, len(widths))], axis=along))


def norm_rows(values, gains):
    centred = values - jnp.mean(values, -1, keepdims=True)
    variance = jnp.mean(centred * centred, -1, keepdims=True)
    inv_std = lax.rsqrt(variance + 1e-05)
    normed = centred * inv_std
    return (normed * gains, normed, inv_std)


def norm_back(grad_out, gains, normed, inv_std):
    scaled = grad_out * gains
    return inv_std * (
        scaled
        - jnp.mean(scaled, -1, keepdims=True)
        - normed * jnp.mean(scaled * normed, -1, keepdims=True)
    )


def outer_sum(left_side, right_side):
    return lax.dot_general(
        left_side, right_side, (((0,), (0,)), ((), ())), preferred_element_type=jnp.float32
    )


def times_trans(left_side, weight):
    return lax.dot_general(
        left_side, weight, (((1,), (1,)), ((), ())), preferred_element_type=jnp.float32
    )


def items_of(lengths, count):
    ends = jnp.cumsum(lengths * 3)
    places = jnp.arange(count, dtype=jnp.int32)
    return jnp.sum((places[:, None] >= ends[None, :]).astype(jnp.int32), axis=1)


def exact_gelu(values):
    return jax.nn.gelu(values, approximate=False)


def block_scores(
    block_queries, block_keys, block_places, block_items, comp_keys, group_item, factor
):
    starts = 3 * jnp.arange(group_item.shape[0], dtype=jnp.int32)
    own_score = (
        jnp.sum(block_queries.astype(jnp.float32) * block_keys.astype(jnp.float32), -1).T * factor
    )
    key_score = (
        jnp.einsum("qhd,hjd->hqj", block_queries, comp_keys, preferred_element_type=jnp.float32)
        * factor
    )
    allowed = (block_items[:, None] == group_item[None, :]) & (
        starts[None, :] + 2 < block_places[:, None]
    )
    return (own_score, jnp.where(allowed[None], key_score, -1e30))


def attend_forward(
    queries, keys, values, comp_keys, comp_values, places, item_rows, group_item, block_rows, factor
):
    rows, heads, size = queries.shape
    count = rows // block_rows

    def forward_block(block_inputs):
        block_queries, block_keys, block_values, block_places, block_items = block_inputs
        own_score, key_score = block_scores(
            block_queries, block_keys, block_places, block_items, comp_keys, group_item, factor
        )
        top_score = jnp.maximum(own_score, jnp.max(key_score, -1))
        own_prob = jnp.exp(own_score - top_score)
        key_prob = jnp.exp(key_score - top_score[..., None])
        total = own_prob + jnp.sum(key_prob, -1)
        own_prob = own_prob / total
        key_prob = key_prob / total[..., None]
        context = own_prob[..., None] * block_values.astype(jnp.float32).transpose(1, 0, 2)
        context = context + jnp.einsum(
            "hqj,hjd->hqd",
            key_prob.astype(jnp.bfloat16),
            comp_values,
            preferred_element_type=jnp.float32,
        )
        return (context.transpose(1, 0, 2), top_score + jnp.log(total))

    def split_blocks(array):
        return array.reshape((count, block_rows) + array.shape[1:])

    contexts, log_totals = lax.map(
        forward_block,
        (
            split_blocks(queries),
            split_blocks(keys),
            split_blocks(values),
            split_blocks(places),
            split_blocks(item_rows),
        ),
    )
    return (contexts.reshape(rows, heads * size), log_totals)


def attend_backward(
    queries,
    keys,
    values,
    comp_keys,
    comp_values,
    places,
    item_rows,
    group_item,
    block_rows,
    factor,
    log_totals,
    context_grad,
):
    rows, heads, size = queries.shape
    count = rows // block_rows

    def backward_block(carry, block_inputs):
        comp_key_sum, comp_value_sum = carry
        (
            block_queries,
            block_keys,
            block_values,
            block_places,
            block_items,
            block_lse,
            block_grad,
        ) = block_inputs
        own_score, key_score = block_scores(
            block_queries, block_keys, block_places, block_items, comp_keys, group_item, factor
        )
        own_prob = jnp.exp(own_score - block_lse)
        key_prob = jnp.exp(key_score - block_lse[..., None])
        grad_float = block_grad.astype(jnp.float32).transpose(1, 0, 2)
        own_dprob = jnp.sum(grad_float * block_values.astype(jnp.float32).transpose(1, 0, 2), -1)
        key_dprob = jnp.einsum(
            "qhd,hjd->hqj", block_grad, comp_values, preferred_element_type=jnp.float32
        )
        delta = own_prob * own_dprob + jnp.sum(key_prob * key_dprob, -1)
        own_dscore = own_prob * (own_dprob - delta)
        key_dscore = (key_prob * (key_dprob - delta[..., None])).astype(jnp.bfloat16)
        query_part = own_dscore[..., None] * block_keys.astype(jnp.float32).transpose(1, 0, 2)
        query_part = factor * (
            query_part
            + jnp.einsum("hqj,hjd->hqd", key_dscore, comp_keys, preferred_element_type=jnp.float32)
        )
        own_key_part = (
            factor * own_dscore[..., None] * block_queries.astype(jnp.float32).transpose(1, 0, 2)
        )
        own_value_part = own_prob[..., None] * grad_float
        comp_key_sum = comp_key_sum + factor * jnp.einsum(
            "hqj,qhd->hjd", key_dscore, block_queries, preferred_element_type=jnp.float32
        )
        comp_value_sum = comp_value_sum + jnp.einsum(
            "hqj,qhd->hjd",
            key_prob.astype(jnp.bfloat16),
            block_grad,
            preferred_element_type=jnp.float32,
        )
        return (
            (comp_key_sum, comp_value_sum),
            (
                query_part.transpose(1, 0, 2),
                own_key_part.transpose(1, 0, 2),
                own_value_part.transpose(1, 0, 2),
            ),
        )

    def split_blocks(array):
        return array.reshape((count, block_rows) + array.shape[1:])

    zero_comp = jnp.zeros((heads, comp_keys.shape[1], size), jnp.float32)
    sums, parts = lax.scan(
        backward_block,
        (zero_comp, zero_comp),
        (
            split_blocks(queries),
            split_blocks(keys),
            split_blocks(values),
            split_blocks(places),
            split_blocks(item_rows),
            log_totals,
            split_blocks(context_grad),
        ),
    )
    width = heads * size
    return (sums, tuple((part.reshape(rows, width) for part in parts)))


def on_device(
    tokens,
    first_gain,
    second_gain,
    query_weight,
    key_weight,
    value_weight,
    out_weight,
    key_conv,
    value_conv,
    up_weight,
    down_weight,
    pad_mask,
    item_lengths,
    cotangent,
):
    tok_rows = tokens.shape[0]
    head_size = key_conv.shape[2]
    factor = 1.0 / math.sqrt(head_size)
    item_all = items_of(item_lengths[0], tok_rows)
    group_item = item_all.reshape(tok_rows // 3, 3)[:, 0]
    query_w, key_w, value_w, up_w, out_w, key_kernel, value_kernel, down_w = (
        query_weight,
        key_weight,
        value_weight,
        up_weight,
        out_weight,
        key_conv,
        value_conv,
        down_weight,
    )
    row_tokens, row_mask, row_items, row_cotangent = (tokens, pad_mask, item_all, cotangent)
    block_rows = min(512, tok_rows)
    local_heads = key_kernel.shape[0]
    width = local_heads * head_size
    own_groups = tok_rows // 3
    places = jnp.arange(tok_rows, dtype=jnp.int32)
    real_mask = row_mask.astype(jnp.float32)[:, None]
    mask_low = row_mask.astype(jnp.bfloat16)[:, None]

    def regroup(sequence):
        return (
            sequence.reshape(own_groups, 3, local_heads, head_size)
            .transpose(2, 0, 1, 3)
            .reshape(local_heads, own_groups, 3 * head_size)
        )

    def ungroup(grouped):
        return (
            grouped.reshape(local_heads, own_groups, 3, head_size)
            .transpose(1, 2, 0, 3)
            .reshape(tok_rows, width)
        )

    def by_heads(array):
        return array.reshape(tok_rows, local_heads, head_size)

    inputs = row_tokens.astype(jnp.float32)
    first_norm, first_hat, first_inv = norm_rows(inputs, first_gain)
    first_in = first_norm.astype(jnp.bfloat16)
    queries = jnp.dot(first_in, query_w, preferred_element_type=jnp.float32).astype(jnp.bfloat16)
    keys = (jnp.dot(first_in, key_w, preferred_element_type=jnp.float32) * real_mask).astype(
        jnp.bfloat16
    )
    values = (jnp.dot(first_in, value_w, preferred_element_type=jnp.float32) * real_mask).astype(
        jnp.bfloat16
    )
    key_grouped = regroup(keys)
    value_grouped = regroup(values)
    own_comp_keys = jnp.einsum(
        "hjc,hcd->hjd", key_grouped, key_kernel, preferred_element_type=jnp.float32
    ).astype(jnp.bfloat16)
    own_comp_values = jnp.einsum(
        "hjc,hcd->hjd", value_grouped, value_kernel, preferred_element_type=jnp.float32
    ).astype(jnp.bfloat16)
    comp_keys, comp_values = (own_comp_keys, own_comp_values)
    contexts, log_totals = attend_forward(
        by_heads(queries),
        by_heads(keys),
        by_heads(values),
        comp_keys,
        comp_values,
        places,
        row_items,
        group_item,
        block_rows,
        factor,
    )
    context = contexts.astype(jnp.bfloat16)
    attended = lax.psum(
        jnp.dot(context, out_w, preferred_element_type=jnp.float32).astype(jnp.bfloat16), "tensor"
    ).astype(jnp.float32)
    resid = inputs + attended
    second_norm, second_hat, second_inv = norm_rows(resid, second_gain)
    second_in = second_norm.astype(jnp.bfloat16)
    hidden_pre = jnp.dot(second_in, up_w, preferred_element_type=jnp.float32)
    activated = exact_gelu(hidden_pre).astype(jnp.bfloat16)
    ffn_total = lax.psum(
        jnp.dot(activated, down_w, preferred_element_type=jnp.float32).astype(jnp.bfloat16),
        "tensor",
    ).astype(jnp.float32)
    mixed_out = (resid + ffn_total).astype(jnp.bfloat16)
    upstream = row_cotangent.astype(jnp.float32)
    down_grad = outer_sum(activated, row_cotangent)
    act_grad = times_trans(row_cotangent, down_w)
    gelu_out, gelu_back = jax.vjp(exact_gelu, hidden_pre)
    hidden_grad = gelu_back(act_grad)[0].astype(jnp.bfloat16)
    up_grad = outer_sum(second_in, hidden_grad)
    second_back = lax.psum(times_trans(hidden_grad, up_w).astype(jnp.bfloat16), "tensor").astype(
        jnp.float32
    )
    second_gain_grad = jnp.sum(second_back * second_hat, 0)
    resid_grad = upstream + norm_back(second_back, second_gain, second_hat, second_inv)
    attn_grad = resid_grad.astype(jnp.bfloat16)
    out_grad = outer_sum(context, attn_grad)
    context_grad = times_trans(attn_grad, out_w).astype(jnp.bfloat16)
    (comp_key_sum, comp_value_sum), (query_part, own_key_part, own_value_part) = attend_backward(
        by_heads(queries),
        by_heads(keys),
        by_heads(values),
        comp_keys,
        comp_values,
        places,
        row_items,
        group_item,
        block_rows,
        factor,
        log_totals,
        by_heads(context_grad),
    )
    query_grad = query_part.astype(jnp.bfloat16)
    comp_key_grad = comp_key_sum.astype(jnp.bfloat16)
    comp_value_grad = comp_value_sum.astype(jnp.bfloat16)
    key_conv_grad = jnp.einsum(
        "hjc,hjd->hcd", key_grouped, comp_key_grad, preferred_element_type=jnp.float32
    )
    value_conv_grad = jnp.einsum(
        "hjc,hjd->hcd", value_grouped, comp_value_grad, preferred_element_type=jnp.float32
    )
    key_total = (
        ungroup(
            jnp.einsum(
                "hjd,hcd->hjc", comp_key_grad, key_kernel, preferred_element_type=jnp.float32
            )
        )
        + own_key_part
    )
    value_total = (
        ungroup(
            jnp.einsum(
                "hjd,hcd->hjc", comp_value_grad, value_kernel, preferred_element_type=jnp.float32
            )
        )
        + own_value_part
    )
    key_grad = key_total.astype(jnp.bfloat16) * mask_low
    value_grad = value_total.astype(jnp.bfloat16) * mask_low
    query_weight_grad = outer_sum(first_in, query_grad)
    key_weight_grad = outer_sum(first_in, key_grad)
    value_weight_grad = outer_sum(first_in, value_grad)
    first_part = (
        times_trans(query_grad, query_w)
        + times_trans(key_grad, key_w)
        + times_trans(value_grad, value_w)
    )
    first_back = lax.psum(first_part.astype(jnp.bfloat16), "tensor").astype(jnp.float32)
    first_gain_grad = jnp.sum(first_back * first_hat, 0)
    grad_tokens = (resid_grad + norm_back(first_back, first_gain, first_hat, first_inv)).astype(
        jnp.bfloat16
    )
    (
        first_share,
        second_share,
        query_share,
        key_share,
        value_share,
        out_share,
        key_conv_share,
        value_conv_share,
        up_share,
        down_share,
    ) = (
        sent_and_summed(first_gain_grad.astype(jnp.bfloat16), "dp", 0),
        *side_by_side(
            (
                second_gain_grad.astype(jnp.bfloat16),
                query_weight_grad.astype(jnp.bfloat16),
                key_weight_grad.astype(jnp.bfloat16),
                value_weight_grad.astype(jnp.bfloat16),
            ),
            "dp",
            0,
            1,
        ),
        sent_and_summed(out_grad.astype(jnp.bfloat16), "dp", 1),
        *sent_together(
            (key_conv_grad.astype(jnp.bfloat16), value_conv_grad.astype(jnp.bfloat16)), "dp", 1, 0
        ),
        sent_and_summed(up_grad.astype(jnp.bfloat16), "dp", 0),
        sent_and_summed(down_grad.astype(jnp.bfloat16), "dp", 1),
    )
    return (
        mixed_out,
        grad_tokens,
        first_share,
        second_share,
        query_share,
        key_share,
        value_share,
        out_share,
        key_conv_share,
        value_conv_share,
        up_share,
        down_share,
    )


def solution(mesh):
    in_specs = (
        P("dp", None),
        P(),
        P(),
        P(None, "tensor"),
        P(None, "tensor"),
        P(None, "tensor"),
        P("tensor", None),
        P("tensor", None, None),
        P("tensor", None, None),
        P(None, "tensor"),
        P("tensor", None),
        P("dp"),
        P("dp", None),
        P("dp", None),
    )
    out_specs = (
        P("dp", None),
        P("dp", None),
        P("dp"),
        P("dp"),
        P("dp", "tensor"),
        P("dp", "tensor"),
        P("dp", "tensor"),
        P("tensor", "dp"),
        P("tensor", "dp", None),
        P("tensor", "dp", None),
        P("dp", "tensor"),
        P("tensor", "dp"),
    )
    return jax.shard_map(
        on_device, mesh=mesh, in_specs=in_specs, out_specs=out_specs, check_vma=False
    )
```

profile of v0, /device:TPU:0, one launch (start us, length us, event | category | flops | bytes accessed | tf_op | source)
XLA Modules:
  0.0 1213.5 jit_solution(17496968403063215444)
XLA Ops:
  29.4 3.7 fusion.77
  40.5 4.7 convolution_convert_fusion.4
  45.3 4.2 reshape.385
  49.5 3.7 copy.118
  53.3 5.6 copy.115
  58.9 6.4 copy.119
  65.3 6.5 copy.117
  71.8 6.1 copy.121
  79.8 93.5 %while.33 = (s32[]{:T(128)}, bf16[9,512,2,64]{1,3,2,0:T(8,128)(2,1)}, f32[9,2,512]{2,1,0:T(2,128)}, bf16[9,512,2,64]{1,3,2,0:T(8,128)(2,1)}, bf16[9,512,2,64]{1,...) while((s32[]{:T(128)}, ...), condition=%wide.region_8.9_spmd.clone, body=%wide.region_4.8_spmd.sunk.clone | while | flops 424356864 | bytes 23713932 | solution.py:123
  180.9 174.7 %all-reduce.5.cloned.1.call-done = bf16[4608,512]{1,0:T(8,128)(2,1)} async-done(((bf16[4608,512]{1,0:T(8,128)(2,1)}), bf16[4608,512]{1,0:T(8,128)(2,1)}) %all-reduce.5.cloned.1.call-update) | async-done | bytes 4718608 | tf_op jit(solution)/shard_map/psum | solution.py:314
  355.6 5.2 fusion.75
  361.0 5.1 multiply_reduce_fusion.1
  369.7 25.5 %add_convert_fusion.1 = (bf16[4608,512]{1,0:T(8,128)(2,1)S(1)}, f32[4608,512]{1,0:T(8,128)}) fusion(f32[4608,512]{1,0:T(8,128)S(1)} %fusion.82, bf16[4608,512]{1,0:T(8,128)(2,1)S(1)} %bitcast.320, bf16[512,512]{1,0:T(8,128)(2,1)S(1)} %copy-done), kind=kOutput, calls=%fused_computation.110 | convolution fusion | flops 2585788416 | bytes 28835840 | tf_op jit(solution)/shard_map/dot_general | solution.py:62
  397.4 4.3 convolution_convert_fusion
  401.8 11.9 multiply_convert_fusion.1
  413.7 7.0 convolution_convert_fusion.1
  420.7 152.1 %all-reduce.7.cloned.1.call-done = bf16[4608,512]{1,0:T(8,128)(2,1)} async-done(((bf16[4608,512]{1,0:T(8,128)(2,1)}), bf16[4608,512]{1,0:T(8,128)(2,1)}) %all-reduce.7.cloned.1.call-update) | async-done | bytes 4718608 | tf_op jit(solution)/shard_map/psum | solution.py:333
  572.8 9.5 fusion.66
  582.3 9.2 fusion.64
  599.1 6.1 copy.126
  605.2 178.0 %while.34 = (s32[]{:T(128)}, f32[2,1536,64]{1,2,0:T(8,128)}, f32[2,1536,64]{1,2,0:T(8,128)S(1)}, bf16[9,512,2,64]{1,3,2,0:T(8,128)(2,1)}, f32[9,512,2,64]{1,3,2,...) while((s32[]{:T(128)}, f32[2,1536,64]{1,2,0:T(8,128)}, ...), condition=%wide.region_20.21_spmd.clone.clone, body=%wide.region_16.20_spmd.clone.sunk.clone | while | flops 1025190912 | bytes 61733132 | solution.py:208
  610.5 3.6 multiply_reduce_fusion.4
  669.7 3.6 multiply_reduce_fusion.4
  768.5 3.6 multiply_reduce_fusion.4
  787.1 7.0 copy.144
  794.1 5.6 reshape.384
  801.6 7.4 copy.130
  809.1 5.6 reshape.366
  816.6 7.4 copy.133
  824.0 5.6 reshape.369
  829.6 7.0 copy.143
  836.5 5.6 reshape.383
  842.1 5.9 fusion.85
  851.2 4.9 add_convert_fusion
  856.1 7.2 convolution_convert_fusion.7
  863.3 3.7 all-to-all-start.5
  867.1 9.0 fusion.83
  881.0 9.0 all-to-all-done.4
  899.0 4.2 convolution_convert_fusion.10
  903.2 4.3 convolution_convert_fusion.8
  907.5 4.6 fusion.86
  914.6 4.2 all-to-all-start.2
  920.1 4.3 all-to-all-done.2
  929.1 8.4 all-to-all-done.1
  938.9 241.6 %all-reduce.9.cloned.1.call-done = (bf16[4608,512]{1,0:T(8,128)(2,1)}, bf16[4608,512]{1,0:T(8,128)(2,1)}) async-done(((bf16[4608,512]{1,0:T(8,128)(2,1)}, bf16[4608,512]{1,0:T(8,128)(2,1)}), (bf16[4608,512]{1,0:T(8,128)(2,1)}, bf16[4608,512]{1,0:T(8,128)(2,1)})) %all-reduce.9.cloned.1.call-update) | async-done | bytes 9437200 | tf_op jit(solution)/shard_map/psum | solution.py:322
  1180.6 7.1 fusion.68
  1188.4 3.7 all-to-all-start
  1192.1 13.8 %fusion.60 = (bf16[4608,512]{1,0:T(8,128)(2,1)}, bf16[4608,512]{1,0:T(8,128)(2,1)}) fusion(f32[4608,512]{1,0:T(8,128)} %copy-done.3, bf16[4608,512]{1,0:T(8,128)(2,1)} %param.18, bf16[4608,512]{1,0:T(8,128)(2,1)} %get-tuple-element.410, f32[4608]{0:T(1024)S(1)} %broadcast_multiply_fusion, f32[4608]{0:T(1024)S(1)} %broadcast_multiply_fusion.1, ...), kind=kLoop, calls=%fused_computation.99 | loop fusion | flops 37748736 | bytes 37824512 | tf_op jit(solution)/shard_map/convert_element_type | solution.py:392
  (458 shorter events, 347.3 us)
Async XLA Ops:
  7.2 362.4 %copy-start = (bf16[512,512]{1,0:T(8,128)(2,1)S(1)}, bf16[512,512]{1,0:T(8,128)(2,1)}, u32[]{:S(2)}) copy-start(bf16[512,512]{1,0:T(8,128)(2,1)} %param.28) | copy-start | bytes 1572868
  7.2 9.8 copy-start.40
  7.2 10.4 copy-start.41
  7.2 348.4 %all-reduce.5.cloned.1.call-start = ((), (), s32[]{:S(2)}) async-start(), calls=%async_computation.6 | async-start | bytes 9437184 | tf_op jit(solution)/shard_map/psum | solution.py:314
  9.9 29.6 %copy-start.13 = (bf16[9,512,2,64]{1,3,2,0:T(8,128)(2,1)}, bf16[9,512,2,64]{1,3,2,0:T(8,128)(2,1)S(1)}, u32[]{:S(2)}) copy-start(bf16[9,512,2,64]{1,3,2,0:T(8,128)(2,1)S(1)} %fusion.98) | copy-start | bytes 3538948
  14.0 6.1 copy-start.25
  14.0 8.3 copy-start.19
  22.3 7.1 copy-start.23
  33.2 7.4 copy-start.21
  53.3 24.6 %copy-start.31 = (bf16[2,192,64]{1,2,0:T(8,128)(2,1)S(1)}, bf16[2,192,64]{1,2,0:T(8,128)(2,1)}, u32[]{:S(2)}) copy-start(bf16[2,192,64]{1,2,0:T(8,128)(2,1)} %param.25) | copy-start | bytes 147460
  58.8 21.0 %copy-start.12 = (bf16[2,1536,3,64]{1,3,2,0:T(8,128)(2,1)}, bf16[2,1536,3,64]{1,3,2,0:T(8,128)(2,1)S(1)}, u32[]{:S(2)}) copy-start(bf16[2,1536,3,64]{1,3,2,0:T(8,128)(2,1)S(1)} %copy.115) | copy-start | bytes 3538948
  58.8 19.3 %copy-start.33 = (bf16[2,192,64]{1,2,0:T(8,128)(2,1)S(1)}, bf16[2,192,64]{1,2,0:T(8,128)(2,1)}, u32[]{:S(2)}) copy-start(bf16[2,192,64]{1,2,0:T(8,128)(2,1)} %param.26) | copy-start | bytes 147460
  173.3 7.6 copy-start.37
  173.3 7.6 copy-start.38
  180.9 391.9 %all-reduce.7.cloned.1.call-start = ((), (), s32[]{:S(2)}) async-start(), calls=%async_computation.7 | async-start | bytes 9437184 | tf_op jit(solution)/shard_map/psum | solution.py:333
  360.9 221.4 %copy-start.29 = (f32[4608]{0:T(1024)}, f32[4608]{0:T(1024)S(1)}, u32[]{:S(2)}) copy-start(f32[4608]{0:T(1024)S(1)} %broadcast_multiply_fusion.4) | copy-start | bytes 55300
  360.9 8.7 slice-start.4
  366.2 216.2 %copy-start.35 = (f32[4608]{0:T(1024)}, f32[4608]{0:T(1024)S(1)}, u32[]{:S(2)}) copy-start(f32[4608]{0:T(1024)S(1)} %add_rsqrt_fusion) | copy-start | bytes 55300
  369.7 25.5 %copy-start.14 = (f32[4608,512]{1,0:T(8,128)}, f32[4608,512]{1,0:T(8,128)S(1)}, u32[]{:S(2)}) copy-start(f32[4608,512]{1,0:T(8,128)S(1)} %fusion.82) | copy-start | bytes 28311556
  401.7 778.9 %all-reduce.9.cloned.1.call-start = ((), (), s32[]{:S(2)}) async-start(), calls=%async_computation.8 | async-start | bytes 18874368 | tf_op jit(solution)/shard_map/psum | solution.py:322
  572.8 9.5 copy-start.9
  618.9 6.1 copy-start.7
  658.4 6.1 copy-start.7
  678.1 6.1 copy-start.7
  697.9 6.1 copy-start.7
  717.6 6.1 copy-start.7
  737.4 6.1 copy-start.7
  757.2 6.1 copy-start.7
  776.9 6.1 copy-start.7
  787.1 12.6 %copy-start.8 = (f32[2,1536,64]{1,2,0:T(8,128)S(1)}, f32[2,1536,64]{1,2,0:T(8,128)}, u32[]{:S(2)}) copy-start(f32[2,1536,64]{1,2,0:T(8,128)} %get-tuple-element.159) | copy-start | bytes 2359300
  787.1 12.6 %copy-start.32 = (bf16[2,192,64]{1,2,0:T(8,128)(2,1)S(1)}, bf16[2,192,64]{1,2,0:T(8,128)(2,1)}, u32[]{:S(2)}) copy-start(bf16[2,192,64]{1,2,0:T(8,128)(2,1)} %param.25) | copy-start | bytes 147460
  801.6 13.0 %copy-start.34 = (bf16[2,192,64]{1,2,0:T(8,128)(2,1)S(1)}, bf16[2,192,64]{1,2,0:T(8,128)(2,1)}, u32[]{:S(2)}) copy-start(bf16[2,192,64]{1,2,0:T(8,128)(2,1)} %param.26) | copy-start | bytes 147460
  829.6 12.6 %copy-start.39 = (bf16[4608]{0:T(1024)(128)(2,1)S(1)}, bf16[4608]{0:T(1024)(128)(2,1)}, u32[]{:S(2)}) copy-start(bf16[4608]{0:T(1024)(128)(2,1)} %get-tuple-element.438) | copy-start | bytes 27652
  856.1 10.9 copy-start.30
  856.1 10.9 copy-start.36
  863.3 13.4 %all-to-all-start.5 = ((bf16[8,512,64]{1,2,0:T(8,128)(2,1)}), bf16[8,512,64]{1,2,0:T(8,128)(2,1)S(1)}, u32[]{:S(2)}, u32[]{:S(2)}) async-start(bf16[8,512,64]{1,2,0:T(8,128)(2,1)} %bitcast.30), calls=%async_computation.5 | async-start | bytes 1048576 | tf_op jit(solution)/shard_map/all_to_all | solution.py:17
  876.8 13.2 %all-to-all-start.4 = ((bf16[8,64,512]{2,1,0:T(8,128)(2,1)}), bf16[8,64,512]{2,1,0:T(8,128)(2,1)S(1)}, u32[]{:S(2)}, u32[]{:S(2)}) async-start(bf16[8,64,512]{2,1,0:T(8,128)(2,1)} %bitcast.28), calls=%async_computation.4 | async-start | bytes 1048576 | tf_op jit(solution)/shard_map/all_to_all | solution.py:17
  894.5 12.9 %copy-start.11 = (bf16[16,8,9,512]{3,1,2,0:T(8,128)(2,1)S(1)}, bf16[16,8,9,512]{3,1,2,0:T(8,128)(2,1)}, u32[]{:S(2)}) copy-start(bf16[16,8,9,512]{3,1,2,0:T(8,128)(2,1)} %copy-done.10) | copy-start | bytes 3538948
  895.4 19.3 %all-to-all-start.3 = ((bf16[8,2,3072]{2,1,0:T(2,128)(2,1)}), bf16[8,2,3072]{2,1,0:T(2,128)(2,1)S(1)}, u32[]{:S(2)}, u32[]{:S(2)}) async-start(bf16[8,2,3072]{2,1,0:T(2,128)(2,1)} %reshape.394), calls=%async_computation.3 | async-start | bytes 196608 | tf_op jit(solution)/shard_map/all_to_all | solution.py:17
  903.2 8.9 slice-start.2
  907.5 6.1 copy-start.44
  912.1 268.4 %copy-start.26 = (f32[4608]{0:T(1024)S(1)}, f32[4608]{0:T(1024)}, u32[]{:S(2)}) copy-start(f32[4608]{0:T(1024)} %copy-done.25) | copy-start | bytes 55300
  912.2 268.4 %copy-start.28 = (f32[4608]{0:T(1024)S(1)}, f32[4608]{0:T(1024)}, u32[]{:S(2)}) copy-start(f32[4608]{0:T(1024)} %copy-done.27) | copy-start | bytes 55300
  912.2 268.4 %copy-start.42 = (f32[512]{0:T(512)S(1)}, f32[512]{0:T(512)}, u32[]{:S(2)}) copy-start(f32[512]{0:T(512)} %param.19) | copy-start | bytes 6148
  914.6 9.7 all-to-all-start.2
  924.3 13.2 %all-to-all-start.1 = ((bf16[8,64,385]{2,1,0:T(8,128)(2,1)}), bf16[8,64,385]{2,1,0:T(8,128)(2,1)S(1)}, u32[]{:S(2)}, u32[]{:S(2)}) async-start(bf16[8,64,385]{2,1,0:T(8,128)(2,1)} %pad_maximum_fusion), calls=%async_computation.1 | async-start | bytes 1048576 | tf_op jit(solution)/shard_map/all_to_all | solution.py:17
  1188.4 17.5 %all-to-all-start = ((bf16[8,1,64]{2,1,0:T(2,128)(2,1)}), bf16[8,1,64]{2,1,0:T(2,128)(2,1)S(1)}, u32[]{:S(2)}, u32[]{:S(2)}) async-start(bf16[8,1,64]{2,1,0:T(2,128)(2,1)} %convert_element_type.287), calls=%async_computation | async-start | bytes 8192 | tf_op jit(solution)/shard_map/all_to_all | solution.py:17
  1192.1 14.4 %copy-start.1 = (bf16[512,512]{1,0:T(8,128)(2,1)S(1)}, bf16[512,512]{1,0:T(8,128)(2,1)}, u32[]{:S(2)}) copy-start(bf16[512,512]{1,0:T(8,128)(2,1)} %param.28) | copy-start | bytes 1572868
  (30 other events, 93.5 us)
Sparse Core Ops, SparseCore 0:
  181.0 174.6 all-reduce.4
  401.8 170.9 all-reduce.6
  856.2 324.3 all-reduce.8
where the time goes:
time: 1230 us; the launch traced here: 1210 us
  waiting for transfers between devices  591 us (48%)
  matrix products  263 us (21%)
  other arithmetic  180 us (15%)
  local copies, waits for them, and re-layouts  141 us (11%)
  starting transfers between devices  22.3 us (2%)
  between operations  15.1 us (1%)
    psum x1, waiting for transfers between devices, on_device(): lax.psum(jnp.dot(activated, down_w, preferred_element_type=jnp.float32).a...  242 us
    psum x1, waiting for transfers between devices, on_device(): lax.psum(jnp.dot(context, out_w, preferred_element_type=jnp.float32).asty...  175 us
    psum x1, waiting for transfers between devices, on_device(): lax.psum(times_trans(hidden_grad, up_w).astype(jnp.bfloat16), 'tensor')  152 us
    dot_general x18, matrix products, block_scores(): jnp.einsum('qhd,hjd->hqj', block_queries, comp_keys, preferred_element_ty...  54.9 us
    dot_general x6, matrix products, times_trans(): lax.dot_general(left_side, weight, (((1,), (1,)), ((), ())), preferred_el...  38.8 us
    dynamic_update_slice x27, other arithmetic, attend_forward(): lax.map(forward_block, (split_blocks(queries), split_blocks(keys), split_...  34.9 us
    dot_general x9, matrix products, forward_block(): jnp.einsum('hqj,hjd->hqd', key_prob.astype(jnp.bfloat16), comp_values, pr...  31.7 us
    dot_general x6, matrix products, outer_sum(): lax.dot_general(left_side, right_side, (((0,), (0,)), ((), ())), preferre...  30.7 us
  transfers between devices with their start and end apart: 9, of which 7 were waited for; matrix products, arithmetic and copies ran while one was open for 6% of the time, Pallas kernels for 0%

commit v1 on v0

v1 whole, which is shorter than its diff:
```python
import functools
import math

import jax
import jax.numpy as jnp
from jax import lax
from jax.experimental import pallas as pl
from jax.experimental.pallas import tpu as pltpu
from jax.sharding import PartitionSpec as P

F32 = jnp.float32
BF16 = jnp.bfloat16
GB = 128
TB = 3 * GB
NEG = -1e30
LOG2E = 1.0 / math.log(2.0)
VMEM = 60 * 1024 * 1024

ERF_P = 0.43
ERF_C = (
    0.24255178053871013,
    0.24376598744271377,
    0.2089868288055898,
    0.23281685899157548,
    -0.05797941172752005,
    0.3523368029188165,
    -0.2915198548110903,
    0.06904073943922798,
)


def nn(a, b):
    return lax.dot_general(a, b, (((1,), (0,)), ((), ())), preferred_element_type=F32)


def nt(a, b):
    return lax.dot_general(a, b, (((1,), (1,)), ((), ())), preferred_element_type=F32)


def tn(a, b):
    return lax.dot_general(a, b, (((0,), (0,)), ((), ())), preferred_element_type=F32)


def norm_rows(values):
    centred = values - jnp.mean(values, -1, keepdims=True)
    inv_std = lax.rsqrt(jnp.mean(centred * centred, -1, keepdims=True) + 1e-05)
    return centred * inv_std, inv_std


def norm_back(grad_out, gains, normed, inv_std):
    scaled = grad_out * gains
    return inv_std * (
        scaled
        - jnp.mean(scaled, -1, keepdims=True)
        - normed * jnp.mean(scaled * normed, -1, keepdims=True)
    )


def tap_major(scratch, values):
    lanes = scratch.shape[2]
    parts = []
    for c in range(scratch.shape[0]):
        scratch[c] = values[:, c * lanes : (c + 1) * lanes]
        taps = [scratch[c, pl.ds(r, GB, stride=3), :] for r in range(3)]
        parts.append(jnp.concatenate(taps, axis=0))
    return jnp.concatenate(parts, axis=1)


def token_major(scratch, values):
    lanes = scratch.shape[2]
    parts = []
    for c in range(scratch.shape[0]):
        for r in range(3):
            scratch[c, pl.ds(r, GB, stride=3), :] = values[
                r * GB : (r + 1) * GB, c * lanes : (c + 1) * lanes
            ]
        parts.append(scratch[c])
    return jnp.concatenate(parts, axis=1)


def gelu_and_slope(h):
    z = jnp.abs(h) * math.sqrt(0.5)
    t = 1.0 / (1.0 + ERF_P * z)
    poly = jnp.full_like(t, ERF_C[-1])
    for c in ERF_C[-2::-1]:
        poly = poly * t + c
    e = jnp.exp(-z * z)
    tail = (0.5 * e) * (poly * t)
    cdf = jnp.where(h >= 0, 1.0 - tail, tail)
    return h * cdf, cdf + h * (e * (1.0 / math.sqrt(2.0 * math.pi)))


def item_starts(lens_ref, block):
    places = block * GB + lax.broadcasted_iota(jnp.int32, (1, GB), 1)
    starts = jnp.zeros((1, GB), jnp.int32)
    least = jnp.int32(0)
    end = jnp.int32(0)
    for i in range(lens_ref.shape[0] - 1):
        end = end + lens_ref[i]
        starts = jnp.where(places >= end, end, starts)
        least = jnp.where(block * GB >= end, end, least)
    return places, starts, least // GB


def mask_bias(places, starts, kb):
    keys = kb * GB + lax.broadcasted_iota(jnp.int32, (GB, GB), 0)
    bias = jnp.where((keys >= starts) & (keys < places), 0.0, NEG)
    return jnp.concatenate([bias] * 3, axis=1)


def key_rows(kb):
    return pl.ds(pl.multiple_of(kb * GB, GB), GB)


def forward_kernel(
    heads, hd, lens_ref, x_ref, gain_ref, w_ref, kconv_ref, vconv_ref, mask_ref,
    q_ref, k_ref, v_ref, ctx_ref, lse_ref, ck_ref, ckt_ref, cv_ref,
    xs, cvt_ref, m_ref, l_ref, acc_ref,
):
    block = pl.program_id(0)
    width = heads * hd
    scale = LOG2E / math.sqrt(hd)
    normed, _ = norm_rows(x_ref[...].astype(F32))
    first_in = tap_major(xs, normed * gain_ref[...]).astype(BF16)
    mask = mask_ref[0, 0:1, :]
    q_ref[...] = nt(w_ref[0:width], first_in).astype(BF16)
    k_ref[...] = (nt(w_ref[width : 2 * width], first_in) * mask).astype(BF16)
    v_ref[...] = (nt(w_ref[2 * width : 3 * width], first_in) * mask).astype(BF16)
    rows = key_rows(block)
    for h in range(heads):
        band = slice(h * hd, (h + 1) * hd)
        for src, conv, plain, trans in ((k_ref, kconv_ref, ck_ref, ckt_ref), (v_ref, vconv_ref, cv_ref, cvt_ref)):
            taps = jnp.concatenate([src[band, r * GB : (r + 1) * GB] for r in range(3)], axis=0)
            comp = nn(conv[h], taps)
            trans[band, rows] = comp.astype(BF16)
            plain[h, rows, :] = comp.T.astype(BF16)
        q, k = q_ref[band, :].astype(F32), k_ref[band, :].astype(F32)
        m_ref[h : h + 1, :] = jnp.sum(q * k, axis=0, keepdims=True) * scale
        acc_ref[band, :] = v_ref[band, :].astype(F32)
    l_ref[...] = jnp.ones_like(l_ref)
    places, starts, low = item_starts(lens_ref, block)

    def step(kb, carry):
        bias = mask_bias(places, starts, kb)
        cols = key_rows(kb)
        for h in range(heads):
            band = slice(h * hd, (h + 1) * hd)
            one = slice(h, h + 1)
            s = nn(ck_ref[h, cols, :], q_ref[band, :]) * scale + bias
            old = m_ref[one, :]
            new = jnp.maximum(old, jnp.max(s, axis=0, keepdims=True))
            p = jnp.exp2(s - new)
            keep = jnp.exp2(old - new)
            m_ref[one, :] = new
            l_ref[one, :] = l_ref[one, :] * keep + jnp.sum(p, axis=0, keepdims=True)
            acc_ref[band, :] = acc_ref[band, :] * keep + nn(cvt_ref[band, cols], p.astype(BF16))
        return carry

    lax.fori_loop(low, block + 1, step, 0)
    lse_ref[...] = m_ref[...] + jnp.log(l_ref[...]) * LOG2E
    inv = 1.0 / l_ref[...]
    for h in range(heads):
        band = slice(h * hd, (h + 1) * hd)
        ctx_ref[band, :] = (acc_ref[band, :] * inv[h : h + 1, :]).astype(BF16)


def middle_kernel(
    heads, hd, x_ref, g_ref, gain_ref, ctx_ref, out_ref, up_ref, down_ref,
    mixed_ref, resid_grad_ref, dctx_ref, delta_ref, grads_ref,
    xs, down_sum, up_sum, out_sum, gain_sum,
):
    block = pl.program_id(0)
    own = out_sum.shape[0]

    @pl.when(block == 0)
    def _():
        down_sum[...] = jnp.zeros_like(down_sum)
        up_sum[...] = jnp.zeros_like(up_sum)
        out_sum[...] = jnp.zeros_like(out_sum)
        gain_sum[...] = jnp.zeros_like(gain_sum)

    gain = gain_ref[...]
    x = tap_major(xs, x_ref[...].astype(F32))
    g = tap_major(xs, g_ref[...].astype(F32))
    g_low = g.astype(BF16)
    resid = x + tn(ctx_ref[...], out_ref[...])
    hat, inv_std = norm_rows(resid)
    second_in = (hat * gain).astype(BF16)
    ffn = jnp.zeros_like(resid)
    back = jnp.zeros_like(resid)
    for c in range(up_ref.shape[0]):
        hidden = nn(second_in, up_ref[c])
        act_grad = nt(g_low, down_ref[c])
        act, slope = gelu_and_slope(hidden)
        act = act.astype(BF16)
        hidden_grad = (act_grad * slope).astype(BF16)
        ffn = ffn + nn(act, down_ref[c])
        back = back + nt(hidden_grad, up_ref[c])
        if c == 0:
            down_sum[...] += tn(act, g_low)
            up_sum[...] += tn(second_in, hidden_grad)
    mixed_ref[...] = token_major(xs, resid + ffn).astype(BF16)
    gain_sum[...] += jnp.sum(back * hat, axis=0, keepdims=True)
    resid_grad = g + norm_back(back, gain, hat, inv_std)
    attn_grad = resid_grad.astype(BF16)
    resid_grad_ref[...] = attn_grad
    out_sum[...] += nn(ctx_ref[0:own, :], attn_grad)
    dctx = nt(out_ref[...], attn_grad).astype(BF16)
    dctx_ref[...] = dctx
    dots = dctx.astype(F32) * ctx_ref[...].astype(F32)
    for h in range(heads):
        delta_ref[h : h + 1, :] = jnp.sum(dots[h * hd : (h + 1) * hd], axis=0, keepdims=True)

    @pl.when(block == pl.num_programs(0) - 1)
    def _():
        units = up_sum.shape[1]
        grads_ref[:, 0:units] = up_sum[...].astype(BF16)
        grads_ref[:, units : 2 * units] = down_sum[...].T.astype(BF16)
        grads_ref[:, 2 * units : 2 * units + own] = out_sum[...].T.astype(BF16)
        grads_ref[:, 2 * units + own :] = jnp.broadcast_to(gain_sum[...], (GB, gain.shape[1])).T.astype(BF16)


def backward_kernel(
    heads, hd, own_heads, lens_ref, x_ref, gain_ref, w_ref, kconv_ref, vconv_ref, mask_ref,
    q_ref, k_ref, v_ref, lse_ref, dctx_ref, delta_ref, resid_grad_ref, ck_ref, ckt_ref, cv_ref,
    tokens_ref, grads_ref, conv_ref,
    xs, dck_sum, dcv_sum, dq_sum, dqkv, weight_sum, kconv_sum, vconv_sum, gain_sum,
):
    step_id = pl.program_id(0)
    block = pl.num_programs(0) - 1 - step_id
    width = heads * hd
    own = own_heads * hd
    factor = 1.0 / math.sqrt(hd)
    scale = LOG2E * factor

    @pl.when(step_id == 0)
    def _():
        dck_sum[...] = jnp.zeros_like(dck_sum)
        dcv_sum[...] = jnp.zeros_like(dcv_sum)
        weight_sum[...] = jnp.zeros_like(weight_sum)
        kconv_sum[...] = jnp.zeros_like(kconv_sum)
        vconv_sum[...] = jnp.zeros_like(vconv_sum)
        gain_sum[...] = jnp.zeros_like(gain_sum)

    dq_sum[...] = jnp.zeros_like(dq_sum)
    places, starts, low = item_starts(lens_ref, block)

    def step(kb, carry):
        bias = mask_bias(places, starts, kb)
        cols = key_rows(kb)
        for h in range(heads):
            band = slice(h * hd, (h + 1) * hd)
            one = slice(h, h + 1)
            q, dctx = q_ref[band, :], dctx_ref[band, :]
            s = nn(ck_ref[h, cols, :], q) * scale + bias
            p = jnp.exp2(s - lse_ref[one, :])
            dp = nn(cv_ref[h, cols, :], dctx)
            ds = (p * (dp - delta_ref[one, :])).astype(BF16)
            dcv_sum[h, cols, :] += nt(p.astype(BF16), dctx)
            dck_sum[h, cols, :] += nt(ds, q)
            dq_sum[band, :] += nn(ckt_ref[band, cols], ds)
        return carry

    lax.fori_loop(low, block + 1, step, 0)
    mask = mask_ref[0, 0:1, :]
    rows = key_rows(block)
    for h in range(heads):
        band = slice(h * hd, (h + 1) * hd)
        one = slice(h, h + 1)
        q, k = q_ref[band, :].astype(F32), k_ref[band, :].astype(F32)
        v, dctx = v_ref[band, :].astype(F32), dctx_ref[band, :].astype(F32)
        own_prob = jnp.exp2(jnp.sum(q * k, axis=0, keepdims=True) * scale - lse_ref[one, :])
        own_dprob = jnp.sum(dctx * v, axis=0, keepdims=True)
        own_dscore = own_prob * (own_dprob - delta_ref[one, :]) * factor
        dqkv[band, :] = (dq_sum[band, :] * factor + own_dscore * k).astype(BF16)
        dck = (dck_sum[h, rows, :] * factor).astype(BF16)
        dcv = dcv_sum[h, rows, :].astype(BF16)
        for at, src, conv, total, grad, beside in (
            (width, k_ref, kconv_ref, kconv_sum, dck, own_dscore * q),
            (2 * width, v_ref, vconv_ref, vconv_sum, dcv, own_prob * dctx),
        ):
            spread = nt(conv[h], grad)
            spread = jnp.concatenate([spread[r * hd : (r + 1) * hd] for r in range(3)], axis=1)
            dqkv[at + h * hd : at + (h + 1) * hd, :] = ((spread + beside) * mask).astype(BF16)
            if h < own_heads:
                taps = jnp.concatenate([src[band, r * GB : (r + 1) * GB] for r in range(3)], axis=0)
                total[h] += nn(taps, grad)
    x = tap_major(xs, x_ref[...].astype(F32))
    hat, inv_std = norm_rows(x)
    gain = gain_ref[...]
    first_in = (hat * gain).astype(BF16)
    for part in range(3):
        weight_sum[part * own : (part + 1) * own, :] += nn(dqkv[part * width : part * width + own, :], first_in)
    back = tn(dqkv[...], w_ref[...])
    gain_sum[...] += jnp.sum(back * hat, axis=0, keepdims=True)
    total = resid_grad_ref[...].astype(F32) + norm_back(back, gain, hat, inv_std)
    tokens_ref[...] = token_major(xs, total).astype(BF16)

    @pl.when(block == 0)
    def _():
        grads_ref[:, 0 : 3 * own] = weight_sum[...].T.astype(BF16)
        grads_ref[:, 3 * own :] = jnp.broadcast_to(gain_sum[...], (GB, gain.shape[1])).T.astype(BF16)
        for h in range(own_heads):
            conv_ref[:, h * hd : (h + 1) * hd] = kconv_sum[h].astype(BF16)
            conv_ref[:, (own_heads + h) * hd : (own_heads + h + 1) * hd] = vconv_sum[h].astype(BF16)


def whole(shape):
    return pl.BlockSpec(shape, lambda *_: (0,) * len(shape))


def params():
    return pltpu.CompilerParams(vmem_limit_bytes=VMEM, dimension_semantics=("arbitrary",))


def gathered(shard):
    half = shard.shape[0] // 2
    core = lax.rem(lax.axis_index("dp"), 2)
    peers = lax.axis_size("tensor")
    pairs = [(i, i ^ 1) for i in range(lax.axis_size("dp"))]
    mine = lax.dynamic_slice_in_dim(shard, core * half, half, 0)
    got = jnp.stack(
        [lax.ppermute(mine, "tensor", [(i, i ^ s) for i in range(peers)]) for s in range(1, peers)]
    )
    other = lax.ppermute(got, "dp", pairs)
    both = jnp.where(
        core == 0, jnp.concatenate([got, other], axis=1), jnp.concatenate([other, got], axis=1)
    )
    return jnp.concatenate([shard[None], both], axis=0)


def sent_and_summed(array):
    count = lax.axis_size("dp")
    parts = array.reshape(count, array.shape[0] // count, *array.shape[1:])
    parts = lax.all_to_all(parts, "dp", 0, 0, tiled=True)
    return jnp.sum(parts.astype(F32), axis=0)


def on_device(
    tokens, first_gain, second_gain, query_weight, key_weight, value_weight, out_weight,
    key_conv, value_conv, up_weight, down_weight, pad_mask, item_lengths, cotangent,
):
    rows, dim = tokens.shape
    blocks = rows // TB
    groups = rows // 3
    own_heads, taps, hd = key_conv.shape
    peers = lax.axis_size("tensor")
    heads = own_heads * peers
    width = heads * hd
    own = own_heads * hd
    units = up_weight.shape[1]
    lens = item_lengths[0]
    mask = pad_mask.reshape(blocks, GB, 3).transpose(0, 2, 1).reshape(blocks, 1, TB).astype(F32)
    gain1, gain2 = first_gain[None], second_gain[None]

    proj = jnp.concatenate([query_weight.T, key_weight.T, value_weight.T], axis=0)
    convs = jnp.concatenate(
        [
            key_conv.transpose(0, 2, 1).reshape(own, taps),
            value_conv.transpose(0, 2, 1).reshape(own, taps),
        ],
        axis=1,
    )
    proj_all = gathered(proj)
    convs_all = gathered(convs)
    w_all = proj_all.reshape(peers, 3, own, dim).transpose(1, 0, 2, 3).reshape(3 * width, dim)
    kconv_t = convs_all[:, :, :taps].reshape(heads, hd, taps)
    vconv_t = convs_all[:, :, taps:].reshape(heads, hd, taps)
    kconv, vconv = kconv_t.transpose(0, 2, 1), vconv_t.transpose(0, 2, 1)
    out_all = gathered(out_weight).reshape(width, dim)
    up_all = gathered(up_weight)
    down_all = gathered(down_weight)

    rows_spec = pl.BlockSpec((TB, dim), lambda b, *_: (b, 0))
    cols_spec = pl.BlockSpec((width, TB), lambda b, *_: (0, b))
    stat_spec = pl.BlockSpec((heads, TB), lambda b, *_: (0, b))
    mask_spec = pl.BlockSpec((1, 1, TB), lambda b, *_: (b, 0, 0))
    q, k, v, ctx, lse, ck, ckt, cv = pl.pallas_call(
        functools.partial(forward_kernel, heads, hd),
        grid_spec=pltpu.PrefetchScalarGridSpec(
            num_scalar_prefetch=1,
            grid=(blocks,),
            in_specs=[
                rows_spec, whole((1, dim)), whole((3 * width, dim)), whole((heads, hd, taps)),
                whole((heads, hd, taps)), mask_spec,
            ],
            out_specs=[
                cols_spec, cols_spec, cols_spec, cols_spec, stat_spec,
                whole((heads, groups, hd)), whole((width, groups)), whole((heads, groups, hd)),
            ],
            scratch_shapes=[
                pltpu.VMEM((dim // 128, TB, 128), F32), pltpu.VMEM((width, groups), BF16), pltpu.VMEM((heads, TB), F32),
                pltpu.VMEM((heads, TB), F32), pltpu.VMEM((width, TB), F32),
            ],
        ),
        out_shape=[jax.ShapeDtypeStruct((width, rows), BF16)] * 4
        + [
            jax.ShapeDtypeStruct((heads, rows), F32),
            jax.ShapeDtypeStruct((heads, groups, hd), BF16),
            jax.ShapeDtypeStruct((width, groups), BF16),
            jax.ShapeDtypeStruct((heads, groups, hd), BF16),
        ],
        compiler_params=params(),
        name="attention_forward",
    )(lens, tokens, gain1, w_all, kconv_t, vconv_t, mask)

    mixed, resid_grad, dctx, delta, middle_grads = pl.pallas_call(
        functools.partial(middle_kernel, heads, hd),
        grid=(blocks,),
        in_specs=[
            rows_spec, rows_spec, whole((1, dim)), cols_spec, whole((width, dim)),
            whole((peers, dim, units)), whole((peers, units, dim)),
        ],
        out_specs=[rows_spec, rows_spec, cols_spec, stat_spec, whole((dim, 2 * units + own + GB))],
        out_shape=[
            jax.ShapeDtypeStruct((rows, dim), BF16),
            jax.ShapeDtypeStruct((rows, dim), BF16),
            jax.ShapeDtypeStruct((width, rows), BF16),
            jax.ShapeDtypeStruct((heads, rows), F32),
            jax.ShapeDtypeStruct((dim, 2 * units + own + GB), BF16),
        ],
        scratch_shapes=[
            pltpu.VMEM((dim // 128, TB, 128), F32), pltpu.VMEM((units, dim), F32), pltpu.VMEM((dim, units), F32),
            pltpu.VMEM((own, dim), F32), pltpu.VMEM((1, dim), F32),
        ],
        compiler_params=params(),
        name="feed_forward",
    )(tokens, cotangent, gain2, ctx, out_all, up_all, down_all)
    middle_share = sent_and_summed(middle_grads)

    back_rows = pl.BlockSpec((TB, dim), lambda b, *_: (blocks - 1 - b, 0))
    back_cols = pl.BlockSpec((width, TB), lambda b, *_: (0, blocks - 1 - b))
    back_stat = pl.BlockSpec((heads, TB), lambda b, *_: (0, blocks - 1 - b))
    back_mask = pl.BlockSpec((1, 1, TB), lambda b, *_: (blocks - 1 - b, 0, 0))
    grad_tokens, last_grads, conv_grads = pl.pallas_call(
        functools.partial(backward_kernel, heads, hd, own_heads),
        grid_spec=pltpu.PrefetchScalarGridSpec(
            num_scalar_prefetch=1,
            grid=(blocks,),
            in_specs=[
                back_rows, whole((1, dim)), whole((3 * width, dim)), whole((heads, taps, hd)),
                whole((heads, taps, hd)), back_mask, back_cols, back_cols, back_cols, back_stat,
                back_cols, back_stat, back_rows, whole((heads, groups, hd)), whole((width, groups)),
                whole((heads, groups, hd)),
            ],
            out_specs=[back_rows, whole((dim, 3 * own + GB)), whole((taps, 2 * own))],
            scratch_shapes=[
                pltpu.VMEM((dim // 128, TB, 128), F32), pltpu.VMEM((heads, groups, hd), F32),
                pltpu.VMEM((heads, groups, hd), F32), pltpu.VMEM((width, TB), F32),
                pltpu.VMEM((3 * width, TB), BF16), pltpu.VMEM((3 * own, dim), F32),
                pltpu.VMEM((own_heads, taps, hd), F32), pltpu.VMEM((own_heads, taps, hd), F32),
                pltpu.VMEM((1, dim), F32),
            ],
        ),
        out_shape=[
            jax.ShapeDtypeStruct((rows, dim), BF16),
            jax.ShapeDtypeStruct((dim, 3 * own + GB), BF16),
            jax.ShapeDtypeStruct((taps, 2 * own), BF16),
        ],
        compiler_params=params(),
        name="attention_backward",
    )(lens, tokens, gain1, w_all, kconv, vconv, mask, q, k, v, lse, dctx, delta, resid_grad, ck, ckt, cv)
    last_share = sent_and_summed(last_grads)
    conv_share = sent_and_summed(conv_grads)
    conv_share = conv_share.reshape(-1, 2, own_heads, hd).transpose(1, 2, 0, 3)

    return (
        mixed,
        grad_tokens,
        last_share[:, 3 * own],
        middle_share[:, 2 * units + own],
        last_share[:, :own],
        last_share[:, own : 2 * own],
        last_share[:, 2 * own : 3 * own],
        middle_share[:, 2 * units : 2 * units + own].T,
        conv_share[0],
        conv_share[1],
        middle_share[:, :units],
        middle_share[:, units : 2 * units].T,
    )


def solution(mesh):
    in_specs = (
        P("dp", None),
        P(),
        P(),
        P(None, "tensor"),
        P(None, "tensor"),
        P(None, "tensor"),
        P("tensor", None),
        P("tensor", None, None),
        P("tensor", None, None),
        P(None, "tensor"),
        P("tensor", None),
        P("dp"),
        P("dp", None),
        P("dp", None),
    )
    out_specs = (
        P("dp", None),
        P("dp", None),
        P("dp"),
        P("dp"),
        P("dp", "tensor"),
        P("dp", "tensor"),
        P("dp", "tensor"),
        P("tensor", "dp"),
        P("tensor", "dp", None),
        P("tensor", "dp", None),
        P("dp", "tensor"),
        P("tensor", "dp"),
    )
    return jax.shard_map(
        on_device, mesh=mesh, in_specs=in_specs, out_specs=out_specs, check_vma=False
    )
```

time: 1230 us -> 468 us (0.38); the launches traced: 1210 us -> 471 us
  waiting for transfers between devices: 591 us -> 54.2 us
  Pallas kernels: 0 us -> 301 us
  matrix products: 263 us -> 0 us
  other arithmetic: 180 us -> 16.8 us
  local copies, waits for them, and re-layouts: 141 us -> 14.7 us
  blocking collectives: 0 us -> 52.4 us
  between operations: 15.1 us -> 1.01 us
    psum x3 -> x0, waiting for transfers between devices: 568 us -> none  [the longest x1 242 us: on_device(): lax.psum(jnp.dot(activated, down_w, preferred_element_type=jnp.float32).a...]
    pallas_call x0 -> x3, Pallas kernels: none -> 301 us  [the longest x1 102 us: on_device(): pl.pallas_call(functools.partial(backward_kernel, heads, hd, own_heads),...]
    dot_general x87 -> x0, matrix products: 263 us -> none  [the longest x18 54.9 us: block_scores(): jnp.einsum('qhd,hjd->hqj', block_queries, comp_keys, preferred_element_ty...]
    reduce_sum x40 -> x3, other arithmetic: 73.6 us -> 0.26 us  [sent_and_summed(): return jnp.sum(parts.astype(F32), axis=0)]
    reshape x12 -> x3, local copies, waits for them, and re-layouts: 57.7 us -> 1.98 us  [the longest x1 0.97 us: on_device(): vconv_t = convs_all[:, :, taps:].reshape(heads, hd, taps)]
    all_to_all x0 -> x2, blocking collectives: none -> 52.4 us  [sent_and_summed(): parts = lax.all_to_all(parts, 'dp', 0, 0, tiled=True)]
    ppermute x0 -> x20, waiting for transfers between devices: none -> 38.7 us  [the longest x15 38.7 us: gathered(): lax.ppermute(mine, 'tensor', [(i, i ^ s) for i in range(peers)])]
    dynamic_update_slice x27 -> x0, other arithmetic: 34.9 us -> none  [attend_forward(): lax.map(forward_block, (split_blocks(queries), split_blocks(keys), split_...]
  transfers between devices with their start and end apart: 9 -> 21, of which waited for: 7 -> 7; matrix products, arithmetic and copies ran while one was open for 6% -> 5% of each run, Pallas kernels for 0% -> 20%
where the time goes in v1:
time: 468 us; the launch traced here: 471 us
  Pallas kernels  301 us (64%)
  waiting for transfers between devices  54.2 us (12%)
  blocking collectives  52.4 us (11%)
  starting transfers between devices  31.3 us (7%)
  other arithmetic  16.8 us (4%)
  local copies, waits for them, and re-layouts  14.7 us (3%)
    pallas_call x1, Pallas kernels, on_device(): pl.pallas_call(functools.partial(backward_kernel, heads, hd, own_heads),...  102 us
    pallas_call x1, Pallas kernels, on_device(): pl.pallas_call(functools.partial(middle_kernel, heads, hd), grid=(blocks,...  102 us
    pallas_call x1, Pallas kernels, on_device(): pl.pallas_call(functools.partial(forward_kernel, heads, hd), grid_spec=pl...  96.2 us
    all_to_all x2, blocking collectives, sent_and_summed(): parts = lax.all_to_all(parts, 'dp', 0, 0, tiled=True)  52.4 us
    ppermute x15, waiting for transfers between devices, gathered(): lax.ppermute(mine, 'tensor', [(i, i ^ s) for i in range(peers)])  38.7 us
    ppermute x15, starting transfers between devices, gathered(): lax.ppermute(mine, 'tensor', [(i, i ^ s) for i in range(peers)])  27.2 us
    all_to_all x1, waiting for transfers between devices, sent_and_summed(): parts = lax.all_to_all(parts, 'dp', 0, 0, tiled=True)  15.4 us
  transfers between devices with their start and end apart: 21, of which 7 were waited for; matrix products, arithmetic and copies ran while one was open for 5% of the time, Pallas kernels for 20%

profile of v1, /device:TPU:0, one launch (start us, length us, event | category | flops | bytes accessed | tf_op | source)
XLA Modules:
  0.0 471.3 jit_solution(9835250086700864819)
XLA Ops:
  0.7 1.1 copy.30
  1.8 1.0 copy.31
  2.8 1.0 copy.32
  3.9 0.7 constant_dynamic-slice_fusion.3
  4.6 3.0 collective-permute-start
  7.6 2.6 collective-permute-start.1
  10.2 0.9 fusion.2
  11.6 3.9 collective-permute-start.6
  15.5 0.7 constant_dynamic-slice_fusion.1
  16.3 0.7 constant_dynamic-slice_fusion
  17.0 1.4 collective-permute-done.4
  18.4 2.5 collective-permute-start.8
  20.8 2.9 collective-permute-done.5
  23.8 0.7 fusion.1
  25.5 0.7 convert_element_type.21.mask_ref
  26.1 2.5 collective-permute-start.2
  28.6 1.3 collective-permute-start.10
  30.0 3.0 collective-permute-done.9
  33.0 3.6 collective-permute-done.10
  36.7 3.7 collective-permute-start.13
  40.4 2.6 collective-permute-start.14
  43.0 0.8 pad_maximum_fusion.8
  43.8 0.9 pad_maximum_fusion.4
  44.7 1.8 collective-permute-start.17
  46.6 2.7 collective-permute-start.18
  49.2 1.0 maximum_select_fusion.4
  50.3 9.5 %collective-permute-done.13 = bf16[256,512]{1,0:T(8,128)(2,1)S(1)} collective-permute-done((bf16[256,512]{1,0:T(8,128)(2,1)}, bf16[256,512]{1,0:T(8,128)(2,1)S(1)}, u32[]{:S(2)}, u32[]{:S(2)}) %collective-permute-start.13) | collective-permute-done | bytes 262176 | tf_op jit(solution)/shard_map/ppermute | solution.py:323
  60.3 1.0 pad_maximum_fusion.2
  61.4 0.9 copy.35
  62.4 1.0 copy.36
  63.3 18.2 %collective-permute-done.17 = bf16[256,512]{1,0:T(8,128)(2,1)S(1)} collective-permute-done((bf16[256,512]{1,0:T(8,128)(2,1)}, bf16[256,512]{1,0:T(8,128)(2,1)S(1)}, u32[]{:S(2)}, u32[]{:S(2)}) %collective-permute-start.17) | collective-permute-done | bytes 262176 | tf_op jit(solution)/shard_map/ppermute | solution.py:323
  81.5 1.0 pad_maximum_fusion.3
  82.5 1.3 maximum_select_fusion.3
  83.8 0.8 pad_maximum_fusion.5
  84.7 1.7 maximum_select_fusion.2
  86.5 1.3 copy.33
  87.9 96.2 %attention_forward.1 = (bf16[512,4608]{1,0:T(8,128)(2,1)}, bf16[512,4608]{1,0:T(8,128)(2,1)}, bf16[512,4608]{1,0:T(8,128)(2,1)}, bf16[512,4608]{1,0:T(8,128)(2,1...) custom-call(s32[6]{0:T(128)} %bitcast.113, ...), custom_call_target="tpu_custom_call" | custom-call | tf_op jit(solution)/shard_map/attention_forward/pallas_call | solution.py:378
  184.1 1.6 maximum_select_fusion
  185.7 1.5 pad_maximum_fusion.up_ref
  187.2 1.7 maximum_select_fusion.1
  188.9 1.5 pad_maximum_fusion.1.down_ref
  190.3 102.3 %feed_forward.1 = (bf16[4608,512]{1,0:T(8,128)(2,1)}, bf16[4608,512]{1,0:T(8,128)(2,1)}, bf16[512,4608]{1,0:T(8,128)(2,1)}, f32[8,4608]{1,0:T(8,128)}, bf16[512,1280]{1,0:T(8,128)(2,1)}) custom-call(bf16[4608,512]{1,0:T(8,128)(2,1)} %x_ref.5, bf16[4608,512]{1,0:T(8,128)(2,1)} %g_ref.1, f32[1,512]{1,0:T(1,128)} %bitcast.112, ...), custom_call_target="tpu_custom_call" | custom-call | tf_op jit(solution)/shard_map/feed_forward/pallas_call | solution.py:407
  292.7 102.4 %attention_backward.1 = (bf16[4608,512]{1,0:T(8,128)(2,1)}, bf16[512,512]{1,0:T(8,128)(2,1)}, bf16[192,256]{1,0:T(8,128)(2,1)}) custom-call(s32[6]{0:T(128)} %bitcast.114, bf16[4608,512]{1,0:T(8,128)(2,1)} %x_ref.5, f32[1,512]{1,0:T(1,128)} %bitcast.111, bf16[1536,512]{1,0:T(8,128)(2,1)} %bitcast.56, bf16[8,192,64]{2,1,0:T(8,128)(2,1)} %bitcast.65, ...), custom_call_target="tpu_custom_call" | custom-call | tf_op jit(solution)/shard_map/attention_backward/pallas_call | solution.py:435
  395.1 39.3 %all_to_all.15 = bf16[8,24,256]{2,1,0:T(8,128)(2,1)S(1)} all-to-all(bf16[8,24,256]{2,1,0:T(8,128)(2,1)} %bitcast.109), channel_id=1, replica_groups=mesh['dp'=8,'tensor'=4] {'dp'}, dimensions={0} | all-to-all | bytes 196608 | tf_op jit(solution)/shard_map/all_to_all | solution.py:335
  434.3 13.1 %all_to_all.16 = bf16[8,64,512]{2,1,0:T(8,128)(2,1)S(1)} all-to-all(bf16[8,64,512]{2,1,0:T(8,128)(2,1)} %bitcast.87), channel_id=1, replica_groups=mesh['dp'=8,'tensor'=4] {'dp'}, dimensions={0} | all-to-all | bytes 1048576 | tf_op jit(solution)/shard_map/all_to_all | solution.py:335
  447.5 3.6 all-to-all-start.1
  453.7 15.4 %all-to-all-done.1 = bf16[8,64,1280]{2,1,0:T(8,128)(2,1)S(1)} async-done(((bf16[8,64,1280]{2,1,0:T(8,128)(2,1)}), bf16[8,64,1280]{2,1,0:T(8,128)(2,1)S(1)}, u32[]{:S(2)}, u32[]{:S(2)}) %all-to-all-start.1) | async-done | bytes 1310752 | tf_op jit(solution)/shard_map/all_to_all | solution.py:335
  469.4 0.7 slice_bitcast_fusion
  (87 shorter events, 6.6 us)
Async XLA Ops:
  0.6 23.2 %copy-start.13 = (bf16[2,192,64]{1,2,0:T(8,128)(2,1)S(1)}, bf16[2,192,64]{1,2,0:T(8,128)(2,1)}, u32[]{:S(2)}) copy-start(bf16[2,192,64]{1,2,0:T(8,128)(2,1)} %param.21) | copy-start | bytes 147460
  0.7 23.1 %copy-start.14 = (bf16[2,192,64]{1,2,0:T(8,128)(2,1)S(1)}, bf16[2,192,64]{1,2,0:T(8,128)(2,1)}, u32[]{:S(2)}) copy-start(bf16[2,192,64]{1,2,0:T(8,128)(2,1)} %param.22) | copy-start | bytes 147460
  0.7 14.9 %copy-start.2 = (bf16[512,512]{1,0:T(8,128)(2,1)S(1)}, bf16[512,512]{1,0:T(8,128)(2,1)}, u32[]{:S(2)}) copy-start(bf16[512,512]{1,0:T(8,128)(2,1)} %param.23) | copy-start | bytes 1572868
  0.7 15.6 %copy-start.3 = (bf16[512,512]{1,0:T(8,128)(2,1)S(1)}, bf16[512,512]{1,0:T(8,128)(2,1)}, u32[]{:S(2)}) copy-start(bf16[512,512]{1,0:T(8,128)(2,1)} %param.24) | copy-start | bytes 1572868
  0.7 16.3 %copy-start.11 = (bf16[128,512]{1,0:T(8,128)(2,1)S(1)}, bf16[128,512]{1,0:T(8,128)(2,1)}, u32[]{:S(2)}) copy-start(bf16[128,512]{1,0:T(8,128)(2,1)} %param.20) | copy-start | bytes 393220
  0.7 23.8 %copy-start.21 = (s32[4608]{0:T(1024)S(1)}, s32[4608]{0:T(1024)}, u32[]{:S(2)}) copy-start(s32[4608]{0:T(1024)} %param.25) | copy-start | bytes 55300
  4.6 35.8 %collective-permute-start = (bf16[192,512]{1,0:T(8,128)(2,1)}, bf16[192,512]{1,0:T(8,128)(2,1)S(1)}, u32[]{:S(2)}, u32[]{:S(2)}) collective-permute-start(bf16[192,512]{1,0:T(8,128)(2,1)} %constant_dynamic-slice_fusion.3), channel_id=1, source_target_pairs={{0,1},{1,0},{2,3},{3,2},{4,5},{5,4},{6,7},{7,6},{8,9},{9,8},{10,11... | collective-permute-start | bytes 589832 | tf_op jit(solution)/shard_map/ppermute | solution.py:323
  7.6 35.3 %collective-permute-start.1 = (bf16[192,512]{1,0:T(8,128)(2,1)}, bf16[192,512]{1,0:T(8,128)(2,1)S(1)}, u32[]{:S(2)}, u32[]{:S(2)}) collective-permute-start(bf16[192,512]{1,0:T(8,128)(2,1)} %constant_dynamic-slice_fusion.3), channel_id=1, source_target_pairs={{0,2},{1,3},{2,0},{3,1},{4,6},{5,7},{6,4},{7,5},{8,10},{9,11},{10,... | collective-permute-start | bytes 589832 | tf_op jit(solution)/shard_map/ppermute | solution.py:323
  11.1 7.3 %collective-permute-start.4 = (bf16[64,384]{1,0:T(8,128)(2,1)S(1)}, bf16[64,384]{1,0:T(8,128)(2,1)S(1)}, u32[]{:S(2)}, u32[]{:S(2)}) collective-permute-start(bf16[64,384]{1,0:T(8,128)(2,1)S(1)} %fusion.2), channel_id=1, source_target_pairs={{0,1},{1,0},{2,3},{3,2},{4,5},{5,4},{6,7},{7,6},{8,9},{9,8},{10,11... | collective-permute-start | bytes 147464 | tf_op jit(solution)/shard_map/ppermute | solution.py:323
  11.6 12.2 %collective-permute-start.5 = (bf16[64,384]{1,0:T(8,128)(2,1)S(1)}, bf16[64,384]{1,0:T(8,128)(2,1)S(1)}, u32[]{:S(2)}, u32[]{:S(2)}) collective-permute-start(bf16[64,384]{1,0:T(8,128)(2,1)S(1)} %fusion.2), channel_id=1, source_target_pairs={{0,2},{1,3},{2,0},{3,1},{4,6},{5,7},{6,4},{7,5},{8,10},{9,11},{10,... | collective-permute-start | bytes 147464 | tf_op jit(solution)/shard_map/ppermute | solution.py:323
  11.6 14.5 %collective-permute-start.6 = (bf16[64,384]{1,0:T(8,128)(2,1)S(1)}, bf16[64,384]{1,0:T(8,128)(2,1)S(1)}, u32[]{:S(2)}, u32[]{:S(2)}) collective-permute-start(bf16[64,384]{1,0:T(8,128)(2,1)S(1)} %fusion.2), channel_id=1, source_target_pairs={{0,3},{1,2},{2,1},{3,0},{4,7},{5,6},{6,5},{7,4},{8,11},{9,10},{10,... | collective-permute-start | bytes 147464 | tf_op jit(solution)/shard_map/ppermute | solution.py:323
  18.4 25.4 %copy-start.18 = (bf16[64,384]{1,0:T(8,128)(2,1)}, bf16[64,384]{1,0:T(8,128)(2,1)S(1)}, u32[]{:S(2)}) copy-start(bf16[64,384]{1,0:T(8,128)(2,1)S(1)} %collective-permute-done.4) | copy-start | bytes 147460
  18.4 10.3 %collective-permute-start.8 = (bf16[64,512]{1,0:T(8,128)(2,1)S(1)}, bf16[64,512]{1,0:T(8,128)(2,1)S(1)}, u32[]{:S(2)}, u32[]{:S(2)}) collective-permute-start(bf16[64,512]{1,0:T(8,128)(2,1)S(1)} %constant_dynamic-slice_fusion.2), channel_id=1, source_target_pairs={{0,1},{1,0},{2,3},{3,2},{4,5},{5,4},{6,7},{7,6},{8,9},{9,8},{10,11... | collective-permute-start | bytes 196616 | tf_op jit(solution)/shard_map/ppermute | solution.py:323
  23.8 19.9 %copy-start.19 = (bf16[64,384]{1,0:T(8,128)(2,1)}, bf16[64,384]{1,0:T(8,128)(2,1)S(1)}, u32[]{:S(2)}) copy-start(bf16[64,384]{1,0:T(8,128)(2,1)S(1)} %collective-permute-done.5) | copy-start | bytes 147460
  23.8 9.2 %collective-permute-start.9 = (bf16[64,512]{1,0:T(8,128)(2,1)S(1)}, bf16[64,512]{1,0:T(8,128)(2,1)S(1)}, u32[]{:S(2)}, u32[]{:S(2)}) collective-permute-start(bf16[64,512]{1,0:T(8,128)(2,1)S(1)} %constant_dynamic-slice_fusion.2), channel_id=1, source_target_pairs={{0,2},{1,3},{2,0},{3,1},{4,6},{5,7},{6,4},{7,5},{8,10},{9,11},{10,... | collective-permute-start | bytes 196616 | tf_op jit(solution)/shard_map/ppermute | solution.py:323
  26.1 35.2 %copy-start.10 = (bf16[1,128,384]{2,1,0:T(8,128)(2,1)S(1)}, bf16[1,128,384]{2,1,0:T(8,128)(2,1)}, u32[]{:S(2)}) copy-start(bf16[1,128,384]{2,1,0:T(8,128)(2,1)} %fusion.1) | copy-start | bytes 294916
  26.1 6.9 %copy-start.20 = (bf16[64,384]{1,0:T(8,128)(2,1)}, bf16[64,384]{1,0:T(8,128)(2,1)S(1)}, u32[]{:S(2)}) copy-start(bf16[64,384]{1,0:T(8,128)(2,1)S(1)} %collective-permute-done.6) | copy-start | bytes 147460
  26.1 17.6 %collective-permute-start.2 = (bf16[192,512]{1,0:T(8,128)(2,1)}, bf16[192,512]{1,0:T(8,128)(2,1)S(1)}, u32[]{:S(2)}, u32[]{:S(2)}) collective-permute-start(bf16[192,512]{1,0:T(8,128)(2,1)} %constant_dynamic-slice_fusion.3), channel_id=1, source_target_pairs={{0,3},{1,2},{2,1},{3,0},{4,7},{5,6},{6,5},{7,4},{8,11},{9,10},{10,... | collective-permute-start | bytes 589832 | tf_op jit(solution)/shard_map/ppermute | solution.py:323
  28.6 15.1 %copy-start.15 = (bf16[64,512]{1,0:T(8,128)(2,1)}, bf16[64,512]{1,0:T(8,128)(2,1)S(1)}, u32[]{:S(2)}) copy-start(bf16[64,512]{1,0:T(8,128)(2,1)S(1)} %collective-permute-done.8) | copy-start | bytes 196612
  28.6 8.1 %collective-permute-start.10 = (bf16[64,512]{1,0:T(8,128)(2,1)S(1)}, bf16[64,512]{1,0:T(8,128)(2,1)S(1)}, u32[]{:S(2)}, u32[]{:S(2)}) collective-permute-start(bf16[64,512]{1,0:T(8,128)(2,1)S(1)} %constant_dynamic-slice_fusion.2), channel_id=1, source_target_pairs={{0,3},{1,2},{2,1},{3,0},{4,7},{5,6},{6,5},{7,4},{8,11},{9,10},{10,... | collective-permute-start | bytes 196616 | tf_op jit(solution)/shard_map/ppermute | solution.py:323
  33.0 10.8 %copy-start.16 = (bf16[64,512]{1,0:T(8,128)(2,1)}, bf16[64,512]{1,0:T(8,128)(2,1)S(1)}, u32[]{:S(2)}) copy-start(bf16[64,512]{1,0:T(8,128)(2,1)S(1)} %collective-permute-done.9) | copy-start | bytes 196612
  33.0 13.6 %collective-permute-start.12 = (bf16[256,512]{1,0:T(8,128)(2,1)}, bf16[256,512]{1,0:T(8,128)(2,1)S(1)}, u32[]{:S(2)}, u32[]{:S(2)}) collective-permute-start(bf16[256,512]{1,0:T(8,128)(2,1)} %constant_dynamic-slice_fusion.1), channel_id=1, source_target_pairs={{0,1},{1,0},{2,3},{3,2},{4,5},{5,4},{6,7},{7,6},{8,9},{9,8},{10,11... | collective-permute-start | bytes 786440 | tf_op jit(solution)/shard_map/ppermute | solution.py:323
  36.7 9.9 %copy-start.17 = (bf16[64,512]{1,0:T(8,128)(2,1)}, bf16[64,512]{1,0:T(8,128)(2,1)S(1)}, u32[]{:S(2)}) copy-start(bf16[64,512]{1,0:T(8,128)(2,1)S(1)} %collective-permute-done.10) | copy-start | bytes 196612
  36.7 23.1 %collective-permute-start.13 = (bf16[256,512]{1,0:T(8,128)(2,1)}, bf16[256,512]{1,0:T(8,128)(2,1)S(1)}, u32[]{:S(2)}, u32[]{:S(2)}) collective-permute-start(bf16[256,512]{1,0:T(8,128)(2,1)} %constant_dynamic-slice_fusion.1), channel_id=1, source_target_pairs={{0,2},{1,3},{2,0},{3,1},{4,6},{5,7},{6,4},{7,5},{8,10},{9,11},{10,... | collective-permute-start | bytes 786440 | tf_op jit(solution)/shard_map/ppermute | solution.py:323
  40.4 4.4 copy-start.4
  40.4 19.4 %collective-permute-start.14 = (bf16[256,512]{1,0:T(8,128)(2,1)}, bf16[256,512]{1,0:T(8,128)(2,1)S(1)}, u32[]{:S(2)}, u32[]{:S(2)}) collective-permute-start(bf16[256,512]{1,0:T(8,128)(2,1)} %constant_dynamic-slice_fusion.1), channel_id=1, source_target_pairs={{0,3},{1,2},{2,1},{3,0},{4,7},{5,6},{6,5},{7,4},{8,11},{9,10},{10,... | collective-permute-start | bytes 786440 | tf_op jit(solution)/shard_map/ppermute | solution.py:323
  43.0 1.8 copy-start.6
  43.0 1.8 collective-permute-start.7
  43.7 2.8 copy-start.8
  43.8 17.5 %collective-permute-start.16 = (bf16[256,512]{1,0:T(8,128)(2,1)}, bf16[256,512]{1,0:T(8,128)(2,1)S(1)}, u32[]{:S(2)}, u32[]{:S(2)}) collective-permute-start(bf16[256,512]{1,0:T(8,128)(2,1)} %constant_dynamic-slice_fusion), channel_id=1, source_target_pairs={{0,1},{1,0},{2,3},{3,2},{4,5},{5,4},{6,7},{7,6},{8,9},{9,8},{10,11... | collective-permute-start | bytes 786440 | tf_op jit(solution)/shard_map/ppermute | solution.py:323
  44.7 36.8 %collective-permute-start.17 = (bf16[256,512]{1,0:T(8,128)(2,1)}, bf16[256,512]{1,0:T(8,128)(2,1)S(1)}, u32[]{:S(2)}, u32[]{:S(2)}) collective-permute-start(bf16[256,512]{1,0:T(8,128)(2,1)} %constant_dynamic-slice_fusion), channel_id=1, source_target_pairs={{0,2},{1,3},{2,0},{3,1},{4,6},{5,7},{6,4},{7,5},{8,10},{9,11},{10,... | collective-permute-start | bytes 786440 | tf_op jit(solution)/shard_map/ppermute | solution.py:323
  46.6 35.0 %collective-permute-start.18 = (bf16[256,512]{1,0:T(8,128)(2,1)}, bf16[256,512]{1,0:T(8,128)(2,1)S(1)}, u32[]{:S(2)}, u32[]{:S(2)}) collective-permute-start(bf16[256,512]{1,0:T(8,128)(2,1)} %constant_dynamic-slice_fusion), channel_id=1, source_target_pairs={{0,3},{1,2},{2,1},{3,0},{4,7},{5,6},{6,5},{7,4},{8,11},{9,10},{10,... | collective-permute-start | bytes 786440 | tf_op jit(solution)/shard_map/ppermute | solution.py:323
  59.8 22.8 %collective-permute-start.11 = (bf16[3,64,512]{2,1,0:T(8,128)(2,1)}, bf16[3,64,512]{2,1,0:T(8,128)(2,1)}, u32[]{:S(2)}, u32[]{:S(2)}) collective-permute-start(bf16[3,64,512]{2,1,0:T(8,128)(2,1)} %pad_maximum_fusion.8), channel_id=1, source_target_pairs={{0,4},{4,0},{8,12},{12,8},{16,20},{20,16},{24,28},{28,24},{1,5},{5... | collective-permute-start | bytes 589832 | tf_op jit(solution)/shard_map/ppermute | solution.py:325
  59.8 24.9 %collective-permute-start.3 = (bf16[3,192,512]{2,1,0:T(8,128)(2,1)}, bf16[3,192,512]{2,1,0:T(8,128)(2,1)}, u32[]{:S(2)}, u32[]{:S(2)}) collective-permute-start(bf16[3,192,512]{2,1,0:T(8,128)(2,1)} %pad_maximum_fusion.4), channel_id=1, source_target_pairs={{0,4},{4,0},{8,12},{12,8},{16,20},{20,16},{24,28},{28,24},{1,5},{5... | collective-permute-start | bytes 1769480 | tf_op jit(solution)/shard_map/ppermute | solution.py:325
  61.3 122.8 %collective-permute-start.15 = (bf16[3,256,512]{2,1,0:T(8,128)(2,1)}, bf16[3,256,512]{2,1,0:T(8,128)(2,1)}, u32[]{:S(2)}, u32[]{:S(2)}) collective-permute-start(bf16[3,256,512]{2,1,0:T(8,128)(2,1)} %pad_maximum_fusion.2), channel_id=1, source_target_pairs={{0,4},{4,0},{8,12},{12,8},{16,20},{20,16},{24,28},{28,24},{1,5},{5... | collective-permute-start | bytes 2359304 | tf_op jit(solution)/shard_map/ppermute | solution.py:325
  61.4 23.2 %copy-start = (bf16[4,128,192]{2,1,0:T(8,128)(2,1)}, bf16[4,128,192]{2,1,0:T(8,128)(2,1)S(1)}, u32[]{:S(2)}) copy-start(bf16[4,128,192]{2,1,0:T(8,128)(2,1)S(1)} %get-tuple-element.56) | copy-start | bytes 589828
  61.4 23.2 %copy-start.1 = (bf16[4,128,192]{2,1,0:T(8,128)(2,1)}, bf16[4,128,192]{2,1,0:T(8,128)(2,1)S(1)}, u32[]{:S(2)}) copy-start(bf16[4,128,192]{2,1,0:T(8,128)(2,1)S(1)} %get-tuple-element.57) | copy-start | bytes 589828
  63.3 20.5 %copy-start.12 = (bf16[128,512]{1,0:T(8,128)(2,1)S(1)}, bf16[128,512]{1,0:T(8,128)(2,1)}, u32[]{:S(2)}) copy-start(bf16[128,512]{1,0:T(8,128)(2,1)} %param.20) | copy-start | bytes 393220
  63.3 21.3 %copy-start.5 = (bf16[192,512]{1,0:T(8,128)(2,1)S(1)}, bf16[192,512]{1,0:T(8,128)(2,1)}, u32[]{:S(2)}) copy-start(bf16[192,512]{1,0:T(8,128)(2,1)} %copy-done.4) | copy-start | bytes 589828
  63.3 21.4 %copy-start.7 = (bf16[192,512]{1,0:T(8,128)(2,1)S(1)}, bf16[192,512]{1,0:T(8,128)(2,1)}, u32[]{:S(2)}) copy-start(bf16[192,512]{1,0:T(8,128)(2,1)} %copy-done.6) | copy-start | bytes 589828
  63.3 21.4 %copy-start.9 = (bf16[192,512]{1,0:T(8,128)(2,1)S(1)}, bf16[192,512]{1,0:T(8,128)(2,1)}, u32[]{:S(2)}) copy-start(bf16[192,512]{1,0:T(8,128)(2,1)} %copy-done.8) | copy-start | bytes 589828
  82.5 104.6 %collective-permute-start.19 = (bf16[3,256,512]{2,1,0:T(8,128)(2,1)}, bf16[3,256,512]{2,1,0:T(8,128)(2,1)}, u32[]{:S(2)}, u32[]{:S(2)}) collective-permute-start(bf16[3,256,512]{2,1,0:T(8,128)(2,1)} %pad_maximum_fusion.3), channel_id=1, source_target_pairs={{0,4},{4,0},{8,12},{12,8},{16,20},{20,16},{24,28},{28,24},{1,5},{5... | collective-permute-start | bytes 2359304 | tf_op jit(solution)/shard_map/ppermute | solution.py:325
  447.5 21.7 %all-to-all-start.1 = ((bf16[8,64,1280]{2,1,0:T(8,128)(2,1)}), bf16[8,64,1280]{2,1,0:T(8,128)(2,1)S(1)}, u32[]{:S(2)}, u32[]{:S(2)}) async-start(bf16[8,64,1280]{2,1,0:T(8,128)(2,1)} %bitcast.40), calls=%async_computation.1 | async-start | bytes 2621440 | tf_op jit(solution)/shard_map/all_to_all | solution.py:335

commit v2 on v1

v2 whole, which is shorter than its diff:
```python
import functools
import math

import jax
import jax.numpy as jnp
from jax import lax
from jax.experimental import pallas as pl
from jax.experimental.pallas import tpu as pltpu
from jax.sharding import PartitionSpec as P

F32 = jnp.float32
BF16 = jnp.bfloat16
GB = 128
TB = 3 * GB
NEG = -1e30
LOG2E = 1.0 / math.log(2.0)
VMEM = 60 * 1024 * 1024

ERF_P = 0.43
ERF_C = (
    0.24255178053871013,
    0.24376598744271377,
    0.2089868288055898,
    0.23281685899157548,
    -0.05797941172752005,
    0.3523368029188165,
    -0.2915198548110903,
    0.06904073943922798,
)


def nn(a, b):
    return lax.dot_general(a, b, (((1,), (0,)), ((), ())), preferred_element_type=F32)


def nt(a, b):
    return lax.dot_general(a, b, (((1,), (1,)), ((), ())), preferred_element_type=F32)


def tn(a, b):
    return lax.dot_general(a, b, (((0,), (0,)), ((), ())), preferred_element_type=F32)


def norm_rows(values):
    centred = values - jnp.mean(values, -1, keepdims=True)
    inv_std = lax.rsqrt(jnp.mean(centred * centred, -1, keepdims=True) + 1e-05)
    return centred * inv_std, inv_std


def norm_back(grad_out, gains, normed, inv_std):
    scaled = grad_out * gains
    return inv_std * (
        scaled
        - jnp.mean(scaled, -1, keepdims=True)
        - normed * jnp.mean(scaled * normed, -1, keepdims=True)
    )


def tap_major(scratch, values):
    lanes = scratch.shape[2]
    parts = []
    for c in range(scratch.shape[0]):
        scratch[c] = values[:, c * lanes : (c + 1) * lanes]
        taps = [scratch[c, pl.ds(r, GB, stride=3), :] for r in range(3)]
        parts.append(jnp.concatenate(taps, axis=0))
    return jnp.concatenate(parts, axis=1)


def token_major(scratch, values):
    lanes = scratch.shape[2]
    parts = []
    for c in range(scratch.shape[0]):
        for r in range(3):
            scratch[c, pl.ds(r, GB, stride=3), :] = values[
                r * GB : (r + 1) * GB, c * lanes : (c + 1) * lanes
            ]
        parts.append(scratch[c])
    return jnp.concatenate(parts, axis=1)


def gelu_and_slope(h):
    z = jnp.abs(h) * math.sqrt(0.5)
    t = 1.0 / (1.0 + ERF_P * z)
    poly = jnp.full_like(t, ERF_C[-1])
    for c in ERF_C[-2::-1]:
        poly = poly * t + c
    e = jnp.exp(-z * z)
    tail = (0.5 * e) * (poly * t)
    cdf = jnp.where(h >= 0, 1.0 - tail, tail)
    return h * cdf, cdf + h * (e * (1.0 / math.sqrt(2.0 * math.pi)))


def item_starts(lens_ref, block, longest_here, half):
    places = block * GB + lax.broadcasted_iota(jnp.int32, (1, GB), 1)
    starts = jnp.zeros((1, GB), jnp.int32)
    end = jnp.int32(0)
    for i in range(lens_ref.shape[0] - 1):
        end = end + jnp.where((lens_ref[i] == half) == longest_here, lens_ref[i], 0)
        starts = jnp.where(places >= end, end, starts)
    return places, starts


def longest_first(lens_ref, half):
    first, ahead = jnp.int32(0), jnp.int32(1)
    for i in range(lens_ref.shape[0]):
        ahead = jnp.where(lens_ref[i] == half, 0, ahead)
        first = first + ahead * lens_ref[i]
    return 3 * first


def own_taps(source, block, first, longest_here):
    half = source.shape[1] // 2
    base = block * TB
    parts = []
    for c in range(source.shape[0]):
        for r in range(3):
            inside = source[c, pl.ds(first + base + r, GB, stride=3), :]
            low = source[c, pl.ds(base + r, GB, stride=3), :]
            high = source[c, pl.ds(half + base + r, GB, stride=3), :]
            place = base + r + 3 * lax.broadcasted_iota(jnp.int32, (GB, 1), 0)
            parts.append(jnp.where(longest_here, inside, jnp.where(place < first, low, high)))
    return jnp.concatenate(
        [jnp.concatenate(parts[3 * c : 3 * c + 3], axis=0) for c in range(source.shape[0])], axis=1
    )


def mask_bias(places, starts, kb):
    keys = kb * GB + lax.broadcasted_iota(jnp.int32, (GB, GB), 0)
    bias = jnp.where((keys >= starts) & (keys < places), 0.0, NEG)
    return jnp.concatenate([bias] * 3, axis=1)


def key_rows(kb):
    return pl.ds(pl.multiple_of(kb * GB, GB), GB)


def remote(src, dst, sems, at, device):
    return pltpu.make_async_remote_copy(
        src_ref=src, dst_ref=dst, send_sem=sems.at[(0, *at)], recv_sem=sems.at[(1, *at)],
        device_id=device, device_id_type=pl.DeviceIdType.MESH,
    )


class Gather:
    def __init__(self, arrays, sems):
        self.arrays, self.sems = arrays, sems
        self.dp, self.tensor = lax.axis_index("dp"), lax.axis_index("tensor")
        self.peers = lax.axis_size("tensor")

    def half(self, array, slot):
        rows = array.shape[1] // 2
        start = pl.multiple_of(lax.rem(self.dp, 2) * rows, rows)
        return array.at[slot, pl.ds(start, rows)]

    def across(self, n, s):
        array = self.arrays[n]
        return remote(
            self.half(array, 0), self.half(array, s), self.sems, (n, 0, s - 1), (self.dp, self.tensor ^ s)
        )

    def beside(self, n, s):
        half = self.half(self.arrays[n], s)
        return remote(half, half, self.sems, (n, 1, s - 1), (self.dp ^ 1, self.tensor))

    def each(self):
        return [(n, s) for s in range(self.peers - 1, 0, -1) for n in range(len(self.arrays))]

    def start(self):
        for n, s in self.each():
            self.across(n, s).start()

    def pass_on(self):
        for n, s in self.each():
            self.across(n, s).wait_recv()
            self.beside(n, s).start()

    def arrive(self):
        for n, s in self.each():
            self.beside(n, s).wait_recv()

    def finish(self):
        for n, s in self.each():
            self.across(n, s).wait_send()
            self.beside(n, s).wait_send()


def forward_kernel(
    heads, hd, lens_ref, x_ref, g_ref, gain_ref, mask_ref, query_ref, key_ref, value_ref, kconv_ref, vconv_ref,
    out_ref, up_ref, down_ref,
    x_own, g_own, q_ref, k_ref, v_ref, ctx_ref, lse_ref, ck_ref, ckt_ref, cv_ref, w_all, conv_all,
    out_all, up_all, down_all,
    xs, gs, w_ref, conv_ref, cvt_ref, m_ref, l_ref, acc_ref, first_sems, last_sems, local_sems,
):
    block = pl.program_id(0)
    blocks = pl.num_programs(0)
    own_heads = kconv_ref.shape[0]
    own = own_heads * hd
    taps = kconv_ref.shape[1]
    scale = LOG2E / math.sqrt(hd)
    me, peer = lax.axis_index("dp"), lax.axis_index("tensor")
    first_gather = Gather((w_ref, conv_ref), first_sems)
    last_gather = Gather((out_all, up_all, down_all), last_sems)
    keep_copies = [
        pltpu.make_async_copy(w_ref, w_all, local_sems.at[3]), pltpu.make_async_copy(conv_ref, conv_all, local_sems.at[4])
    ]

    @pl.when(block == 0)
    def _():
        barrier = pltpu.get_barrier_semaphore()
        others = [(me, peer ^ s) for s in range(1, lax.axis_size("tensor"))] + [(me ^ 1, peer)]
        for device in others:
            pl.semaphore_signal(barrier, inc=1, device_id=device, device_id_type=pl.DeviceIdType.MESH)
        for n, src in enumerate((query_ref, key_ref, value_ref)):
            w_ref[0, n * own : (n + 1) * own, :] = src[...].T
        for n, src in enumerate((kconv_ref, vconv_ref)):
            conv_ref[0, n * taps : (n + 1) * taps, :] = jnp.concatenate([src[h] for h in range(own_heads)], axis=1)
        pl.semaphore_wait(barrier, len(others))
        first_gather.start()
        own_copies = [
            pltpu.make_async_copy(src, dst.at[0], local_sems.at[n])
            for n, (src, dst) in enumerate(((out_ref, out_all), (up_ref, up_all), (down_ref, down_all)))
        ]
        for copy in own_copies:
            copy.start()
        for src, dst in ((x_ref, xs), (g_ref, gs)):
            for c in range(dst.shape[0]):
                dst[c] = src[:, c * 128 : (c + 1) * 128].astype(F32)
        for copy in own_copies:
            copy.wait()
        first_gather.pass_on()
        last_gather.start()
        first_gather.arrive()
        first_gather.finish()
        for copy in keep_copies:
            copy.start()

    half = x_ref.shape[0] // 2
    longest_here = lax.rem(peer, 2) == 0
    first = longest_first(lens_ref, half // 3)
    x = own_taps(xs, block, first, longest_here)
    x_own[...] = x.astype(BF16)
    g_own[...] = own_taps(gs, block, first, longest_here).astype(BF16)
    normed, _ = norm_rows(x)
    first_in = (normed * gain_ref[...]).astype(BF16)
    mask = mask_ref[0, 0:1, :]
    for slot in range(w_ref.shape[0]):
        at = slice(slot * own, (slot + 1) * own)
        part = nt(w_ref[slot], first_in)
        q_ref[at, :] = part[0:own].astype(BF16)
        k_ref[at, :] = (part[own : 2 * own] * mask).astype(BF16)
        v_ref[at, :] = (part[2 * own : 3 * own] * mask).astype(BF16)
    rows = key_rows(block)
    for h in range(heads):
        band = slice(h * hd, (h + 1) * hd)
        slot, i = divmod(h, own_heads)
        for n, src, plain, trans in ((0, k_ref, ck_ref, ckt_ref), (1, v_ref, cv_ref, cvt_ref)):
            grouped = jnp.concatenate([src[band, r * GB : (r + 1) * GB] for r in range(3)], axis=0)
            comp = tn(conv_ref[slot, n * taps : (n + 1) * taps, i * hd : (i + 1) * hd], grouped)
            trans[band, rows] = comp.astype(BF16)
            plain[h, rows, :] = comp.T.astype(BF16)
        q, k = q_ref[band, :].astype(F32), k_ref[band, :].astype(F32)
        m_ref[h : h + 1, :] = jnp.sum(q * k, axis=0, keepdims=True) * scale
        acc_ref[band, :] = v_ref[band, :].astype(F32)
    l_ref[...] = jnp.ones_like(l_ref)
    places, starts = item_starts(lens_ref, block, longest_here, half // 3)

    def step(kb, carry):
        bias = mask_bias(places, starts, kb)
        cols = key_rows(kb)
        for h in range(heads):
            band = slice(h * hd, (h + 1) * hd)
            one = slice(h, h + 1)
            s = nn(ck_ref[h, cols, :], q_ref[band, :]) * scale + bias
            old = m_ref[one, :]
            new = jnp.maximum(old, jnp.max(s, axis=0, keepdims=True))
            p = jnp.exp2(s - new)
            keep = jnp.exp2(old - new)
            m_ref[one, :] = new
            l_ref[one, :] = l_ref[one, :] * keep + jnp.sum(p, axis=0, keepdims=True)
            acc_ref[band, :] = acc_ref[band, :] * keep + nn(cvt_ref[band, cols], p.astype(BF16))
        return carry

    lax.fori_loop(0, block + 1, step, 0)
    lse_ref[...] = m_ref[...] + jnp.log(l_ref[...]) * LOG2E
    inv = 1.0 / l_ref[...]
    for h in range(heads):
        band = slice(h * hd, (h + 1) * hd)
        ctx_ref[band, :] = (acc_ref[band, :] * inv[h : h + 1, :]).astype(BF16)

    @pl.when(block == blocks - 2)
    def _():
        last_gather.pass_on()

    @pl.when(block == blocks - 1)
    def _():
        last_gather.arrive()
        last_gather.finish()
        for copy in keep_copies:
            copy.wait()


def middle_kernel(
    heads, hd, x_ref, g_ref, gain_ref, ctx_ref, out_ref, up_ref, down_ref,
    mixed_ref, resid_grad_ref, dctx_ref, delta_ref, grads_ref,
    xs, down_sum, up_sum, out_sum, gain_sum,
):
    block = pl.program_id(0)
    own = out_sum.shape[0]

    @pl.when(block == 0)
    def _():
        down_sum[...] = jnp.zeros_like(down_sum)
        up_sum[...] = jnp.zeros_like(up_sum)
        out_sum[...] = jnp.zeros_like(out_sum)
        gain_sum[...] = jnp.zeros_like(gain_sum)

    gain = gain_ref[...]
    x = x_ref[...].astype(F32)
    g_low = g_ref[...]
    g = g_low.astype(F32)
    resid = x + tn(ctx_ref[...], out_ref[...])
    hat, inv_std = norm_rows(resid)
    second_in = (hat * gain).astype(BF16)
    ffn = jnp.zeros_like(resid)
    back = jnp.zeros_like(resid)
    for c in range(up_ref.shape[0]):
        hidden = nn(second_in, up_ref[c])
        act_grad = nt(g_low, down_ref[c])
        act, slope = gelu_and_slope(hidden)
        act = act.astype(BF16)
        hidden_grad = (act_grad * slope).astype(BF16)
        ffn = ffn + nn(act, down_ref[c])
        back = back + nt(hidden_grad, up_ref[c])
        if c < down_sum.shape[0]:
            down_sum[c] += tn(act, g_low)
            up_sum[c] += tn(second_in, hidden_grad)
    mixed_ref[...] = token_major(xs, resid + ffn).astype(BF16)
    gain_sum[...] += jnp.sum(back * hat, axis=0, keepdims=True)
    resid_grad = g + norm_back(back, gain, hat, inv_std)
    attn_grad = resid_grad.astype(BF16)
    resid_grad_ref[...] = attn_grad
    out_sum[...] += nn(ctx_ref[0:own, :], attn_grad)
    dctx = nt(out_ref[...], attn_grad).astype(BF16)
    dctx_ref[...] = dctx
    dots = dctx.astype(F32) * ctx_ref[...].astype(F32)
    for h in range(heads):
        delta_ref[h : h + 1, :] = jnp.sum(dots[h * hd : (h + 1) * hd], axis=0, keepdims=True)

    @pl.when(block == pl.num_programs(0) - 1)
    def _():
        units = up_sum.shape[2]
        at = 0
        for c in range(up_sum.shape[0]):
            grads_ref[:, at : at + units] = up_sum[c].astype(BF16)
            grads_ref[:, at + units : at + 2 * units] = down_sum[c].T.astype(BF16)
            at += 2 * units
        grads_ref[:, at : at + own] = out_sum[...].T.astype(BF16)
        grads_ref[:, at + own :] = jnp.broadcast_to(gain_sum[...], (GB, gain.shape[1])).T.astype(BF16)


def backward_kernel(
    heads, hd, own_heads, lens_ref, x_ref, gain_ref, w_ref, conv_ref, mask_ref,
    q_ref, k_ref, v_ref, lse_ref, dctx_ref, delta_ref, resid_grad_ref, ck_ref, ckt_ref, cv_ref,
    tokens_ref, grads_ref, conv_grads_ref,
    xs, dck_sum, dcv_sum, dq_sum, dqkv, weight_sum, kconv_sum, vconv_sum, gain_sum,
):
    step_id = pl.program_id(0)
    block = pl.num_programs(0) - 1 - step_id
    own = own_heads * hd
    slots, _, dim = w_ref.shape
    taps = conv_ref.shape[1] // 2
    slot_heads = heads // slots
    lanes = slot_heads * hd
    factor = 1.0 / math.sqrt(hd)
    scale = LOG2E * factor

    @pl.when(step_id == 0)
    def _():
        dck_sum[...] = jnp.zeros_like(dck_sum)
        dcv_sum[...] = jnp.zeros_like(dcv_sum)
        weight_sum[...] = jnp.zeros_like(weight_sum)
        kconv_sum[...] = jnp.zeros_like(kconv_sum)
        vconv_sum[...] = jnp.zeros_like(vconv_sum)
        gain_sum[...] = jnp.zeros_like(gain_sum)

    dq_sum[...] = jnp.zeros_like(dq_sum)
    longest_here = lax.rem(lax.axis_index("tensor"), 2) == 0
    places, starts = item_starts(lens_ref, block, longest_here, ck_ref.shape[1])

    def step(kb, carry):
        bias = mask_bias(places, starts, kb)
        cols = key_rows(kb)
        for h in range(heads):
            band = slice(h * hd, (h + 1) * hd)
            one = slice(h, h + 1)
            q, dctx = q_ref[band, :], dctx_ref[band, :]
            s = nn(ck_ref[h, cols, :], q) * scale + bias
            p = jnp.exp2(s - lse_ref[one, :])
            dp = nn(cv_ref[h, cols, :], dctx)
            ds = (p * (dp - delta_ref[one, :])).astype(BF16)
            dcv_sum[h, cols, :] += nt(p.astype(BF16), dctx)
            dck_sum[h, cols, :] += nt(ds, q)
            dq_sum[band, :] += nn(ckt_ref[band, cols], ds)
        return carry

    lax.fori_loop(0, block + 1, step, 0)
    mask = mask_ref[0, 0:1, :]
    rows = key_rows(block)
    for h in range(heads):
        band = slice(h * hd, (h + 1) * hd)
        one = slice(h, h + 1)
        q, k = q_ref[band, :].astype(F32), k_ref[band, :].astype(F32)
        v, dctx = v_ref[band, :].astype(F32), dctx_ref[band, :].astype(F32)
        own_prob = jnp.exp2(jnp.sum(q * k, axis=0, keepdims=True) * scale - lse_ref[one, :])
        own_dprob = jnp.sum(dctx * v, axis=0, keepdims=True)
        own_dscore = own_prob * (own_dprob - delta_ref[one, :]) * factor
        slot, i = divmod(h, slot_heads)
        base = slot * 3 * lanes + i * hd
        dqkv[base : base + hd, :] = (dq_sum[band, :] * factor + own_dscore * k).astype(BF16)
        dck = (dck_sum[h, rows, :] * factor).astype(BF16)
        dcv = dcv_sum[h, rows, :].astype(BF16)
        for n, src, total, grad, beside in (
            (0, k_ref, kconv_sum, dck, own_dscore * q),
            (1, v_ref, vconv_sum, dcv, own_prob * dctx),
        ):
            spread = nt(conv_ref[slot, n * taps : (n + 1) * taps, i * hd : (i + 1) * hd], grad)
            spread = jnp.concatenate([spread[r * hd : (r + 1) * hd] for r in range(3)], axis=1)
            at = base + (n + 1) * lanes
            dqkv[at : at + hd, :] = ((spread + beside) * mask).astype(BF16)
            if h < own_heads:
                grouped = jnp.concatenate([src[band, r * GB : (r + 1) * GB] for r in range(3)], axis=0)
                total[h] += nn(grouped, grad)
    hat, inv_std = norm_rows(x_ref[...].astype(F32))
    gain = gain_ref[...]
    first_in = (hat * gain).astype(BF16)
    weight_sum[...] += nn(dqkv[0 : 3 * own, :], first_in)
    back = tn(dqkv[...], w_ref[...].reshape(slots * 3 * lanes, dim))
    gain_sum[...] += jnp.sum(back * hat, axis=0, keepdims=True)
    total = resid_grad_ref[...].astype(F32) + norm_back(back, gain, hat, inv_std)
    tokens_ref[...] = token_major(xs, total).astype(BF16)

    @pl.when(block == 0)
    def _():
        grads_ref[:, 0 : 3 * own] = weight_sum[...].T.astype(BF16)
        grads_ref[:, 3 * own :] = jnp.broadcast_to(gain_sum[...], (GB, dim)).T.astype(BF16)
        for h in range(own_heads):
            conv_grads_ref[:, h * hd : (h + 1) * hd] = kconv_sum[h].astype(BF16)
            conv_grads_ref[:, (own_heads + h) * hd : (own_heads + h + 1) * hd] = vconv_sum[h].astype(BF16)


def whole(shape):
    return pl.BlockSpec(shape, lambda *_: (0,) * len(shape))


def cost(micros):
    return pl.CostEstimate(flops=int(micros * 1e9), bytes_accessed=1 << 20, transcendentals=0)


def params():
    return pltpu.CompilerParams(vmem_limit_bytes=VMEM, dimension_semantics=("arbitrary",))


def sent_and_summed(array):
    count = lax.axis_size("dp")
    parts = array.reshape(count, array.shape[0] // count, *array.shape[1:])
    parts = lax.all_to_all(parts, "dp", 0, 0, tiled=True)
    return jnp.sum(parts.astype(F32), axis=0)


def halves(lengths, rows):
    longest = jnp.argmax(lengths)
    before = jnp.arange(lengths.shape[0]) < longest
    first = 3 * jnp.sum(jnp.where(before, lengths, 0))
    return longest, first, jnp.arange(rows // 2, dtype=jnp.int32)


def own_rows(array, place, first, longest_here):
    half = place.shape[0]
    inside = lax.dynamic_slice_in_dim(array, first, half, 0)
    others = jnp.where(place < first, array[:half], array[half:])
    return jnp.where(longest_here, inside, others)


def all_rows(own, place, first, longest_here):
    half = place.shape[0]
    place = place[:, None]
    theirs = lax.ppermute(own, "tensor", neighbours("tensor"))
    inside = jnp.where(longest_here, own, theirs)
    others = jnp.where(longest_here, theirs, own)
    turned = lax.dynamic_slice_in_dim(jnp.concatenate([inside, inside]), half - first, half, 0)
    return jnp.concatenate(
        [jnp.where(place < first, others, turned), jnp.where(place < first, turned, others)]
    )


def neighbours(axis):
    return [(i, i ^ 1) for i in range(lax.axis_size(axis))]


def on_device(
    tokens, first_gain, second_gain, query_weight, key_weight, value_weight, out_weight,
    key_conv, value_conv, up_weight, down_weight, pad_mask, item_lengths, cotangent,
):
    dim = tokens.shape[1]
    own_heads, taps, hd = key_conv.shape
    peers = lax.axis_size("tensor")
    heads = own_heads * peers
    width = heads * hd
    own = own_heads * hd
    units = up_weight.shape[1]
    longest_here = lax.rem(lax.axis_index("tensor"), 2) == 0
    longest, first, place = halves(item_lengths[0], tokens.shape[0])
    lens = item_lengths[0]
    pack = (place, first, longest_here)
    rows = tokens.shape[0] // 2
    blocks = rows // TB
    groups = rows // 3
    mask = own_rows(pad_mask, *pack)
    mask = mask.reshape(blocks, GB, 3).transpose(0, 2, 1).reshape(blocks, 1, TB).astype(F32)
    gain1, gain2 = first_gain[None], second_gain[None]

    rows_spec = pl.BlockSpec((TB, dim), lambda b, *_: (b, 0))
    cols_spec = pl.BlockSpec((width, TB), lambda b, *_: (0, b))
    stat_spec = pl.BlockSpec((heads, TB), lambda b, *_: (0, b))
    mask_spec = pl.BlockSpec((1, 1, TB), lambda b, *_: (b, 0, 0))
    anywhere = pl.BlockSpec(memory_space=pl.ANY)
    inside = pl.BlockSpec(memory_space=pltpu.VMEM)
    x, g, q, k, v, ctx, lse, ck, ckt, cv, w_all, conv_all, out_all, up_all, down_all = pl.pallas_call(
        functools.partial(forward_kernel, heads, hd),
        grid_spec=pltpu.PrefetchScalarGridSpec(
            num_scalar_prefetch=1,
            grid=(blocks,),
            in_specs=[inside, inside, whole((1, dim)), mask_spec] + [inside] * 5 + [anywhere] * 3,
            out_specs=[
                rows_spec, rows_spec, cols_spec, cols_spec, cols_spec, cols_spec, stat_spec,
                whole((heads, groups, hd)), whole((width, groups)), whole((heads, groups, hd)),
                anywhere, anywhere, anywhere, anywhere, anywhere,
            ],
            scratch_shapes=[
                pltpu.VMEM((dim // 128, 2 * rows, 128), F32), pltpu.VMEM((dim // 128, 2 * rows, 128), F32),
                pltpu.VMEM((peers, 3 * own, dim), BF16), pltpu.VMEM((peers, 2 * taps, own), BF16),
                pltpu.VMEM((width, groups), BF16),
                pltpu.VMEM((heads, TB), F32), pltpu.VMEM((heads, TB), F32), pltpu.VMEM((width, TB), F32),
                pltpu.SemaphoreType.DMA((2, 2, 2, peers - 1)), pltpu.SemaphoreType.DMA((2, 3, 2, peers - 1)),
                pltpu.SemaphoreType.DMA((5,)),
            ],
        ),
        out_shape=[jax.ShapeDtypeStruct((rows, dim), BF16)] * 2
        + [jax.ShapeDtypeStruct((width, rows), BF16)] * 4
        + [
            jax.ShapeDtypeStruct((heads, rows), F32),
            jax.ShapeDtypeStruct((heads, groups, hd), BF16),
            jax.ShapeDtypeStruct((width, groups), BF16),
            jax.ShapeDtypeStruct((heads, groups, hd), BF16),
            jax.ShapeDtypeStruct((peers, 3 * own, dim), BF16),
            jax.ShapeDtypeStruct((peers, 2 * taps, own), BF16),
            jax.ShapeDtypeStruct((peers, own, dim), BF16),
            jax.ShapeDtypeStruct((peers, dim, units), BF16),
            jax.ShapeDtypeStruct((peers, units, dim), BF16),
        ],
        compiler_params=pltpu.CompilerParams(
            vmem_limit_bytes=VMEM, dimension_semantics=("arbitrary",), collective_id=0, has_side_effects=True
        ),
        cost_estimate=cost(55),
        name="attention_forward",
    )(
        lens, tokens, cotangent, gain1, mask, query_weight, key_weight, value_weight, key_conv, value_conv,
        out_weight, up_weight, down_weight,
    )

    mid_cols = 4 * units + 2 * own + GB
    mixed, resid_grad, dctx, delta, middle_grads = pl.pallas_call(
        functools.partial(middle_kernel, heads, hd),
        grid=(blocks,),
        in_specs=[
            rows_spec, rows_spec, whole((1, dim)), cols_spec, whole((width, dim)),
            whole((peers, dim, units)), whole((peers, units, dim)),
        ],
        out_specs=[rows_spec, rows_spec, cols_spec, stat_spec, whole((dim, mid_cols))],
        out_shape=[
            jax.ShapeDtypeStruct((rows, dim), BF16),
            jax.ShapeDtypeStruct((rows, dim), BF16),
            jax.ShapeDtypeStruct((width, rows), BF16),
            jax.ShapeDtypeStruct((heads, rows), F32),
            jax.ShapeDtypeStruct((dim, mid_cols), BF16),
        ],
        scratch_shapes=[
            pltpu.VMEM((dim // 128, TB, 128), F32), pltpu.VMEM((2, units, dim), F32),
            pltpu.VMEM((2, dim, units), F32), pltpu.VMEM((2 * own, dim), F32), pltpu.VMEM((1, dim), F32),
        ],
        compiler_params=params(),
        cost_estimate=cost(55),
        name="feed_forward",
    )(x, g, gain2, ctx, out_all.reshape(width, dim), up_all, down_all)
    mixed_out = all_rows(mixed, *pack)
    middle_share = sent_and_summed(middle_grads)

    back_rows = pl.BlockSpec((TB, dim), lambda b, *_: (blocks - 1 - b, 0))
    back_cols = pl.BlockSpec((width, TB), lambda b, *_: (0, blocks - 1 - b))
    back_stat = pl.BlockSpec((heads, TB), lambda b, *_: (0, blocks - 1 - b))
    back_mask = pl.BlockSpec((1, 1, TB), lambda b, *_: (blocks - 1 - b, 0, 0))
    two = 2 * own_heads
    grad_rows, last_grads, conv_grads = pl.pallas_call(
        functools.partial(backward_kernel, heads, hd, two),
        grid_spec=pltpu.PrefetchScalarGridSpec(
            num_scalar_prefetch=1,
            grid=(blocks,),
            in_specs=[
                back_rows, whole((1, dim)), whole((peers, 3 * own, dim)), whole((peers, 2 * taps, own)), back_mask, back_cols, back_cols, back_cols, back_stat,
                back_cols, back_stat, back_rows, whole((heads, groups, hd)), whole((width, groups)),
                whole((heads, groups, hd)),
            ],
            out_specs=[back_rows, whole((dim, 6 * own + GB)), whole((taps, 4 * own))],
            scratch_shapes=[
                pltpu.VMEM((dim // 128, TB, 128), F32), pltpu.VMEM((heads, groups, hd), F32),
                pltpu.VMEM((heads, groups, hd), F32), pltpu.VMEM((width, TB), F32),
                pltpu.VMEM((3 * width, TB), BF16), pltpu.VMEM((6 * own, dim), F32),
                pltpu.VMEM((two, taps, hd), F32), pltpu.VMEM((two, taps, hd), F32),
                pltpu.VMEM((1, dim), F32),
            ],
        ),
        out_shape=[
            jax.ShapeDtypeStruct((rows, dim), BF16),
            jax.ShapeDtypeStruct((dim, 6 * own + GB), BF16),
            jax.ShapeDtypeStruct((taps, 4 * own), BF16),
        ],
        compiler_params=params(),
        cost_estimate=cost(60),
        name="attention_backward",
    )(lens, x, gain1, w_all, conv_all, mask, q, k, v, lse, dctx, delta, resid_grad, ck, ckt, cv)
    grad_tokens = all_rows(grad_rows, *pack)
    last_share = sent_and_summed(last_grads)
    conv_share = sent_and_summed(conv_grads).reshape(-1, 2, 2, own)

    def parts(slot):
        half = 2 * units
        return (
            middle_share[:, slot * half : slot * half + half],
            middle_share[:, 2 * half + slot * own : 2 * half + slot * own + own],
            middle_share[:, 2 * half + 2 * own],
            *(last_share[:, (3 * slot + n) * own : (3 * slot + n + 1) * own] for n in range(3)),
            last_share[:, 6 * own],
            conv_share[:, :, slot],
        )

    shapes = [p.shape for p in parts(1)]
    sizes = [math.prod(d) for d in shapes]
    ends = [sum(sizes[: n + 1]) for n in range(len(sizes))]
    theirs = lax.ppermute(
        jnp.concatenate([p.reshape(-1) for p in parts(1)]).astype(BF16), "tensor", neighbours("tensor")
    ).astype(F32)
    ff, out, gain2_grad, query, key, value, gain1_grad, conv = (
        p + t.reshape(d) for p, t, d in zip(parts(0), jnp.split(theirs, ends[:-1]), shapes)
    )
    conv = conv.reshape(-1, 2, own_heads, hd).transpose(1, 2, 0, 3)
    return (
        mixed_out,
        grad_tokens,
        gain1_grad,
        gain2_grad,
        query,
        key,
        value,
        out.T,
        conv[0],
        conv[1],
        ff[:, :units],
        ff[:, units:].T,
    )


def solution(mesh):
    in_specs = (
        P("dp", None),
        P(),
        P(),
        P(None, "tensor"),
        P(None, "tensor"),
        P(None, "tensor"),
        P("tensor", None),
        P("tensor", None, None),
        P("tensor", None, None),
        P(None, "tensor"),
        P("tensor", None),
        P("dp"),
        P("dp", None),
        P("dp", None),
    )
    out_specs = (
        P("dp", None),
        P("dp", None),
        P("dp"),
        P("dp"),
        P("dp", "tensor"),
        P("dp", "tensor"),
        P("dp", "tensor"),
        P("tensor", "dp"),
        P("tensor", "dp", None),
        P("tensor", "dp", None),
        P("dp", "tensor"),
        P("tensor", "dp"),
    )
    return jax.shard_map(
        on_device, mesh=mesh, in_specs=in_specs, out_specs=out_specs, check_vma=False
    )
```

time: 468 us -> 398 us (0.85)
  Pallas kernels: 301 us -> 233 us
  waiting for transfers between devices: 54.2 us -> 97 us
  starting transfers between devices: 31.3 us -> 5.79 us
  blocking collectives: 52.4 us -> 27.7 us
  other arithmetic: 16.8 us -> 23.8 us
  local copies, waits for them, and re-layouts: 14.7 us -> 8.68 us
    pallas_call x1, Pallas kernels: 102 us -> 57.5 us  [on_device(): pl.pallas_call(functools.partial(middle_kernel, heads, hd), grid=(blocks,...]
    pallas_call x1, Pallas kernels: 102 us -> 60.1 us  [on_device(): pl.pallas_call(functools.partial(backward_kernel, heads, hd, two), grid_s...]
    ppermute x20 -> x3, waiting for transfers between devices: 38.7 us -> 70.3 us  [the longest x2 70.3 us: all_rows(): theirs = lax.ppermute(own, 'tensor', neighbours('tensor'))]
    ppermute x20 -> x3, starting transfers between devices: 27.7 us -> 2.17 us  [the longest x2 2.1 us: all_rows(): theirs = lax.ppermute(own, 'tensor', neighbours('tensor'))]
    all_to_all x2, blocking collectives: 52.4 us -> 27.7 us  [sent_and_summed(): parts = lax.all_to_all(parts, 'dp', 0, 0, tiled=True)]
    pallas_call x1, Pallas kernels: 96.2 us -> 115 us  [on_device(): pl.pallas_call(functools.partial(forward_kernel, heads, hd), grid_spec=pl...]
    all_to_all x1, waiting for transfers between devices: 15.4 us -> 26.6 us  [sent_and_summed(): parts = lax.all_to_all(parts, 'dp', 0, 0, tiled=True)]
    select_n x5 -> x3, other arithmetic: 7.26 us -> 12 us  [the longest x1 9.85 us: all_rows(): jnp.where(place < first, others, turned)]
  transfers between devices with their start and end apart: 21 -> 4, of which waited for: 7 -> 3; matrix products, arithmetic and copies ran while one was open for 5% -> 5% of each run, Pallas kernels for 20% -> 0%
where the time goes in v2:
time: 398 us; the launch traced here: 397 us
  Pallas kernels  233 us (59%)
  waiting for transfers between devices  97 us (24%)
  blocking collectives  27.7 us (7%)
  other arithmetic  23.8 us (6%)
  local copies, waits for them, and re-layouts  8.68 us (2%)
  starting transfers between devices  5.79 us (1%)
    pallas_call x1, Pallas kernels, on_device(): pl.pallas_call(functools.partial(forward_kernel, heads, hd), grid_spec=pl...  115 us
    ppermute x2, waiting for transfers between devices, all_rows(): theirs = lax.ppermute(own, 'tensor', neighbours('tensor'))  70.3 us
    pallas_call x1, Pallas kernels, on_device(): pl.pallas_call(functools.partial(backward_kernel, heads, hd, two), grid_s...  60.1 us
    pallas_call x1, Pallas kernels, on_device(): pl.pallas_call(functools.partial(middle_kernel, heads, hd), grid=(blocks,...  57.5 us
    all_to_all x2, blocking collectives, sent_and_summed(): parts = lax.all_to_all(parts, 'dp', 0, 0, tiled=True)  27.7 us
    all_to_all x1, waiting for transfers between devices, sent_and_summed(): parts = lax.all_to_all(parts, 'dp', 0, 0, tiled=True)  26.6 us
    select_n x1, other arithmetic, all_rows(): jnp.where(place < first, others, turned)  9.85 us
  transfers between devices with their start and end apart: 4, of which 3 were waited for; matrix products, arithmetic and copies ran while one was open for 5% of the time, Pallas kernels for 0%

profile of v2, /device:TPU:0, one launch (start us, length us, event | category | flops | bytes accessed | tf_op | source)
XLA Modules:
  0.0 397.4 jit_solution(12954034479719440837)
XLA Ops:
  0.6 1.3 iota_reduce_fusion
  2.0 1.9 fusion.9
  4.6 0.9 select_convert_fusion
  5.5 0.3 convert_element_type.23
  5.7 0.1 copy.35
  5.9 0.6 convert_element_type.25.mask_ref
  6.5 1.6 copy.36.kconv_ref
  8.1 1.6 copy.37.vconv_ref
  9.7 115.3 %attention_forward.1 = (bf16[2304,512]{1,0:T(8,128)(2,1)}, bf16[2304,512]{1,0:T(8,128)(2,1)}, bf16[512,2304]{1,0:T(8,128)(2,1)}, bf16[512,2304]{1,0:T(8,128)(2,1...) custom-call(s32[6]{0:T(128)} %bitcast.63, ...), custom_call_target="tpu_custom_call" | custom-call | flops 54999998464 | bytes 1048576 | tf_op jit(solution)/shard_map/attention_forward/pallas_call | solution.py:528
  125.0 57.5 %feed_forward.1 = (bf16[2304,512]{1,0:T(8,128)(2,1)}, bf16[2304,512]{1,0:T(8,128)(2,1)}, bf16[512,2304]{1,0:T(8,128)(2,1)}, f32[8,2304]{1,0:T(8,128)}, bf16[512,2432]{1,0:T(8,128)(2,1)}) custom-call(bf16[2304,512]{1,0:T(8,128)(2,1)} %get-tuple-element.37.x_ref, bf16[2304,512]{1,0:T(8,128)(2,1)} %get-tuple-element.38.g_ref, f32[1,512]{1,0:T(1,128)} %bitcast.60, ...), custom_call_target="tpu_custom_call" | custom-call | flops 54999998464 | bytes 1048576 | tf_op jit(solution)/shard_map/feed_forward/pallas_call | solution.py:572
  182.5 60.1 %attention_backward.1 = (bf16[2304,512]{1,0:T(8,128)(2,1)}, bf16[512,896]{1,0:T(8,128)(2,1)}, bf16[192,512]{1,0:T(8,128)(2,1)}) custom-call(s32[6]{0:T(128)} %bitcast.64, bf16[2304,512]{1,0:T(8,128)(2,1)} %get-tuple-element.37.x_ref, f32[1,512]{1,0:T(1,128)} %bitcast.62, bf16[4,384,512]{2,1,0:T(8,128)(2,1)} %get-tuple-element.44.w_ref, ...), custom_call_target="tpu_custom_call" | custom-call | flops 60000002048 | bytes 1048576 | tf_op jit(solution)/shard_map/attention_backward/pallas_call | solution.py:603
  242.6 10.2 %all_to_all.15 = bf16[8,24,512]{2,1,0:T(8,128)(2,1)} all-to-all(bf16[8,24,512]{2,1,0:T(8,128)(2,1)} %bitcast.58), channel_id=1, replica_groups=mesh['dp'=8,'tensor'=4] {'dp'}, dimensions={0} | all-to-all | bytes 393216 | tf_op jit(solution)/shard_map/all_to_all | solution.py:466
  252.9 17.4 %all_to_all.16 = bf16[8,64,896]{2,1,0:T(8,128)(2,1)S(1)} all-to-all(bf16[8,64,896]{2,1,0:T(8,128)(2,1)} %bitcast.56), channel_id=1, replica_groups=mesh['dp'=8,'tensor'=4] {'dp'}, dimensions={0} | all-to-all | bytes 1835008 | tf_op jit(solution)/shard_map/all_to_all | solution.py:466
  270.3 3.6 all-to-all-start.1
  273.9 0.1 collective-permute-start
  274.0 2.0 collective-permute-start.1
  276.0 1.0 convert_reduce_fusion.2
  277.1 0.1 squeeze.24
  277.2 0.1 fusion.8
  277.2 0.1 convert_reduce_fusion.1
  277.4 0.0 copy-start.2
  277.4 0.1 slice_reduce_fusion.1
  277.5 0.5 copy-done.2
  278.1 26.6 %all-to-all-done.1 = bf16[8,64,2432]{2,1,0:T(8,128)(2,1)S(1)} async-done(((bf16[8,64,2432]{2,1,0:T(8,128)(2,1)}), bf16[8,64,2432]{2,1,0:T(8,128)(2,1)S(1)}, u32[]{:S(2)}, u32[]{:S(2)}) %all-to-all-start.1) | async-done | bytes 2490400 | tf_op jit(solution)/shard_map/all_to_all | solution.py:466
  304.7 0.3 convert_reduce_fusion
  305.1 0.1 slice_reduce_fusion
  305.3 1.3 concatenate.20
  306.6 0.0 copy-start.1
  306.6 0.1 collective-permute-start.2
  306.7 21.7 %collective-permute-done = bf16[2304,512]{1,0:T(8,128)(2,1)} collective-permute-done((bf16[2304,512]{1,0:T(8,128)(2,1)}, bf16[2304,512]{1,0:T(8,128)(2,1)}, u32[]{:S(2)}, u32[]{:S(2)}) %collective-permute-start) | collective-permute-done | bytes 2359328 | tf_op jit(solution)/shard_map/ppermute | solution.py:487
  328.4 1.9 broadcast_select_fusion.6
  330.3 0.0 copy-start
  330.3 48.6 %collective-permute-done.1 = bf16[2304,512]{1,0:T(8,128)(2,1)} collective-permute-done((bf16[2304,512]{1,0:T(8,128)(2,1)}, bf16[2304,512]{1,0:T(8,128)(2,1)}, u32[]{:S(2)}, u32[]{:S(2)}) %collective-permute-start.1) | collective-permute-done | bytes 2359328 | tf_op jit(solution)/shard_map/ppermute | solution.py:487
  378.9 0.0 copy-done.1
  378.9 0.2 broadcast_select_fusion.4
  379.2 0.0 copy-done
  379.2 9.9 %broadcast_select_fusion.1 = (bf16[2304,512]{1,0:T(8,128)(2,1)S(1)}, bf16[2304,512]{1,0:T(8,128)(2,1)S(1)}, bf16[2304,512]{1,0:T(8,128)(2,1)S(1)}, bf16[2304,512]{1,0:T(8,128)(2,1)S(1)}) fusion(pred[2304]{0:T(1024)(128)(4,1)S(1)} %iota_compare_fusion, bf16[2304,512]{1,0:T(8,128)(2,1)} %collective-permute-done.1, bf16[2304,512]{1,0:T(8,128)(2,1)S(1)} %copy-done.1, ...), kind=kLoop, calls=%fused_computation.10 | loop fusion | flops 25952256 | bytes 23595268 | tf_op jit(solution)/shard_map/jit(_where)/select_n | solution.py:492
  389.1 4.0 %pad_maximum_fusion = (bf16[4608,512]{1,0:T(8,128)(2,1)}, bf16[4608,512]{1,0:T(8,128)(2,1)}) fusion(bf16[2304,512]{1,0:T(8,128)(2,1)S(1)} %get-tuple-element.101, bf16[2304,512]{1,0:T(8,128)(2,1)S(1)} %get-tuple-element.102, bf16[2304,512]{1,0:T(8,128)(2,1)S(1)} %get-tuple-element.85, bf16[2304,512]{1,0:T(8,128)(2,1)S(1)} %get-tuple-element.84), kind=kLoop, calls=%fused_computation.3 | loop fusion | flops 18874368 | bytes 18874368 | tf_op jit(solution)/shard_map/concatenate | solution.py:491
  393.1 0.0 collective-permute-done.2
  393.1 1.5 fusion.5
  394.6 0.6 slice_add_fusion.1
  395.3 0.7 slice_bitcast_fusion
  396.0 0.1 reshape.120
  396.2 0.6 copy.40
  396.8 0.6 copy.41
  (19 shorter events, 0.3 us)
Async XLA Ops:
  270.3 34.4 %all-to-all-start.1 = ((bf16[8,64,2432]{2,1,0:T(8,128)(2,1)}), bf16[8,64,2432]{2,1,0:T(8,128)(2,1)S(1)}, u32[]{:S(2)}, u32[]{:S(2)}) async-start(bf16[8,64,2432]{2,1,0:T(8,128)(2,1)} %bitcast.54), calls=%async_computation.1 | async-start | bytes 4980736 | tf_op jit(solution)/shard_map/all_to_all | solution.py:466
  273.9 54.5 %collective-permute-start = (bf16[2304,512]{1,0:T(8,128)(2,1)}, bf16[2304,512]{1,0:T(8,128)(2,1)}, u32[]{:S(2)}, u32[]{:S(2)}) collective-permute-start(bf16[2304,512]{1,0:T(8,128)(2,1)} %get-tuple-element.43), channel_id=1, source_target_pairs={{0,1},{1,0},{2,3},{3,2},{4,5},{5,4},{6,7},{7,6},{8,9},{9,8},{10,11... | collective-permute-start | bytes 7077896 | tf_op jit(solution)/shard_map/ppermute | solution.py:487
  274.0 104.9 %collective-permute-start.1 = (bf16[2304,512]{1,0:T(8,128)(2,1)}, bf16[2304,512]{1,0:T(8,128)(2,1)}, u32[]{:S(2)}, u32[]{:S(2)}) collective-permute-start(bf16[2304,512]{1,0:T(8,128)(2,1)} %get-tuple-element.56), channel_id=1, source_target_pairs={{0,1},{1,0},{2,3},{3,2},{4,5},{5,4},{6,7},{7,6},{8,9},{9,8},{10,11... | collective-permute-start | bytes 7077896 | tf_op jit(solution)/shard_map/ppermute | solution.py:487
  277.4 0.7 copy-start.2
  306.6 72.4 %copy-start.1 = (bf16[2304,512]{1,0:T(8,128)(2,1)S(1)}, bf16[2304,512]{1,0:T(8,128)(2,1)}, u32[]{:S(2)}) copy-start(bf16[2304,512]{1,0:T(8,128)(2,1)} %get-tuple-element.56) | copy-start | bytes 7077892
  306.6 86.5 %collective-permute-start.2 = (bf16[104576]{0:T(1024)(128)(2,1)S(1)}, bf16[104576]{0:T(1024)(128)(2,1)S(1)}, u32[]{:S(2)}, u32[]{:S(2)}) collective-permute-start(bf16[104576]{0:T(1024)(128)(2,1)S(1)} %concatenate.20), channel_id=1, source_target_pairs={{0,1},{1,0},{2,3},{3,2},{4,5},{5,4},{6,7},{7,6},{8,9},{9,8},{10,11... | collective-permute-start | bytes 627464 | tf_op jit(solution)/shard_map/ppermute | solution.py:649
  330.3 48.9 %copy-start = (bf16[2304,512]{1,0:T(8,128)(2,1)S(1)}, bf16[2304,512]{1,0:T(8,128)(2,1)}, u32[]{:S(2)}) copy-start(bf16[2304,512]{1,0:T(8,128)(2,1)} %get-tuple-element.43) | copy-start | bytes 7077892

commit v3 on v2

--- a/solution.py
+++ b/solution.py
@@ -139,6 +139,101 @@
         src_ref=src, dst_ref=dst, send_sem=sems.at[(0, *at)], recv_sem=sems.at[(1, *at)],
         device_id=device, device_id_type=pl.DeviceIdType.MESH,
     )
+
+
+def meet(devices):
+    barrier = pltpu.get_barrier_semaphore()
+    for device in devices:
+        pl.semaphore_signal(barrier, inc=1, device_id=device, device_id_type=pl.DeviceIdType.MESH)
+    pl.semaphore_wait(barrier, len(devices))
+
+
+def put_rows(ref, pieces):
+    count, rows, _ = ref.shape
+    at = 0
+    for piece in pieces:
+        cols = piece.shape[1]
+        for d in range(count):
+            ref[d, :, at : at + cols] = piece[d * rows : (d + 1) * rows].astype(ref.dtype)
+        at += cols
+
+
+class Swap:
+    def __init__(self, staged, mine, theirs, sems, local_sems):
+        self.staged, self.mine, self.theirs, self.sems, self.local_sems = staged, mine, theirs, sems, local_sems
+        self.device = (lax.axis_index("dp"), lax.axis_index("tensor") ^ 1)
+        self.blocks = mine.shape[0] // TB
+
+    def rows(self, block):
+        return pl.ds(pl.multiple_of(block * TB, TB), TB)
+
+    def local(self, step, block):
+        staged = self.staged.at[lax.rem(step, 2)]
+        return pltpu.make_async_copy(staged, self.mine.at[self.rows(block)], self.local_sems.at[step])
+
+    def far(self, step, block):
+        staged = self.staged.at[lax.rem(step, 2)]
+        return remote(staged, self.theirs.at[self.rows(block)], self.sems, (step,), self.device)
+
+    def settle(self, step, block):
+        self.local(step, block).wait()
+        self.far(step, block).wait_send()
+
+    def send(self, step, block, values):
+        @pl.when(step >= 2)
+        def _():
+            self.settle(step - 2, block)
+
+        self.staged[lax.rem(step, 2)] = values
+        self.local(step, block).start()
+        self.far(step, block).start()
+
+    def finish(self, block):
+        for step in range(max(self.blocks - 2, 0), self.blocks):
+            self.settle(step, block)
+        for step in range(self.blocks):
+            self.far(step, block).wait_recv()
+
+
+class Spread:
+    def __init__(self, source, landed, total, sems, local_sem):
+        self.source, self.landed, self.sums, self.sems, self.local_sem = source, landed, total, sems, local_sem
+        self.me, self.peer = lax.axis_index("dp"), lax.axis_index("tensor")
+        self.count = lax.axis_size("dp")
+
+    def copy(self, s):
+        there = lax.rem(self.me + s, self.count)
+        return remote(self.source.at[there], self.landed.at[s], self.sems, (s,), (there, self.peer))
+
+    def own(self):
+        return pltpu.make_async_copy(self.source.at[self.me], self.landed.at[0], self.local_sem)
+
+    def start(self):
+        self.own().start()
+
+        def step(s, carry):
+            self.copy(s).start()
+            return carry
+
+        lax.fori_loop(1, self.count, step, 0)
+
+    def total(self):
+        self.own().wait()
+
+        def step(s, carry):
+            self.copy(s).wait()
+            return carry
+
+        lax.fori_loop(1, self.count, step, 0)
+
+        self.sums[...] = self.landed[0].astype(F32)
+
+        def add(s, carry):
+            self.sums[...] += self.landed[s].astype(F32)
+            return carry
+
+        lax.fori_loop(1, self.count, add, 0)
+        return self.sums
 
 
 class Gather:
@@ -301,14 +396,16 @@
 
 def middle_kernel(
     heads, hd, x_ref, g_ref, gain_ref, ctx_ref, out_ref, up_ref, down_ref,
-    mixed_ref, resid_grad_ref, dctx_ref, delta_ref, grads_ref,
-    xs, down_sum, up_sum, out_sum, gain_sum,
+    mixed_ref, mixed_peer, resid_grad_ref, dctx_ref, delta_ref, grads_ref,
+    staged, down_sum, up_sum, out_sum, gain_sum, sems, local_sems,
 ):
     block = pl.program_id(0)
     own = out_sum.shape[0]
+    swap = Swap(staged, mixed_ref, mixed_peer, sems, local_sems)
 
     @pl.when(block == 0)
     def _():
+        meet([swap.device])
         down_sum[...] = jnp.zeros_like(down_sum)
         up_sum[...] = jnp.zeros_like(up_sum)
         out_sum[...] = jnp.zeros_like(out_sum)
@@ -334,7 +431,7 @@
         if c < down_sum.shape[0]:
             down_sum[c] += tn(act, g_low)
             up_sum[c] += tn(second_in, hidden_grad)
-    mixed_ref[...] = token_major(xs, resid + ffn).astype(BF16)
+    swap.send(block, block, (resid + ffn).astype(BF16))
     gain_sum[...] += jnp.sum(back * hat, axis=0, keepdims=True)
     resid_grad = g + norm_back(back, gain, hat, inv_std)
     attn_grad = resid_grad.astype(BF16)
@@ -348,21 +445,26 @@
 
     @pl.when(block == pl.num_programs(0) - 1)
     def _():
-        units = up_sum.shape[2]
-        at = 0
-        for c in range(up_sum.shape[0]):
-            grads_ref[:, at : at + units] = up_sum[c].astype(BF16)
-            grads_ref[:, at + units : at + 2 * units] = down_sum[c].T.astype(BF16)
-            at += 2 * units
-        grads_ref[:, at : at + own] = out_sum[...].T.astype(BF16)
-        grads_ref[:, at + own :] = jnp.broadcast_to(gain_sum[...], (GB, gain.shape[1])).T.astype(BF16)
+        put_rows(
+            grads_ref,
+            [
+                piece
+                for c in range(up_sum.shape[0])
+                for piece in (up_sum[c], down_sum[c].T, out_sum[c * own // 2 : (c + 1) * own // 2].T)
+            ]
+            + [jnp.broadcast_to(gain_sum[...], (GB, gain.shape[1])).T],
+        )
+        swap.finish(block)
 
 
 def backward_kernel(
     heads, hd, own_heads, lens_ref, x_ref, gain_ref, w_ref, conv_ref, mask_ref,
-    q_ref, k_ref, v_ref, lse_ref, dctx_ref, delta_ref, resid_grad_ref, ck_ref, ckt_ref, cv_ref,
-    tokens_ref, grads_ref, conv_grads_ref,
-    xs, dck_sum, dcv_sum, dq_sum, dqkv, weight_sum, kconv_sum, vconv_sum, gain_sum,
+    q_ref, k_ref, v_ref, lse_ref, dctx_ref, delta_ref, resid_grad_ref, ck_ref, ckt_ref, cv_ref, middle_ref,
+    tokens_ref, tokens_peer, middle_out, last_out, conv_out,
+    staged, dck_sum, dcv_sum, dq_sum, dqkv, weight_sum, kconv_sum, vconv_sum, gain_sum,
+    middle_in, last_parts, last_in, conv_parts, conv_in,
+    middle_turn, last_turn, conv_turn, middle_sum, last_sum, conv_sum,
+    swap_sems, swap_local, middle_sems, last_sems, conv_sems, turn_sems, local_sems,
 ):
     step_id = pl.program_id(0)
     block = pl.num_programs(0) - 1 - step_id
@@ -373,9 +475,23 @@
     lanes = slot_heads * hd
     factor = 1.0 / math.sqrt(hd)
     scale = LOG2E * factor
+    swap = Swap(staged, tokens_ref, tokens_peer, swap_sems, swap_local)
+    middle = Spread(middle_ref, middle_in, middle_sum, middle_sems, local_sems.at[0])
+    last = Spread(last_parts, last_in, last_sum, last_sems, local_sems.at[1])
+    convs = Spread(conv_parts, conv_in, conv_sum, conv_sems, local_sems.at[2])
+
+    def turned(n, ref):
+        return remote(ref.at[0], ref.at[1], turn_sems, (n,), swap.device)
+
+    def turn(n, ref, total):
+        ref[0] = total[:, total.shape[1] - ref.shape[2] :].astype(BF16)
+        turned(n, ref).start()
 
     @pl.when(step_id == 0)
     def _():
+        count = lax.axis_size("dp")
+        meet([swap.device] + [(lax.rem(lax.axis_index("dp") + s, count), lax.axis_index("tensor")) for s in range(1, count)])
+        middle.start()
         dck_sum[...] = jnp.zeros_like(dck_sum)
         dcv_sum[...] = jnp.zeros_like(dcv_sum)
         weight_sum[...] = jnp.zeros_like(weight_sum)
@@ -437,15 +553,94 @@
     back = tn(dqkv[...], w_ref[...].reshape(slots * 3 * lanes, dim))
     gain_sum[...] += jnp.sum(back * hat, axis=0, keepdims=True)
     total = resid_grad_ref[...].astype(F32) + norm_back(back, gain, hat, inv_std)
-    tokens_ref[...] = token_major(xs, total).astype(BF16)
+    swap.send(step_id, block, total.astype(BF16))
 
     @pl.when(block == 0)
     def _():
-        grads_ref[:, 0 : 3 * own] = weight_sum[...].T.astype(BF16)
-        grads_ref[:, 3 * own :] = jnp.broadcast_to(gain_sum[...], (GB, dim)).T.astype(BF16)
-        for h in range(own_heads):
-            conv_grads_ref[:, h * hd : (h + 1) * hd] = kconv_sum[h].astype(BF16)
-            conv_grads_ref[:, (own_heads + h) * hd : (own_heads + h + 1) * hd] = vconv_sum[h].astype(BF16)
+        put_rows(last_parts, [weight_sum[...].T, jnp.broadcast_to(gain_sum[...], (GB, dim)).T])
+        last.start()
+        put_rows(
+            conv_parts,
+            [
+                total[h]
+                for slot in range(2)
+                for total in (kconv_sum, vconv_sum)
+                for h in range(slot * slot_heads, (slot + 1) * slot_heads)
+            ],
+        )
+        convs.start()
+        middle_total = middle.total()
+        turn(0, middle_turn, middle_total)
+        last_total = last.total()
+        turn(1, last_turn, last_total)
+        conv_total = convs.total()
+        turn(2, conv_turn, conv_total)
+        for n, (out, ref, total) in enumerate(
+            ((middle_out, middle_turn, middle_total), (last_out, last_turn, last_total), (conv_out, conv_turn, conv_total))
+        ):
+            turned(n, ref).wait()
+            cols = out.shape[1]
+            split = total.shape[1] - cols
+            kept = [total[:, :split]] + ([total[:, 2 * split :]] if cols > split else [])
+            out[...] = ref[1].astype(F32) + jnp.concatenate(kept, axis=1)
+        swap.finish(block)
+
+
+def place_rows(lens_ref, longest_here, mine, theirs, natural, out_ref):
+    half = mine.shape[0]
+    first = longest_first(lens_ref, half // 3)
+    chunks = natural.shape[0]
+
+    def taps(block, r):
+        rows = pl.ds(pl.multiple_of(block * TB + r * GB, GB), GB)
+        return mine[rows, :].astype(F32), theirs[rows, :].astype(F32)
+
+    def outside(block, carry):
+        for r in range(3):
+            a, b = taps(block, r)
+            other = jnp.where(longest_here, b, a)
+            for c in range(chunks):
+                for base in (0, half):
+                    natural[c, pl.ds(base + block * TB + r, GB, stride=3), :] = other[:, c * 128 : (c + 1) * 128]
+        return carry
+
+    def inside(block, carry):
+        for r in range(3):
+            a, b = taps(block, r)
+            longest = jnp.where(longest_here, a, b)
+            for c in range(chunks):
+                natural[c, pl.ds(first + block * TB + r, GB, stride=3), :] = longest[:, c * 128 : (c + 1) * 128]
+        return carry
+
+    def written(block, carry):
+        rows = pl.ds(pl.multiple_of(block * TB, TB), TB)
+        out_ref[rows, :] = jnp.concatenate([natural[c, rows, :] for c in range(chunks)], axis=1).astype(BF16)
+        return carry
+
+    lax.fori_loop(0, half // TB, outside, 0)
+    lax.fori_loop(0, half // TB, inside, 0)
+    lax.fori_loop(0, 2 * half // TB, written, 0)
+
+
+def last_kernel(
+    hd, lens_ref, mixed_ref, mixed_peer, tokens_ref, tokens_peer, middle_ref, last_ref, conv_ref,
+    mixed_out, tokens_out, gain1_out, gain2_out, query_out, key_out, value_out, out_out, kconv_out, vconv_out,
+    up_out, down_out, natural,
+):
+    longest_here = lax.rem(lax.axis_index("tensor"), 2) == 0
+    place_rows(lens_ref, longest_here, mixed_ref, mixed_peer, natural, mixed_out)
+    place_rows(lens_ref, longest_here, tokens_ref, tokens_peer, natural, tokens_out)
+    units, own = up_out.shape[1], query_out.shape[1]
+    up_out[...] = middle_ref[:, 0:units]
+    down_out[...] = middle_ref[:, units : 2 * units].T
+    out_out[...] = middle_ref[:, 2 * units : 2 * units + own].T
+    gain2_out[...] = middle_ref[:, 2 * units + own :].T[0:1]
+    for n, out in enumerate((query_out, key_out, value_out)):
+        out[...] = last_ref[:, n * own : (n + 1) * own]
+    gain1_out[...] = last_ref[:, 3 * own :].T[0:1]
+    for n, out in enumerate((kconv_out, vconv_out)):
+        for h in range(out.shape[0]):
+            out[h] = conv_ref[:, n * own + h * hd : n * own + (h + 1) * hd]
 
 
 def whole(shape):
@@ -458,13 +653,6 @@
 
 def params():
     return pltpu.CompilerParams(vmem_limit_bytes=VMEM, dimension_semantics=("arbitrary",))
-
-
-def sent_and_summed(array):
-    count = lax.axis_size("dp")
-    parts = array.reshape(count, array.shape[0] // count, *array.shape[1:])
-    parts = lax.all_to_all(parts, "dp", 0, 0, tiled=True)
-    return jnp.sum(parts.astype(F32), axis=0)
 
 
 def halves(lengths, rows):
@@ -479,22 +667,6 @@
     inside = lax.dynamic_slice_in_dim(array, first, half, 0)
     others = jnp.where(place < first, array[:half], array[half:])
     return jnp.where(longest_here, inside, others)
-
-
-def all_rows(own, place, first, longest_here):
-    half = place.shape[0]
-    place = place[:, None]
-    theirs = lax.ppermute(own, "tensor", neighbours("tensor"))
-    inside = jnp.where(longest_here, own, theirs)
-    others = jnp.where(longest_here, theirs, own)
-    turned = lax.dynamic_slice_in_dim(jnp.concatenate([inside, inside]), half - first, half, 0)
-    return jnp.concatenate(
-        [jnp.where(place < first, others, turned), jnp.where(place < first, turned, others)]
-    )
-
-
-def neighbours(axis):
-    return [(i, i ^ 1) for i in range(lax.axis_size(axis))]
 
 
 def on_device(
@@ -568,105 +740,103 @@
         out_weight, up_weight, down_weight,
     )
 
-    mid_cols = 4 * units + 2 * own + GB
-    mixed, resid_grad, dctx, delta, middle_grads = pl.pallas_call(
+    count = lax.axis_size("dp")
+    slot_cols = 2 * units + own
+    mid_cols = 2 * slot_cols + GB
+    mixed, mixed_peer, resid_grad, dctx, delta, middle_grads = pl.pallas_call(
         functools.partial(middle_kernel, heads, hd),
         grid=(blocks,),
         in_specs=[
             rows_spec, rows_spec, whole((1, dim)), cols_spec, whole((width, dim)),
             whole((peers, dim, units)), whole((peers, units, dim)),
         ],
-        out_specs=[rows_spec, rows_spec, cols_spec, stat_spec, whole((dim, mid_cols))],
+        out_specs=[anywhere, anywhere, rows_spec, cols_spec, stat_spec, whole((count, dim // count, mid_cols))],
         out_shape=[
+            jax.ShapeDtypeStruct((rows, dim), BF16),
             jax.ShapeDtypeStruct((rows, dim), BF16),
             jax.ShapeDtypeStruct((rows, dim), BF16),
             jax.ShapeDtypeStruct((width, rows), BF16),
             jax.ShapeDtypeStruct((heads, rows), F32),
-            jax.ShapeDtypeStruct((dim, mid_cols), BF16),
+            jax.ShapeDtypeStruct((count, dim // count, mid_cols), BF16),
         ],
         scratch_shapes=[
-            pltpu.VMEM((dim // 128, TB, 128), F32), pltpu.VMEM((2, units, dim), F32),
+            pltpu.VMEM((2, TB, dim), BF16), pltpu.VMEM((2, units, dim), F32),
             pltpu.VMEM((2, dim, units), F32), pltpu.VMEM((2 * own, dim), F32), pltpu.VMEM((1, dim), F32),
+            pltpu.SemaphoreType.DMA((2, blocks)), pltpu.SemaphoreType.DMA((blocks,)),
         ],
-        compiler_params=params(),
+        compiler_params=pltpu.CompilerParams(
+            vmem_limit_bytes=VMEM, dimension_semantics=("arbitrary",), collective_id=1, has_side_effects=True
+        ),
         cost_estimate=cost(55),
         name="feed_forward",
     )(x, g, gain2, ctx, out_all.reshape(width, dim), up_all, down_all)
-    mixed_out = all_rows(mixed, *pack)
-    middle_share = sent_and_summed(middle_grads)
 
     back_rows = pl.BlockSpec((TB, dim), lambda b, *_: (blocks - 1 - b, 0))
     back_cols = pl.BlockSpec((width, TB), lambda b, *_: (0, blocks - 1 - b))
     back_stat = pl.BlockSpec((heads, TB), lambda b, *_: (0, blocks - 1 - b))
     back_mask = pl.BlockSpec((1, 1, TB), lambda b, *_: (blocks - 1 - b, 0, 0))
     two = 2 * own_heads
-    grad_rows, last_grads, conv_grads = pl.pallas_call(
+    last_cols = 6 * own + GB
+    out_dims = [(dim // count, slot_cols + GB), (dim // count, 3 * own + GB), (taps // count, 2 * own)]
+    grad_rows, grad_peer, middle_share, last_share, conv_share = pl.pallas_call(
         functools.partial(backward_kernel, heads, hd, two),
         grid_spec=pltpu.PrefetchScalarGridSpec(
             num_scalar_prefetch=1,
             grid=(blocks,),
             in_specs=[
-                back_rows, whole((1, dim)), whole((peers, 3 * own, dim)), whole((peers, 2 * taps, own)), back_mask, back_cols, back_cols, back_cols, back_stat,
+                back_rows, whole((1, dim)), whole((peers, 3 * own, dim)), whole((peers, 2 * taps, own)), back_mask,
+                back_cols, back_cols, back_cols, back_stat,
                 back_cols, back_stat, back_rows, whole((heads, groups, hd)), whole((width, groups)),
-                whole((heads, groups, hd)),
+                whole((heads, groups, hd)), anywhere,
             ],
-            out_specs=[back_rows, whole((dim, 6 * own + GB)), whole((taps, 4 * own))],
+            out_specs=[anywhere, anywhere] + [whole(d) for d in out_dims],
             scratch_shapes=[
-                pltpu.VMEM((dim // 128, TB, 128), F32), pltpu.VMEM((heads, groups, hd), F32),
+                pltpu.VMEM((2, TB, dim), BF16), pltpu.VMEM((heads, groups, hd), F32),
                 pltpu.VMEM((heads, groups, hd), F32), pltpu.VMEM((width, TB), F32),
                 pltpu.VMEM((3 * width, TB), BF16), pltpu.VMEM((6 * own, dim), F32),
                 pltpu.VMEM((two, taps, hd), F32), pltpu.VMEM((two, taps, hd), F32),
                 pltpu.VMEM((1, dim), F32),
+                pltpu.VMEM((count, dim // count, mid_cols), BF16),
+                pltpu.VMEM((count, dim // count, last_cols), BF16), pltpu.VMEM((count, dim // count, last_cols), BF16),
+                pltpu.VMEM((count, taps // count, 4 * own), BF16), pltpu.VMEM((count, taps // count, 4 * own), BF16),
+            ]
+            + [pltpu.VMEM((2, *d), BF16) for d in out_dims]
+            + [
+                pltpu.VMEM((dim // count, mid_cols), F32), pltpu.VMEM((dim // count, last_cols), F32),
+                pltpu.VMEM((taps // count, 4 * own), F32),
+            ]
+            + [
+                pltpu.SemaphoreType.DMA((2, blocks)), pltpu.SemaphoreType.DMA((blocks,)),
+                pltpu.SemaphoreType.DMA((2, count)), pltpu.SemaphoreType.DMA((2, count)),
+                pltpu.SemaphoreType.DMA((2, count)), pltpu.SemaphoreType.DMA((2, 3)), pltpu.SemaphoreType.DMA((3,)),
             ],
         ),
-        out_shape=[
-            jax.ShapeDtypeStruct((rows, dim), BF16),
-            jax.ShapeDtypeStruct((dim, 6 * own + GB), BF16),
-            jax.ShapeDtypeStruct((taps, 4 * own), BF16),
-        ],
-        compiler_params=params(),
+        out_shape=[jax.ShapeDtypeStruct((rows, dim), BF16)] * 2 + [jax.ShapeDtypeStruct(d, F32) for d in out_dims],
+        compiler_params=pltpu.CompilerParams(
+            vmem_limit_bytes=VMEM, dimension_semantics=("arbitrary",), collective_id=2, has_side_effects=True
+        ),
         cost_estimate=cost(60),
         name="attention_backward",
-    )(lens, x, gain1, w_all, conv_all, mask, q, k, v, lse, dctx, delta, resid_grad, ck, ckt, cv)
-    grad_tokens = all_rows(grad_rows, *pack)
-    last_share = sent_and_summed(last_grads)
-    conv_share = sent_and_summed(conv_grads).reshape(-1, 2, 2, own)
-
-    def parts(slot):
-        half = 2 * units
-        return (
-            middle_share[:, slot * half : slot * half + half],
-            middle_share[:, 2 * half + slot * own : 2 * half + slot * own + own],
-            middle_share[:, 2 * half + 2 * own],
-            *(last_share[:, (3 * slot + n) * own : (3 * slot + n + 1) * own] for n in range(3)),
-            last_share[:, 6 * own],
-            conv_share[:, :, slot],
-        )
-
-    shapes = [p.shape for p in parts(1)]
-    sizes = [math.prod(d) for d in shapes]
-    ends = [sum(sizes[: n + 1]) for n in range(len(sizes))]
-    theirs = lax.ppermute(
-        jnp.concatenate([p.reshape(-1) for p in parts(1)]).astype(BF16), "tensor", neighbours("tensor")
-    ).astype(F32)
-    ff, out, gain2_grad, query, key, value, gain1_grad, conv = (
-        p + t.reshape(d) for p, t, d in zip(parts(0), jnp.split(theirs, ends[:-1]), shapes)
-    )
-    conv = conv.reshape(-1, 2, own_heads, hd).transpose(1, 2, 0, 3)
-    return (
-        mixed_out,
-        grad_tokens,
-        gain1_grad,
-        gain2_grad,
-        query,
-        key,
-        value,
-        out.T,
-        conv[0],
-        conv[1],
-        ff[:, :units],
-        ff[:, units:].T,
-    )
+    )(lens, x, gain1, w_all, conv_all, mask, q, k, v, lse, dctx, delta, resid_grad, ck, ckt, cv, middle_grads)
+
+    share = dim // count
+    shapes = [
+        ((2 * rows, dim), BF16), ((2 * rows, dim), BF16), ((1, share), F32), ((1, share), F32),
+        ((share, own), F32), ((share, own), F32), ((share, own), F32), ((own, share), F32),
+        ((own_heads, taps // count, hd), F32), ((own_heads, taps // count, hd), F32),
+        ((share, units), F32), ((units, share), F32),
+    ]
+    outs = pl.pallas_call(
+        functools.partial(last_kernel, hd),
+        in_specs=[pl.BlockSpec(memory_space=pltpu.SMEM)] + [inside] * 7,
+        out_specs=[inside] * len(shapes),
+        out_shape=[jax.ShapeDtypeStruct(d, t) for d, t in shapes],
+        scratch_shapes=[pltpu.VMEM((dim // 128, 2 * rows, 128), F32)],
+        compiler_params=pltpu.CompilerParams(vmem_limit_bytes=VMEM),
+        cost_estimate=cost(15),
+        name="in_order",
+    )(lens, mixed, mixed_peer, grad_rows, grad_peer, middle_share, last_share, conv_share)
+    return (*outs[:2], outs[2].reshape(share), outs[3].reshape(share), *outs[4:])
 
 
 def solution(mesh):

time: 398 us -> 291 us (0.73)
  waiting for transfers between devices: 97 us -> 0 us
  Pallas kernels: 233 us -> 278 us
  blocking collectives: 27.7 us -> 0 us
  other arithmetic: 23.8 us -> 4.15 us
  starting transfers between devices: 5.79 us -> 0 us
    ppermute x3 -> x0, waiting for transfers between devices: 70.3 us -> none  [the longest x2 70.3 us: all_rows(): theirs = lax.ppermute(own, 'tensor', neighbours('tensor'))]
    all_to_all x2 -> x0, blocking collectives: 27.7 us -> none  [sent_and_summed(): parts = lax.all_to_all(parts, 'dp', 0, 0, tiled=True)]
    all_to_all x1 -> x0, waiting for transfers between devices: 26.6 us -> none  [sent_and_summed(): parts = lax.all_to_all(parts, 'dp', 0, 0, tiled=True)]
    pallas_call x1, Pallas kernels: 60.1 us -> 84.3 us  [on_device(): pl.pallas_call(functools.partial(backward_kernel, heads, hd, two), grid_s...]
    select_n x3 -> x0, other arithmetic: 12 us -> none  [the longest x1 9.85 us: all_rows(): jnp.where(place < first, others, turned)]
    pallas_call x0 -> x1, Pallas kernels: none -> 11 us  [on_device(): pl.pallas_call(functools.partial(last_kernel, hd), in_specs=[pl.BlockSpec...]
    pallas_call x1, Pallas kernels: 57.5 us -> 67.4 us  [on_device(): pl.pallas_call(functools.partial(middle_kernel, heads, hd), grid=(blocks,...]
    concatenate x1 -> x0, other arithmetic: 4 us -> none  [all_rows(): jnp.concatenate([jnp.where(place < first, others, turned), jnp.where(plac...]
  transfers between devices with their start and end apart: 4 -> 0, of which waited for: 3 -> 0; matrix products, arithmetic and copies ran while one was open for 5% -> 0% of each run, Pallas kernels for 0% -> 0%
where the time goes in v3:
time: 291 us
  Pallas kernels  278 us (96%)
  local copies, waits for them, and re-layouts  7.48 us (3%)
  other arithmetic  4.15 us (1%)
    pallas_call x1, Pallas kernels, on_device(): pl.pallas_call(functools.partial(forward_kernel, heads, hd), grid_spec=pl...  115 us
    pallas_call x1, Pallas kernels, on_device(): pl.pallas_call(functools.partial(backward_kernel, heads, hd, two), grid_s...  84.3 us
    pallas_call x1, Pallas kernels, on_device(): pl.pallas_call(functools.partial(middle_kernel, heads, hd), grid=(blocks,...  67.4 us
    pallas_call x1, Pallas kernels, on_device(): pl.pallas_call(functools.partial(last_kernel, hd), in_specs=[pl.BlockSpec...  11 us
    unnamed x4, local copies, waits for them, and re-layouts  6.42 us

profile of v3, /device:TPU:0, one launch (start us, length us, event | category | flops | bytes accessed | tf_op | source)
XLA Modules:
  0.0 291.1 jit_solution(14035467230695889703)
XLA Ops:
  0.6 1.3 iota_reduce_fusion
  2.0 1.9 fusion
  4.6 0.9 select_convert_fusion
  5.5 1.6 copy.31.kconv_ref
  7.0 1.6 copy.32.vconv_ref
  8.6 0.3 convert_element_type.10
  8.9 0.1 copy.30
  9.1 0.6 convert_element_type.12.mask_ref
  9.7 115.3 %attention_forward.1 = (bf16[2304,512]{1,0:T(8,128)(2,1)}, bf16[2304,512]{1,0:T(8,128)(2,1)}, bf16[512,2304]{1,0:T(8,128)(2,1)}, bf16[512,2304]{1,0:T(8,128)(2,1...) custom-call(s32[6]{0:T(128)} %bitcast.13, ...), custom_call_target="tpu_custom_call" | custom-call | flops 54999998464 | bytes 1048576 | tf_op jit(solution)/shard_map/attention_forward/pallas_call | solution.py:700
  125.0 67.4 %feed_forward.1 = (bf16[2304,512]{1,0:T(8,128)(2,1)}, bf16[2304,512]{1,0:T(8,128)(2,1)}, bf16[2304,512]{1,0:T(8,128)(2,1)}, bf16[512,2304]{1,0:T(8,128)(2,1)}, f...) custom-call(bf16[2304,512]{1,0:T(8,128)(2,1)} %get-tuple-element.52.x_ref, bf16[2304,512]{1,0:T(8,128)(2,1)} %get-tuple-element.53.g_ref, ...), custom_call_target="tpu_custom_call" | custom-call | flops 54999998464 | bytes 1048576 | tf_op jit(solution)/shard_map/feed_forward/pallas_call | solution.py:746
  192.5 84.3 %attention_backward.1 = (bf16[2304,512]{1,0:T(8,128)(2,1)}, bf16[2304,512]{1,0:T(8,128)(2,1)}, f32[64,1280]{1,0:T(8,128)}, f32[64,512]{1,0:T(8,128)}, f32[24,256]{1,0:T(8,128)}) custom-call(s32[6]{0:T(128)} %bitcast.14, bf16[2304,512]{1,0:T(8,128)(2,1)} %get-tuple-element.52.x_ref, f32[1,512]{1,0:T(1,128)} %bitcast.12, ...), custom_call_target="tpu_custom_call" | custom-call | flops 60000002048 | bytes 1048576 | tf_op jit(solution)/shard_map/attention_backward/pallas_call | solution.py:781
  276.8 11.0 %in_order.1 = (bf16[4608,512]{1,0:T(8,128)(2,1)}, bf16[4608,512]{1,0:T(8,128)(2,1)}, f32[1,64]{1,0:T(1,128)}, f32[1,64]{1,0:T(1,128)}, f32[64,128]{1,0:T(8,128)}...) custom-call(s32[6]{0:T(128)} %bitcast.15, ...), custom_call_target="tpu_custom_call" | custom-call | flops 15000000512 | bytes 1048576 | tf_op jit(solution)/shard_map/in_order/pallas_call | solution.py:829
  287.8 1.5 copy.33
  289.3 1.7 copy.34

commit v4 on v3

v4 whole, which is shorter than its diff:
```python
import functools
import math

import jax
import jax.numpy as jnp
from jax import lax
from jax.experimental import pallas as pl
from jax.experimental.pallas import tpu as pltpu
from jax.sharding import PartitionSpec as P

F32 = jnp.float32
BF16 = jnp.bfloat16
GB = 128
TB = 3 * GB
NEG = -1e30
LOG2E = 1.0 / math.log(2.0)
VMEM = 60 * 1024 * 1024

ERF_P = 0.43
ERF_C = (
    0.24255178053871013,
    0.24376598744271377,
    0.2089868288055898,
    0.23281685899157548,
    -0.05797941172752005,
    0.3523368029188165,
    -0.2915198548110903,
    0.06904073943922798,
)


def nn(a, b):
    return lax.dot_general(a, b, (((1,), (0,)), ((), ())), preferred_element_type=F32)


def nt(a, b):
    return lax.dot_general(a, b, (((1,), (1,)), ((), ())), preferred_element_type=F32)


def tn(a, b):
    return lax.dot_general(a, b, (((0,), (0,)), ((), ())), preferred_element_type=F32)


def norm_rows(values):
    centred = values - jnp.mean(values, -1, keepdims=True)
    inv_std = lax.rsqrt(jnp.mean(centred * centred, -1, keepdims=True) + 1e-05)
    return centred * inv_std, inv_std


def norm_back(grad_out, gains, normed, inv_std):
    scaled = grad_out * gains
    return inv_std * (
        scaled
        - jnp.mean(scaled, -1, keepdims=True)
        - normed * jnp.mean(scaled * normed, -1, keepdims=True)
    )


def gelu_and_slope(h):
    t = 1.0 / (1.0 + (ERF_P * math.sqrt(0.5)) * jnp.abs(h))
    poly = t * (0.5 * ERF_C[-1]) + 0.5 * ERF_C[-2]
    for c in ERF_C[-3::-1]:
        poly = poly * t + 0.5 * c
    e = jnp.exp2((h * h) * (-0.5 * LOG2E))
    tail = e * (poly * t)
    cdf = jnp.where(h >= 0, 1.0 - tail, tail)
    return h * cdf, cdf + h * (e * (1.0 / math.sqrt(2.0 * math.pi)))


def item_starts(lens_ref, block, longest_here, half):
    places = block * GB + lax.broadcasted_iota(jnp.int32, (1, GB), 1)
    starts = jnp.zeros((1, GB), jnp.int32)
    end = jnp.int32(0)
    for i in range(lens_ref.shape[0] - 1):
        end = end + jnp.where((lens_ref[i] == half) == longest_here, lens_ref[i], 0)
        starts = jnp.where(places >= end, end, starts)
    return places, starts


def longest_first(lens_ref, half):
    first, ahead = jnp.int32(0), jnp.int32(1)
    for i in range(lens_ref.shape[0]):
        ahead = jnp.where(lens_ref[i] == half, 0, ahead)
        first = first + ahead * lens_ref[i]
    return 3 * first


def own_taps(source, block, first, longest_here):
    half = source.shape[1] // 2
    base = block * TB
    parts = []
    for c in range(source.shape[0]):
        for r in range(3):
            inside = source[c, pl.ds(first + base + r, GB, stride=3), :]
            low = source[c, pl.ds(base + r, GB, stride=3), :]
            high = source[c, pl.ds(half + base + r, GB, stride=3), :]
            place = base + r + 3 * lax.broadcasted_iota(jnp.int32, (GB, 1), 0)
            parts.append(jnp.where(longest_here, inside, jnp.where(place < first, low, high)))
    return jnp.concatenate(
        [jnp.concatenate(parts[3 * c : 3 * c + 3], axis=0) for c in range(source.shape[0])], axis=1
    )


def put_bias(bias_ref, places, starts, count):
    for kb in range(count):
        keys = kb * GB + lax.broadcasted_iota(jnp.int32, (GB, GB), 0)
        bias_ref[kb * GB : (kb + 1) * GB, :] = jnp.where((keys >= starts) & (keys < places), 0.0, NEG)


def each_head(heads, hd, work):
    def some(i, carry):
        for n in range(4):
            h = 4 * i + n
            work(h, pl.ds(pl.multiple_of(h * hd, hd), hd), pl.ds(h, 1))
        return carry

    lax.fori_loop(0, heads // 4, some, 0)


def key_rows(kb):
    return pl.ds(pl.multiple_of(kb * GB, GB), GB)


def remote(src, dst, sems, at, device):
    return pltpu.make_async_remote_copy(
        src_ref=src, dst_ref=dst, send_sem=sems.at[(0, *at)], recv_sem=sems.at[(1, *at)],
        device_id=device, device_id_type=pl.DeviceIdType.MESH,
    )


def meet(devices):
    barrier = pltpu.get_barrier_semaphore()
    for device in devices:
        pl.semaphore_signal(barrier, inc=1, device_id=device, device_id_type=pl.DeviceIdType.MESH)
    pl.semaphore_wait(barrier, len(devices))


def put_rows(ref, pieces, at=0):
    count, rows, _ = ref.shape
    for piece in pieces:
        cols = piece.shape[1]
        for d in range(count):
            ref[d, :, at : at + cols] = piece[d * rows : (d + 1) * rows].astype(ref.dtype)
        at += cols


class Swap:
    def __init__(self, staged, mine, theirs, sems, local_sems):
        self.staged, self.mine, self.theirs, self.sems, self.local_sems = staged, mine, theirs, sems, local_sems
        self.device = (lax.axis_index("dp"), lax.axis_index("tensor") ^ 1)
        self.blocks = mine.shape[0] // TB

    def rows(self, block):
        return pl.ds(pl.multiple_of(block * TB, TB), TB)

    def local(self, step, block):
        staged = self.staged.at[lax.rem(step, 2)]
        return pltpu.make_async_copy(staged, self.mine.at[self.rows(block)], self.local_sems.at[step])

    def far(self, step, block):
        staged = self.staged.at[lax.rem(step, 2)]
        return remote(staged, self.theirs.at[self.rows(block)], self.sems, (step,), self.device)

    def settle(self, step, block):
        self.local(step, block).wait()
        self.far(step, block).wait_send()

    def send(self, step, block, values):
        @pl.when(step >= 2)
        def _():
            self.settle(step - 2, block)

        self.staged[lax.rem(step, 2)] = values
        self.local(step, block).start()
        self.far(step, block).start()

    def finish(self, block):
        for step in range(max(self.blocks - 2, 0), self.blocks):
            self.settle(step, block)
        for step in range(self.blocks):
            self.far(step, block).wait_recv()


class Spread:
    def __init__(self, source, landed, total, sems, local_sem):
        self.source, self.landed, self.sums, self.sems, self.local_sem = source, landed, total, sems, local_sem
        self.me, self.peer = lax.axis_index("dp"), lax.axis_index("tensor")
        self.count = lax.axis_size("dp")

    def copy(self, s):
        there = lax.rem(self.me + s, self.count)
        return remote(self.source.at[there], self.landed.at[s], self.sems, (s,), (there, self.peer))

    def own(self):
        return pltpu.make_async_copy(self.source.at[self.me], self.landed.at[0], self.local_sem)

    def start(self):
        self.own().start()

        def step(s, carry):
            self.copy(s).start()
            return carry

        lax.fori_loop(1, self.count, step, 0)

    def total(self):
        self.own().wait()

        def step(s, carry):
            self.copy(s).wait()
            return carry

        lax.fori_loop(1, self.count, step, 0)

        self.sums[...] = self.landed[0].astype(F32)

        def add(s, carry):
            self.sums[...] += self.landed[s].astype(F32)
            return carry

        lax.fori_loop(1, self.count, add, 0)
        return self.sums


class Gather:
    def __init__(self, own, far, sems):
        self.own, self.far, self.sems = own, far, sems
        self.dp, self.tensor = lax.axis_index("dp"), lax.axis_index("tensor")
        self.peers = lax.axis_size("tensor")

    def devices(self):
        return [(self.dp, self.tensor ^ s) for s in range(1, self.peers)] + [
            (self.dp ^ m, self.tensor) for m in (1, 2, 4, 6)
        ]

    def eighth(self, array):
        rows = array.shape[0] // 8
        place = lax.rem(self.dp, 2) * 4 + lax.rem(self.dp, 8) // 2
        return array.at[pl.ds(pl.multiple_of(place * rows, rows), rows)]

    def half(self, array):
        rows = array.shape[0] // 2
        return array.at[pl.ds(pl.multiple_of(lax.rem(self.dp, 2) * rows, rows), rows)]

    def across(self, n, s):
        device = (self.dp, self.tensor ^ s)
        return remote(
            self.eighth(self.own[n]), self.eighth(self.far[n].at[s - 1]), self.sems, (n, 0, s - 1), device
        )

    def around(self, n, s, m):
        part = self.eighth(self.far[n].at[s - 1])
        return remote(part, part, self.sems, (n, m // 2, s - 1), (self.dp ^ m, self.tensor))

    def beside(self, n, s):
        part = self.half(self.far[n].at[s - 1])
        return remote(part, part, self.sems, (n, 4, s - 1), (self.dp ^ 1, self.tensor))

    def each(self):
        return [(n, s) for s in range(self.peers - 1, 0, -1) for n in range(len(self.far))]

    def start(self):
        for n, s in self.each():
            self.across(n, s).start()

    def pass_around(self):
        for n, s in self.each():
            self.across(n, s).wait_recv()
            for m in (6, 4, 2):
                self.around(n, s, m).start()

    def pass_beside(self):
        for n, s in self.each():
            for m in (2, 4, 6):
                self.around(n, s, m).wait_recv()
            self.beside(n, s).start()

    def arrive(self):
        for n, s in self.each():
            self.beside(n, s).wait_recv()

    def finish(self):
        for n, s in self.each():
            self.across(n, s).wait_send()
            for m in (2, 4, 6):
                self.around(n, s, m).wait_send()
            self.beside(n, s).wait_send()


def forward_kernel(
    heads, hd, lens_ref, x_ref, g_ref, gain_ref, pad_ref, query_ref, key_ref, value_ref, kconv_ref, vconv_ref,
    out_ref, up_ref, down_ref,
    x_own, g_own, q_ref, k_ref, v_ref, ctx_ref, lse_ref, ck_ref, ckt_ref, cv_ref, w_all, conv_all,
    out_far, up_far, down_far,
    xs, gs, w_ref, conv_ref, cvt_ref, bias_ref, first_sems, last_sems, local_sems,
):
    block = pl.program_id(0)
    blocks = pl.num_programs(0)
    own_heads, _, taps = kconv_ref.shape
    own = own_heads * hd
    dim = x_ref.shape[1]
    conv_cols = conv_ref.shape[2] // 2
    scale = LOG2E / math.sqrt(hd)
    first_gather = Gather((w_ref.at[0], conv_ref.at[0]), (w_ref.at[1:], conv_ref.at[1:]), first_sems)
    last_gather = Gather((out_ref, up_ref, down_ref), (out_far, up_far, down_far), last_sems)
    keep_copies = [
        pltpu.make_async_copy(w_ref, w_all, local_sems.at[0]), pltpu.make_async_copy(conv_ref, conv_all, local_sems.at[1])
    ]

    @pl.when(block == 0)
    def _():
        for n, src in enumerate((query_ref, key_ref, value_ref)):
            w_ref[0, n * own : (n + 1) * own, :] = src[...].T
        conv_ref[0] = jnp.zeros_like(conv_ref[0])
        for n, src in enumerate((kconv_ref, vconv_ref)):
            for h in range(own_heads):
                conv_ref[0, h * hd : (h + 1) * hd, n * conv_cols : n * conv_cols + taps] = src[h]
        meet(first_gather.devices())
        first_gather.start()
        for src, dst in ((x_ref, xs), (g_ref, gs)):
            for c in range(dim // 128):
                dst[c] = src[:, c * 128 : (c + 1) * 128].astype(F32)
        first_gather.pass_around()
        pads = pad_ref[...].astype(F32).T
        for c in range(pads.shape[1]):
            xs[dim // 128, c * 128 : (c + 1) * 128, :] = jnp.broadcast_to(pads[:, c : c + 1], (128, 128))
        first_gather.pass_beside()
        last_gather.start()
        first_gather.arrive()
        first_gather.finish()
        for copy in keep_copies:
            copy.start()

    half = x_ref.shape[0] // 2
    longest_here = lax.rem(lax.axis_index("tensor"), 2) == 0
    first = longest_first(lens_ref, half // 3)
    x = own_taps(xs, block, first, longest_here)
    mask = x[:, dim:].T[0:1]
    x = x[:, :dim]
    x_own[...] = x.astype(BF16)
    g_own[...] = own_taps(gs, block, first, longest_here).astype(BF16)
    normed, _ = norm_rows(x)
    first_in = (normed * gain_ref[...]).astype(BF16)
    for slot in range(w_ref.shape[0]):
        at = slice(slot * own, (slot + 1) * own)
        part = nt(w_ref[slot], first_in)
        q_ref[at, :] = part[0:own].astype(BF16)
        k_ref[at, :] = (part[own : 2 * own] * mask).astype(BF16)
        v_ref[at, :] = (part[2 * own : 3 * own] * mask).astype(BF16)
    rows = key_rows(block)
    for h in range(heads):
        band = slice(h * hd, (h + 1) * hd)
        slot, i = divmod(h, own_heads)
        for n, src, plain, trans in ((0, k_ref, ck_ref, ckt_ref), (1, v_ref, cv_ref, cvt_ref)):
            grouped = jnp.concatenate([src[band, r * GB : (r + 1) * GB] for r in range(3)], axis=0)
            comp = nn(conv_ref[slot, i * hd : (i + 1) * hd, n * conv_cols : n * conv_cols + taps], grouped)
            trans[band, rows] = comp.astype(BF16)
            plain[h, rows, :] = comp.T.astype(BF16)
    places, starts = item_starts(lens_ref, block, longest_here, half // 3)
    lse_ref[heads:, :] = jnp.broadcast_to(mask, (lse_ref.shape[0] - heads, TB))

    def attend(count):
        keys = slice(0, count * GB)
        put_bias(bias_ref, places, starts, count)

        def head(h, band, one):
            q = q_ref[band, :]
            own_score = jnp.sum(q.astype(F32) * k_ref[band, :].astype(F32), axis=0, keepdims=True) * scale
            s = nn(ck_ref[h, keys, :], q) * scale + jnp.concatenate([bias_ref[keys, :]] * 3, axis=1)
            top = jnp.maximum(own_score, jnp.max(s, axis=0, keepdims=True))
            p = jnp.exp2(s - top)
            own_prob = jnp.exp2(own_score - top)
            total = own_prob + jnp.sum(p, axis=0, keepdims=True)
            mixed = own_prob * v_ref[band, :].astype(F32) + nn(cvt_ref[band, keys], p.astype(BF16))
            ctx_ref[band, :] = (mixed * (1.0 / total)).astype(BF16)
            lse_ref[one, :] = top + jnp.log(total) * LOG2E

        each_head(heads, hd, head)

    for n in range(half // TB):
        pl.when(block == n)(functools.partial(attend, n + 1))

    @pl.when(block == 1)
    def _():
        last_gather.pass_around()

    @pl.when(block == blocks - 2)
    def _():
        last_gather.pass_beside()

    @pl.when(block == blocks - 1)
    def _():
        last_gather.arrive()
        last_gather.finish()
        for copy in keep_copies:
            copy.wait()


def middle_kernel(
    heads, hd, x_ref, g_ref, gain_ref, ctx_ref, out_ref, up_ref, down_ref, out_far, up_far, down_far,
    mixed_ref, mixed_peer, resid_grad_ref, dctx_ref, delta_ref, grads_ref,
    staged, acts, hidden_grads, pre, act_grads, kept_acts, kept_grads, kept_in, kept_g, out_sum, gain_sum,
    sems, local_sems,
):
    block = pl.program_id(0)
    own, two = out_ref.shape[0], out_sum.shape[0]
    units = up_ref.shape[1]
    step = pre.shape[2]
    slots = up_far.shape[0] + 1
    swap = Swap(staged, mixed_ref, mixed_peer, sems, local_sems)

    @pl.when(block == 0)
    def _():
        meet([swap.device])
        out_sum[...] = jnp.zeros_like(out_sum)
        gain_sum[...] = jnp.zeros_like(gain_sum)

    gain = gain_ref[...]
    g_low = g_ref[...]
    resid = x_ref[...].astype(F32) + tn(ctx_ref[0:own, :], out_ref[...]) + tn(ctx_ref[own:, :], out_far[...])
    hat, inv_std = norm_rows(resid)
    second_in = (hat * gain).astype(BF16)
    kept_in[block] = second_in
    kept_g[block] = g_low

    def up(slot, cols=slice(None)):
        return up_ref[:, cols] if slot == 0 else up_far[slot - 1, :, cols]

    def down(slot, rows=slice(None)):
        return down_ref[rows, :] if slot == 0 else down_far[slot - 1, rows, :]

    def products(c):
        slot, at = divmod(c * step, units)
        part = slice(at, at + step)
        pre[c % 2] = nn(second_in, up(slot, part))
        act_grads[c % 2] = nt(g_low, down(slot, part))

    count = slots * units // step
    products(0)
    for c in range(count):
        if c + 1 < count:
            products(c + 1)
        act, slope = gelu_and_slope(pre[c % 2])
        act = act.astype(BF16)
        hidden_grad = (act_grads[c % 2] * slope).astype(BF16)
        part = slice(c * step, (c + 1) * step)
        acts[:, part] = act
        hidden_grads[:, part] = hidden_grad
        if c * step < 2 * units:
            kept_acts[block, :, part] = act
            kept_grads[block, :, part] = hidden_grad
    parts = [slice(slot * units, (slot + 1) * units) for slot in range(slots)]
    ffn = sum(nn(acts[:, part], down(slot)) for slot, part in enumerate(parts))
    swap.send(block, block, (resid + ffn).astype(BF16))
    back = sum(nt(hidden_grads[:, part], up(slot)) for slot, part in enumerate(parts))
    gain_sum[...] += jnp.sum(back * hat, axis=0, keepdims=True)
    resid_grad = g_low.astype(F32) + norm_back(back, gain, hat, inv_std)
    attn_grad = resid_grad.astype(BF16)
    resid_grad_ref[...] = attn_grad
    out_sum[...] += nn(ctx_ref[0:two, :], attn_grad)
    dctx = jnp.concatenate([nt(out_ref[...], attn_grad), nt(out_far[...], attn_grad)], axis=0).astype(BF16)
    dctx_ref[...] = dctx
    dots = dctx.astype(F32) * ctx_ref[...].astype(F32)
    for h in range(heads):
        delta_ref[h : h + 1, :] = jnp.sum(dots[h * hd : (h + 1) * hd], axis=0, keepdims=True)

    @pl.when(block == pl.num_programs(0) - 1)
    def _():
        rows = kept_in.shape[0] * kept_in.shape[1]
        dim = kept_in.shape[2]
        inputs, upstream = kept_in[...].reshape(rows, dim), kept_g[...].reshape(rows, dim)
        at = 0
        for slot in range(2):
            for left, kept in ((inputs, kept_grads), (upstream, kept_acts)):
                for c in range(slot * units, (slot + 1) * units, step):
                    put_rows(grads_ref, [tn(left, kept[:, :, c : c + step].reshape(rows, step))], at)
                    at += step
            put_rows(grads_ref, [out_sum[slot * own : (slot + 1) * own].T], at)
            at += own
        put_rows(grads_ref, [jnp.broadcast_to(gain_sum[...], (GB, dim)).T], at)
        swap.finish(block)


def backward_kernel(
    heads, hd, own_heads, lens_ref, x_ref, gain_ref, w_ref, conv_ref,
    q_ref, k_ref, v_ref, lse_ref, dctx_ref, delta_ref, resid_grad_ref, ck_ref, ckt_ref, cv_ref, middle_ref,
    tokens_ref, tokens_peer, middle_out, last_out, conv_out,
    staged, bias_ref, convs_ref, dck_sum, dcv_sum, dq_sum, dqkv, weight_sum, kconv_sum, vconv_sum, gain_sum,
    middle_in, last_parts, last_in, conv_parts, conv_in,
    middle_turn, last_turn, conv_turn, middle_sum, last_sum, conv_sum,
    swap_sems, swap_local, middle_sems, last_sems, conv_sems, turn_sems, local_sems,
):
    step_id = pl.program_id(0)
    block = pl.num_programs(0) - 1 - step_id
    own = own_heads * hd
    slots, _, dim = w_ref.shape
    taps = convs_ref.shape[2]
    conv_cols = conv_ref.shape[2] // 2
    slot_heads = heads // slots
    lanes = slot_heads * hd
    factor = 1.0 / math.sqrt(hd)
    scale = LOG2E * factor
    swap = Swap(staged, tokens_ref, tokens_peer, swap_sems, swap_local)
    middle = Spread(middle_ref, middle_in, middle_sum, middle_sems, local_sems.at[0])
    last = Spread(last_parts, last_in, last_sum, last_sems, local_sems.at[1])
    convs = Spread(conv_parts, conv_in, conv_sum, conv_sems, local_sems.at[2])

    def turned(n, ref):
        return remote(ref.at[0], ref.at[1], turn_sems, (n,), swap.device)

    def turn(n, ref, total):
        ref[0] = total[:, total.shape[1] - ref.shape[2] :].astype(BF16)
        turned(n, ref).start()

    @pl.when(step_id == 0)
    def _():
        count = lax.axis_size("dp")
        meet([swap.device] + [(lax.rem(lax.axis_index("dp") + s, count), lax.axis_index("tensor")) for s in range(1, count)])
        middle.start()
        for h in range(heads):
            slot, i = divmod(h, slot_heads)
            for n in range(2):
                conv = conv_ref[slot, i * hd : (i + 1) * hd, n * conv_cols : n * conv_cols + taps]
                convs_ref[n, h] = conv.astype(F32).T.astype(BF16)
        dck_sum[...] = jnp.zeros_like(dck_sum)
        dcv_sum[...] = jnp.zeros_like(dcv_sum)
        weight_sum[...] = jnp.zeros_like(weight_sum)
        kconv_sum[...] = jnp.zeros_like(kconv_sum)
        vconv_sum[...] = jnp.zeros_like(vconv_sum)
        gain_sum[...] = jnp.zeros_like(gain_sum)

    longest_here = lax.rem(lax.axis_index("tensor"), 2) == 0
    places, starts = item_starts(lens_ref, block, longest_here, ck_ref.shape[1])

    def attend(count):
        keys = slice(0, count * GB)
        put_bias(bias_ref, places, starts, count)

        def head(h, band, one):
            q, dctx = q_ref[band, :], dctx_ref[band, :]
            s = nn(ck_ref[h, keys, :], q) * scale + jnp.concatenate([bias_ref[keys, :]] * 3, axis=1)
            p = jnp.exp2(s - lse_ref[one, :])
            dp = nn(cv_ref[h, keys, :], dctx)
            ds = (p * (dp - delta_ref[one, :])).astype(BF16)
            dcv_sum[h, keys, :] += nt(p.astype(BF16), dctx)
            dck_sum[h, keys, :] += nt(ds, q)
            dq_sum[band, :] = nn(ckt_ref[band, keys], ds)

        each_head(heads, hd, head)

    for n in range(ck_ref.shape[1] // GB):
        pl.when(block == n)(functools.partial(attend, n + 1))
    mask = lse_ref[heads : heads + 1, :]
    rows = key_rows(block)
    for h in range(heads):
        band = slice(h * hd, (h + 1) * hd)
        one = slice(h, h + 1)
        q, k = q_ref[band, :].astype(F32), k_ref[band, :].astype(F32)
        v, dctx = v_ref[band, :].astype(F32), dctx_ref[band, :].astype(F32)
        own_prob = jnp.exp2(jnp.sum(q * k, axis=0, keepdims=True) * scale - lse_ref[one, :])
        own_dprob = jnp.sum(dctx * v, axis=0, keepdims=True)
        own_dscore = own_prob * (own_dprob - delta_ref[one, :]) * factor
        slot, i = divmod(h, slot_heads)
        base = slot * 3 * lanes + i * hd
        dqkv[base : base + hd, :] = (dq_sum[band, :] * factor + own_dscore * k).astype(BF16)
        dck = (dck_sum[h, rows, :] * factor).astype(BF16)
        dcv = dcv_sum[h, rows, :].astype(BF16)
        for n, src, total, grad, beside in (
            (0, k_ref, kconv_sum, dck, own_dscore * q),
            (1, v_ref, vconv_sum, dcv, own_prob * dctx),
        ):
            spread = nt(convs_ref[n, h], grad)
            spread = jnp.concatenate([spread[r * hd : (r + 1) * hd] for r in range(3)], axis=1)
            at = base + (n + 1) * lanes
            dqkv[at : at + hd, :] = ((spread + beside) * mask).astype(BF16)
            if h < own_heads:
                grouped = jnp.concatenate([src[band, r * GB : (r + 1) * GB] for r in range(3)], axis=0)
                total[h] += nn(grouped, grad)
    hat, inv_std = norm_rows(x_ref[...].astype(F32))
    gain = gain_ref[...]
    first_in = (hat * gain).astype(BF16)
    weight_sum[...] += nn(dqkv[0 : 3 * own, :], first_in)
    back = tn(dqkv[...], w_ref[...].reshape(slots * 3 * lanes, dim))
    gain_sum[...] += jnp.sum(back * hat, axis=0, keepdims=True)
    total = resid_grad_ref[...].astype(F32) + norm_back(back, gain, hat, inv_std)
    swap.send(step_id, block, total.astype(BF16))

    @pl.when(block == 0)
    def _():
        put_rows(last_parts, [weight_sum[...].T, jnp.broadcast_to(gain_sum[...], (GB, dim)).T])
        last.start()
        put_rows(
            conv_parts,
            [
                total[h]
                for slot in range(2)
                for total in (kconv_sum, vconv_sum)
                for h in range(slot * slot_heads, (slot + 1) * slot_heads)
            ],
        )
        convs.start()
        middle_total = middle.total()
        turn(0, middle_turn, middle_total)
        last_total = last.total()
        turn(1, last_turn, last_total)
        conv_total = convs.total()
        turn(2, conv_turn, conv_total)
        for n, (out, ref, total) in enumerate(
            ((middle_out, middle_turn, middle_total), (last_out, last_turn, last_total), (conv_out, conv_turn, conv_total))
        ):
            turned(n, ref).wait()
            cols = out.shape[1]
            split = total.shape[1] - cols
            kept = [total[:, :split]] + ([total[:, 2 * split :]] if cols > split else [])
            out[...] = ref[1].astype(F32) + jnp.concatenate(kept, axis=1)
        swap.finish(block)


def place_rows(lens_ref, longest_here, mine, theirs, natural, out_ref):
    half = mine.shape[0]
    first = longest_first(lens_ref, half // 3)

    def taps(block, r, other):
        rows = pl.ds(pl.multiple_of(block * TB + r * GB, GB), GB)
        a, b = mine[rows, :].astype(F32), theirs[rows, :].astype(F32)
        return jnp.where(longest_here == other, b, a)

    for block in range(half // TB):
        for r in range(3):
            others = taps(block, r, True)
            for base in (0, half):
                natural[pl.ds(base + block * TB + r, GB, stride=3), :] = others
    for block in range(half // TB):
        for r in range(3):
            natural[pl.ds(first + block * TB + r, GB, stride=3), :] = taps(block, r, False)
    out_ref[...] = natural[...].astype(BF16)


def last_kernel(
    hd, lens_ref, mixed_ref, mixed_peer, tokens_ref, tokens_peer, middle_ref, last_ref, conv_ref,
    mixed_out, tokens_out, gain1_out, gain2_out, query_out, key_out, value_out, out_out, kconv_out, vconv_out,
    up_out, down_out, natural_mixed, natural_tokens,
):
    longest_here = lax.rem(lax.axis_index("tensor"), 2) == 0
    place_rows(lens_ref, longest_here, mixed_ref, mixed_peer, natural_mixed, mixed_out)
    place_rows(lens_ref, longest_here, tokens_ref, tokens_peer, natural_tokens, tokens_out)

    @pl.when(pl.program_id(0) == 0)
    def _():
        units, own = up_out.shape[1], query_out.shape[1]
        up_out[...] = middle_ref[:, 0:units]
        down_out[...] = middle_ref[:, units : 2 * units].T
        out_out[...] = middle_ref[:, 2 * units : 2 * units + own].T
        gain2_out[...] = middle_ref[:, 2 * units + own :].T[0:1]
        for n, out in enumerate((query_out, key_out, value_out)):
            out[...] = last_ref[:, n * own : (n + 1) * own]
        gain1_out[...] = last_ref[:, 3 * own :].T[0:1]
        for n, out in enumerate((kconv_out, vconv_out)):
            for h in range(out.shape[0]):
                out[h] = conv_ref[:, n * own + h * hd : n * own + (h + 1) * hd].T


def whole(shape):
    return pl.BlockSpec(shape, lambda *_: (0,) * len(shape))


def cost(micros):
    return pl.CostEstimate(flops=int(micros * 1e9), bytes_accessed=1 << 20, transcendentals=0)


def params():
    return pltpu.CompilerParams(vmem_limit_bytes=VMEM, dimension_semantics=("arbitrary",))


def on_device(
    tokens, first_gain, second_gain, query_weight, key_weight, value_weight, out_weight,
    key_conv, value_conv, up_weight, down_weight, pad_mask, item_lengths, cotangent,
):
    dim = tokens.shape[1]
    own_heads, taps, hd = key_conv.shape
    peers = lax.axis_size("tensor")
    heads = own_heads * peers
    width = heads * hd
    own = own_heads * hd
    units = up_weight.shape[1]
    lens = item_lengths[0]
    rows = tokens.shape[0] // 2
    blocks = rows // TB
    groups = rows // 3
    pads = pad_mask.reshape(-1, 128)
    key_conv, value_conv = key_conv.transpose(0, 2, 1), value_conv.transpose(0, 2, 1)
    conv_cols = -(-taps // 128) * 128
    stats = heads + 8
    gain1, gain2 = first_gain[None], second_gain[None]

    rows_spec = pl.BlockSpec((TB, dim), lambda b, *_: (b, 0))
    cols_spec = pl.BlockSpec((width, TB), lambda b, *_: (0, b))
    stat_spec = pl.BlockSpec((heads, TB), lambda b, *_: (0, b))
    lse_spec = pl.BlockSpec((stats, TB), lambda b, *_: (0, b))
    anywhere = pl.BlockSpec(memory_space=pl.ANY)
    inside = pl.BlockSpec(memory_space=pltpu.VMEM)
    x, g, q, k, v, ctx, lse, ck, ckt, cv, w_all, conv_all, out_far, up_far, down_far = pl.pallas_call(
        functools.partial(forward_kernel, heads, hd),
        grid_spec=pltpu.PrefetchScalarGridSpec(
            num_scalar_prefetch=1,
            grid=(blocks,),
            in_specs=[inside, inside, whole((1, dim))] + [inside] * 6 + [anywhere] * 3,
            out_specs=[
                rows_spec, rows_spec, cols_spec, cols_spec, cols_spec, cols_spec, lse_spec,
                whole((heads, groups, hd)), whole((width, groups)), whole((heads, groups, hd)),
                anywhere, anywhere, anywhere, anywhere, anywhere,
            ],
            scratch_shapes=[
                pltpu.VMEM((dim // 128 + 1, 2 * rows, 128), F32), pltpu.VMEM((dim // 128, 2 * rows, 128), F32),
                pltpu.VMEM((peers, 3 * own, dim), BF16), pltpu.VMEM((peers, own, 2 * conv_cols), BF16),
                pltpu.VMEM((width, groups), BF16), pltpu.VMEM((groups, GB), F32),
                pltpu.SemaphoreType.DMA((2, 2, 5, peers - 1)), pltpu.SemaphoreType.DMA((2, 3, 5, peers - 1)),
                pltpu.SemaphoreType.DMA((2,)),
            ],
        ),
        out_shape=[jax.ShapeDtypeStruct((rows, dim), BF16)] * 2
        + [jax.ShapeDtypeStruct((width, rows), BF16)] * 4
        + [
            jax.ShapeDtypeStruct((stats, rows), F32),
            jax.ShapeDtypeStruct((heads, groups, hd), BF16),
            jax.ShapeDtypeStruct((width, groups), BF16),
            jax.ShapeDtypeStruct((heads, groups, hd), BF16),
            jax.ShapeDtypeStruct((peers, 3 * own, dim), BF16),
            jax.ShapeDtypeStruct((peers, own, 2 * conv_cols), BF16),
            jax.ShapeDtypeStruct((peers - 1, own, dim), BF16),
            jax.ShapeDtypeStruct((peers - 1, dim, units), BF16),
            jax.ShapeDtypeStruct((peers - 1, units, dim), BF16),
        ],
        compiler_params=pltpu.CompilerParams(
            vmem_limit_bytes=VMEM, dimension_semantics=("arbitrary",), collective_id=0, has_side_effects=True
        ),
        cost_estimate=cost(55),
        name="attention_forward",
    )(
        lens, tokens, cotangent, gain1, pads, query_weight, key_weight, value_weight, key_conv, value_conv,
        out_weight, up_weight, down_weight,
    )

    count = lax.axis_size("dp")
    slot_cols = 2 * units + own
    mid_cols = 2 * slot_cols + GB
    step = 256
    mixed, mixed_peer, resid_grad, dctx, delta, middle_grads = pl.pallas_call(
        functools.partial(middle_kernel, heads, hd),
        grid=(blocks,),
        in_specs=[
            rows_spec, rows_spec, whole((1, dim)), cols_spec, whole((own, dim)),
            whole((dim, units)), whole((units, dim)), whole((width - own, dim)),
            whole((peers - 1, dim, units)), whole((peers - 1, units, dim)),
        ],
        out_specs=[anywhere, anywhere, rows_spec, cols_spec, stat_spec, whole((count, dim // count, mid_cols))],
        out_shape=[
            jax.ShapeDtypeStruct((rows, dim), BF16),
            jax.ShapeDtypeStruct((rows, dim), BF16),
            jax.ShapeDtypeStruct((rows, dim), BF16),
            jax.ShapeDtypeStruct((width, rows), BF16),
            jax.ShapeDtypeStruct((heads, rows), F32),
            jax.ShapeDtypeStruct((count, dim // count, mid_cols), BF16),
        ],
        scratch_shapes=[
            pltpu.VMEM((2, TB, dim), BF16), pltpu.VMEM((TB, peers * units), BF16), pltpu.VMEM((TB, peers * units), BF16),
            pltpu.VMEM((2, TB, step), F32), pltpu.VMEM((2, TB, step), F32),
            pltpu.VMEM((blocks, TB, 2 * units), BF16), pltpu.VMEM((blocks, TB, 2 * units), BF16),
            pltpu.VMEM((blocks, TB, dim), BF16), pltpu.VMEM((blocks, TB, dim), BF16),
            pltpu.VMEM((2 * own, dim), F32), pltpu.VMEM((1, dim), F32),
            pltpu.SemaphoreType.DMA((2, blocks)), pltpu.SemaphoreType.DMA((blocks,)),
        ],
        compiler_params=pltpu.CompilerParams(
            vmem_limit_bytes=VMEM, dimension_semantics=("arbitrary",), collective_id=1, has_side_effects=True
        ),
        cost_estimate=cost(55),
        name="feed_forward",
    )(x, g, gain2, ctx, out_weight, up_weight, down_weight, out_far.reshape(width - own, dim), up_far, down_far)

    back_rows = pl.BlockSpec((TB, dim), lambda b, *_: (blocks - 1 - b, 0))
    back_cols = pl.BlockSpec((width, TB), lambda b, *_: (0, blocks - 1 - b))
    back_stat = pl.BlockSpec((heads, TB), lambda b, *_: (0, blocks - 1 - b))
    back_lse = pl.BlockSpec((stats, TB), lambda b, *_: (0, blocks - 1 - b))
    two = 2 * own_heads
    last_cols = 6 * own + GB
    out_dims = [(dim // count, slot_cols + GB), (dim // count, 3 * own + GB), (taps // count, 2 * own)]
    grad_rows, grad_peer, middle_share, last_share, conv_share = pl.pallas_call(
        functools.partial(backward_kernel, heads, hd, two),
        grid_spec=pltpu.PrefetchScalarGridSpec(
            num_scalar_prefetch=1,
            grid=(blocks,),
            in_specs=[
                back_rows, whole((1, dim)), whole((peers, 3 * own, dim)), whole((peers, own, 2 * conv_cols)),
                back_cols, back_cols, back_cols, back_lse,
                back_cols, back_stat, back_rows, whole((heads, groups, hd)), whole((width, groups)),
                whole((heads, groups, hd)), anywhere,
            ],
            out_specs=[anywhere, anywhere] + [whole(d) for d in out_dims],
            scratch_shapes=[
                pltpu.VMEM((2, TB, dim), BF16), pltpu.VMEM((groups, GB), F32),
                pltpu.VMEM((2, heads, taps, hd), BF16), pltpu.VMEM((heads, groups, hd), F32),
                pltpu.VMEM((heads, groups, hd), F32), pltpu.VMEM((width, TB), F32),
                pltpu.VMEM((3 * width, TB), BF16), pltpu.VMEM((6 * own, dim), F32),
                pltpu.VMEM((two, taps, hd), F32), pltpu.VMEM((two, taps, hd), F32),
                pltpu.VMEM((1, dim), F32),
                pltpu.VMEM((count, dim // count, mid_cols), BF16),
                pltpu.VMEM((count, dim // count, last_cols), BF16), pltpu.VMEM((count, dim // count, last_cols), BF16),
                pltpu.VMEM((count, taps // count, 4 * own), BF16), pltpu.VMEM((count, taps // count, 4 * own), BF16),
            ]
            + [pltpu.VMEM((2, *d), BF16) for d in out_dims]
            + [
                pltpu.VMEM((dim // count, mid_cols), F32), pltpu.VMEM((dim // count, last_cols), F32),
                pltpu.VMEM((taps // count, 4 * own), F32),
            ]
            + [
                pltpu.SemaphoreType.DMA((2, blocks)), pltpu.SemaphoreType.DMA((blocks,)),
                pltpu.SemaphoreType.DMA((2, count)), pltpu.SemaphoreType.DMA((2, count)),
                pltpu.SemaphoreType.DMA((2, count)), pltpu.SemaphoreType.DMA((2, 3)), pltpu.SemaphoreType.DMA((3,)),
            ],
        ),
        out_shape=[jax.ShapeDtypeStruct((rows, dim), BF16)] * 2 + [jax.ShapeDtypeStruct(d, F32) for d in out_dims],
        compiler_params=pltpu.CompilerParams(
            vmem_limit_bytes=VMEM, dimension_semantics=("arbitrary",), collective_id=2, has_side_effects=True
        ),
        cost_estimate=cost(60),
        name="attention_backward",
    )(lens, x, gain1, w_all, conv_all, q, k, v, lse, dctx, delta, resid_grad, ck, ckt, cv, middle_grads)

    share = dim // count
    own_conv = (own_heads, hd, taps // count)
    shapes = [
        ((1, share), F32), ((1, share), F32), ((share, own), F32), ((share, own), F32), ((share, own), F32),
        ((own, share), F32), (own_conv, F32), (own_conv, F32), ((share, units), F32), ((units, share), F32),
    ]
    lane_half = pl.BlockSpec((rows, 128), lambda c: (0, c))
    lane_all = pl.BlockSpec((2 * rows, 128), lambda c: (0, c))
    outs = pl.pallas_call(
        functools.partial(last_kernel, hd),
        grid=(dim // 128,),
        in_specs=[pl.BlockSpec(memory_space=pltpu.SMEM)] + [lane_half] * 4 + [whole(d) for d in out_dims],
        out_specs=[lane_all] * 2 + [whole(d) for d, _ in shapes],
        out_shape=[jax.ShapeDtypeStruct((2 * rows, dim), BF16)] * 2 + [jax.ShapeDtypeStruct(d, t) for d, t in shapes],
        scratch_shapes=[pltpu.VMEM((2 * rows, 128), F32)] * 2,
        compiler_params=params(),
        cost_estimate=cost(15),
        name="in_order",
    )(lens, mixed, mixed_peer, grad_rows, grad_peer, middle_share, last_share, conv_share)
    mixed, grad_tokens, gain1, gain2, query, key, value, out, kconv, vconv, up, down = outs
    return (
        mixed, grad_tokens, gain1.reshape(share), gain2.reshape(share), query, key, value, out,
        kconv.transpose(0, 2, 1), vconv.transpose(0, 2, 1), up, down,
    )


def solution(mesh):
    in_specs = (
        P("dp", None),
        P(),
        P(),
        P(None, "tensor"),
        P(None, "tensor"),
        P(None, "tensor"),
        P("tensor", None),
        P("tensor", None, None),
        P("tensor", None, None),
        P(None, "tensor"),
        P("tensor", None),
        P("dp"),
        P("dp", None),
        P("dp", None),
    )
    out_specs = (
        P("dp", None),
        P("dp", None),
        P("dp"),
        P("dp"),
        P("dp", "tensor"),
        P("dp", "tensor"),
        P("dp", "tensor"),
        P("tensor", "dp"),
        P("tensor", "dp", None),
        P("tensor", "dp", None),
        P("dp", "tensor"),
        P("tensor", "dp"),
    )
    return jax.shard_map(
        on_device, mesh=mesh, in_specs=in_specs, out_specs=out_specs, check_vma=False
    )
```

time: 291 us -> 235 us (0.81); the launches traced: 291 us -> 231 us
  Pallas kernels: 278 us -> 224 us
  other arithmetic: 4.15 us -> 0 us
    pallas_call x1, Pallas kernels: 115 us -> 65.4 us  [on_device(): pl.pallas_call(functools.partial(forward_kernel, heads, hd), grid_spec=pl...]
    pallas_call x1, Pallas kernels: 67.4 us -> 62.9 us  [on_device(): pl.pallas_call(functools.partial(middle_kernel, heads, hd), grid=(blocks,...]
where the time goes in v4:
time: 235 us; the launch traced here: 231 us
  Pallas kernels  224 us (95%)
  local copies, waits for them, and re-layouts  6.3 us (3%)
    pallas_call x1, Pallas kernels, on_device(): pl.pallas_call(functools.partial(backward_kernel, heads, hd, two), grid_s...  86.3 us
    pallas_call x1, Pallas kernels, on_device(): pl.pallas_call(functools.partial(forward_kernel, heads, hd), grid_spec=pl...  65.4 us
    pallas_call x1, Pallas kernels, on_device(): pl.pallas_call(functools.partial(middle_kernel, heads, hd), grid=(blocks,...  62.9 us
    pallas_call x1, Pallas kernels, on_device(): pl.pallas_call(functools.partial(last_kernel, hd), grid=(dim // 128,), in...  9.69 us
    unnamed x4, local copies, waits for them, and re-layouts  6.3 us

profile of v4, /device:TPU:0, one launch (start us, length us, event | category | flops | bytes accessed | tf_op | source)
XLA Modules:
  0.0 231.5 jit_solution(3731707875639058523)
XLA Ops:
  0.6 65.4 %attention_forward.1 = (bf16[2304,512]{1,0:T(8,128)(2,1)}, bf16[2304,512]{1,0:T(8,128)(2,1)}, bf16[512,2304]{1,0:T(8,128)(2,1)}, bf16[512,2304]{1,0:T(8,128)(2,1...) custom-call(s32[6]{0:T(128)} %bitcast.19, ...), custom_call_target="tpu_custom_call" | custom-call | flops 54999998464 | bytes 1048576 | tf_op jit(solution)/shard_map/attention_forward/pallas_call | solution.py:702
  66.0 62.9 %feed_forward.1 = (bf16[2304,512]{1,0:T(8,128)(2,1)}, bf16[2304,512]{1,0:T(8,128)(2,1)}, bf16[2304,512]{1,0:T(8,128)(2,1)}, bf16[512,2304]{1,0:T(8,128)(2,1)}, f...) custom-call(bf16[2304,512]{1,0:T(8,128)(2,1)} %get-tuple-element.50.x_ref, bf16[2304,512]{1,0:T(8,128)(2,1)} %get-tuple-element.51.g_ref, ...), custom_call_target="tpu_custom_call" | custom-call | flops 54999998464 | bytes 1048576 | tf_op jit(solution)/shard_map/feed_forward/pallas_call | solution.py:748
  129.0 86.3 %attention_backward.1 = (bf16[2304,512]{1,0:T(8,128)(2,1)}, bf16[2304,512]{1,0:T(8,128)(2,1)}, f32[64,1280]{1,0:T(8,128)}, f32[64,512]{1,0:T(8,128)}, f32[24,256]{1,0:T(8,128)}) custom-call(s32[6]{0:T(128)} %bitcast.20, bf16[2304,512]{1,0:T(8,128)(2,1)} %get-tuple-element.50.x_ref, f32[1,512]{1,0:T(1,128)} %bitcast.18, ...), custom_call_target="tpu_custom_call" | custom-call | flops 60000002048 | bytes 1048576 | tf_op jit(solution)/shard_map/attention_backward/pallas_call | solution.py:787
  215.3 9.7 %in_order.1 = (bf16[4608,512]{1,0:T(8,128)(2,1)}, bf16[4608,512]{1,0:T(8,128)(2,1)}, f32[1,64]{1,0:T(1,128)}, f32[1,64]{1,0:T(1,128)}, f32[64,128]{1,0:T(8,128)}...) custom-call(s32[6]{0:T(128)} %bitcast.21, ...), custom_call_target="tpu_custom_call" | custom-call | flops 15000000512 | bytes 1048576 | tf_op jit(solution)/shard_map/in_order/pallas_call | solution.py:837
  225.0 1.5 copy.27
  226.5 1.5 copy.28
  228.0 1.5 copy.26
  229.6 1.7 copy.29

commit v5 on v4

--- a/solution.py
+++ b/solution.py
@@ -109,12 +109,12 @@
 
 def each_head(heads, hd, work):
     def some(i, carry):
-        for n in range(4):
-            h = 4 * i + n
+        for n in range(2):
+            h = 2 * i + n
             work(h, pl.ds(pl.multiple_of(h * hd, hd), hd), pl.ds(h, 1))
         return carry
 
-    lax.fori_loop(0, heads // 4, some, 0)
+    lax.fori_loop(0, heads // 2, some, 0)
 
 
 def key_rows(kb):
@@ -165,19 +165,24 @@
         self.local(step, block).wait()
         self.far(step, block).wait_send()
 
-    def send(self, step, block, values):
+    def send(self, step, block, values, far=True):
         @pl.when(step >= 2)
         def _():
             self.settle(step - 2, block)
 
         self.staged[lax.rem(step, 2)] = values
         self.local(step, block).start()
-        self.far(step, block).start()
-
-    def finish(self, block):
+        if far is True:
+            self.far(step, block).start()
+        else:
+            pl.when(far)(lambda: self.far(step, block).start())
+
+    def finish(self, block, count):
         for step in range(max(self.blocks - 2, 0), self.blocks):
-            self.settle(step, block)
-        for step in range(self.blocks):
+            self.local(step, block).wait()
+            if step < count:
+                self.far(step, block).wait_send()
+        for step in range(count):
             self.far(step, block).wait_recv()
 
 
@@ -257,7 +262,7 @@
         return remote(part, part, self.sems, (n, 4, s - 1), (self.dp ^ 1, self.tensor))
 
     def each(self):
-        return [(n, s) for s in range(self.peers - 1, 0, -1) for n in range(len(self.far))]
+        return [(n, s) for s in range(1, self.peers) for n in range(len(self.far))]
 
     def start(self):
         for n, s in self.each():
@@ -292,7 +297,7 @@
     out_ref, up_ref, down_ref,
     x_own, g_own, q_ref, k_ref, v_ref, ctx_ref, lse_ref, ck_ref, ckt_ref, cv_ref, w_all, conv_all,
     out_far, up_far, down_far,
-    xs, gs, w_ref, conv_ref, cvt_ref, bias_ref, first_sems, last_sems, local_sems,
+    xs, gs, first_all, mask_rows, w_ref, conv_ref, cvt_ref, bias_ref, first_sems, last_sems, local_sems,
 ):
     block = pl.program_id(0)
     blocks = pl.num_programs(0)
@@ -307,6 +312,10 @@
         pltpu.make_async_copy(w_ref, w_all, local_sems.at[0]), pltpu.make_async_copy(conv_ref, conv_all, local_sems.at[1])
     ]
 
+    half = x_ref.shape[0] // 2
+    longest_here = lax.rem(lax.axis_index("tensor"), 2) == 0
+    first = longest_first(lens_ref, half // 3)
+
     @pl.when(block == 0)
     def _():
         for n, src in enumerate((query_ref, key_ref, value_ref)):
@@ -320,27 +329,33 @@
         for src, dst in ((x_ref, xs), (g_ref, gs)):
             for c in range(dim // 128):
                 dst[c] = src[:, c * 128 : (c + 1) * 128].astype(F32)
-        first_gather.pass_around()
         pads = pad_ref[...].astype(F32).T
         for c in range(pads.shape[1]):
             xs[dim // 128, c * 128 : (c + 1) * 128, :] = jnp.broadcast_to(pads[:, c : c + 1], (128, 128))
+        first_gather.pass_around()
+        last_gather.start()
+
+        def prepare(n, carry):
+            x = own_taps(xs, n, first, longest_here)
+            mask_rows[n] = jnp.broadcast_to(x[:, dim:].T[0:1], mask_rows.shape[1:])
+            x = x[:, :dim]
+            normed, _ = norm_rows(x)
+            first_all[n] = (normed * gain_ref[...]).astype(BF16)
+            rows = pl.ds(pl.multiple_of(n * TB, TB), TB)
+            x_own[rows, :] = x.astype(BF16)
+            g_own[rows, :] = own_taps(gs, n, first, longest_here).astype(BF16)
+            return carry
+
+        lax.fori_loop(0, half // TB // 2, prepare, 0)
         first_gather.pass_beside()
-        last_gather.start()
+        lax.fori_loop(half // TB // 2, half // TB, prepare, 0)
         first_gather.arrive()
         first_gather.finish()
         for copy in keep_copies:
             copy.start()
 
-    half = x_ref.shape[0] // 2
-    longest_here = lax.rem(lax.axis_index("tensor"), 2) == 0
-    first = longest_first(lens_ref, half // 3)
-    x = own_taps(xs, block, first, longest_here)
-    mask = x[:, dim:].T[0:1]
-    x = x[:, :dim]
-    x_own[...] = x.astype(BF16)
-    g_own[...] = own_taps(gs, block, first, longest_here).astype(BF16)
-    normed, _ = norm_rows(x)
-    first_in = (normed * gain_ref[...]).astype(BF16)
+    mask = mask_rows[block, 0:1]
+    first_in = first_all[block]
     for slot in range(w_ref.shape[0]):
         at = slice(slot * own, (slot + 1) * own)
         part = nt(w_ref[slot], first_in)
@@ -377,12 +392,12 @@
 
         each_head(heads, hd, head)
 
-    for n in range(half // TB):
-        pl.when(block == n)(functools.partial(attend, n + 1))
-
     @pl.when(block == 1)
     def _():
         last_gather.pass_around()
+
+    for n in range(half // TB):
+        pl.when(block == n)(functools.partial(attend, n + 1))
 
     @pl.when(block == blocks - 2)
     def _():
@@ -451,7 +466,7 @@
             kept_grads[block, :, part] = hidden_grad
     parts = [slice(slot * units, (slot + 1) * units) for slot in range(slots)]
     ffn = sum(nn(acts[:, part], down(slot)) for slot, part in enumerate(parts))
-    swap.send(block, block, (resid + ffn).astype(BF16))
+    swap.send(block, block, (resid + ffn).astype(BF16), block < pl.num_programs(0) - 1)
     back = sum(nt(hidden_grads[:, part], up(slot)) for slot, part in enumerate(parts))
     gain_sum[...] += jnp.sum(back * hat, axis=0, keepdims=True)
     resid_grad = g_low.astype(F32) + norm_back(back, gain, hat, inv_std)
@@ -478,13 +493,13 @@
             put_rows(grads_ref, [out_sum[slot * own : (slot + 1) * own].T], at)
             at += own
         put_rows(grads_ref, [jnp.broadcast_to(gain_sum[...], (GB, dim)).T], at)
-        swap.finish(block)
+        swap.finish(block, kept_in.shape[0] - 1)
 
 
 def backward_kernel(
     heads, hd, own_heads, lens_ref, x_ref, gain_ref, w_ref, conv_ref,
-    q_ref, k_ref, v_ref, lse_ref, dctx_ref, delta_ref, resid_grad_ref, ck_ref, ckt_ref, cv_ref, middle_ref,
-    tokens_ref, tokens_peer, middle_out, last_out, conv_out,
+    q_ref, k_ref, v_ref, lse_ref, dctx_ref, delta_ref, resid_grad_ref, ck_ref, ckt_ref, cv_ref, middle_ref, mixed_ref,
+    tokens_ref, tokens_peer, mixed_last, middle_out, last_out, conv_out,
     staged, bias_ref, convs_ref, dck_sum, dcv_sum, dq_sum, dqkv, weight_sum, kconv_sum, vconv_sum, gain_sum,
     middle_in, last_parts, last_in, conv_parts, conv_in,
     middle_turn, last_turn, conv_turn, middle_sum, last_sum, conv_sum,
@@ -505,6 +520,10 @@
     last = Spread(last_parts, last_in, last_sum, last_sems, local_sems.at[1])
     convs = Spread(conv_parts, conv_in, conv_sum, conv_sems, local_sems.at[2])
 
+    def mixed_tail():
+        rows = mixed_ref.shape[0]
+        return remote(mixed_ref.at[rows - TB : rows], mixed_last, turn_sems, (3,), swap.device)
+
     def turned(n, ref):
         return remote(ref.at[0], ref.at[1], turn_sems, (n,), swap.device)
 
@@ -516,6 +535,7 @@
     def _():
         count = lax.axis_size("dp")
         meet([swap.device] + [(lax.rem(lax.axis_index("dp") + s, count), lax.axis_index("tensor")) for s in range(1, count)])
+        mixed_tail().start()
         middle.start()
         for h in range(heads):
             slot, i = divmod(h, slot_heads)
@@ -585,6 +605,10 @@
     total = resid_grad_ref[...].astype(F32) + norm_back(back, gain, hat, inv_std)
     swap.send(step_id, block, total.astype(BF16))
 
+    @pl.when(block == 1)
+    def _():
+        turn(0, middle_turn, middle.total())
+
     @pl.when(block == 0)
     def _():
         put_rows(last_parts, [weight_sum[...].T, jnp.broadcast_to(gain_sum[...], (GB, dim)).T])
@@ -599,30 +623,31 @@
             ],
         )
         convs.start()
-        middle_total = middle.total()
-        turn(0, middle_turn, middle_total)
         last_total = last.total()
         turn(1, last_turn, last_total)
         conv_total = convs.total()
         turn(2, conv_turn, conv_total)
         for n, (out, ref, total) in enumerate(
-            ((middle_out, middle_turn, middle_total), (last_out, last_turn, last_total), (conv_out, conv_turn, conv_total))
+            ((middle_out, middle_turn, middle_sum), (last_out, last_turn, last_total), (conv_out, conv_turn, conv_total))
         ):
             turned(n, ref).wait()
             cols = out.shape[1]
             split = total.shape[1] - cols
             kept = [total[:, :split]] + ([total[:, 2 * split :]] if cols > split else [])
             out[...] = ref[1].astype(F32) + jnp.concatenate(kept, axis=1)
-        swap.finish(block)
-
-
-def place_rows(lens_ref, longest_here, mine, theirs, natural, out_ref):
+        swap.finish(block, swap.blocks)
+        mixed_tail().wait()
+
+
+def place_rows(lens_ref, longest_here, mine, theirs, theirs_last, natural, out_ref):
     half = mine.shape[0]
     first = longest_first(lens_ref, half // 3)
 
     def taps(block, r, other):
-        rows = pl.ds(pl.multiple_of(block * TB + r * GB, GB), GB)
-        a, b = mine[rows, :].astype(F32), theirs[rows, :].astype(F32)
+        rows = slice(block * TB + r * GB, block * TB + (r + 1) * GB)
+        apart = theirs_last is not None and (block + 1) * TB == half
+        a = mine[rows, :].astype(F32)
+        b = (theirs_last[r * GB : (r + 1) * GB, :] if apart else theirs[rows, :]).astype(F32)
         return jnp.where(longest_here == other, b, a)
 
     for block in range(half // TB):
@@ -637,27 +662,27 @@
 
 
 def last_kernel(
-    hd, lens_ref, mixed_ref, mixed_peer, tokens_ref, tokens_peer, middle_ref, last_ref, conv_ref,
+    hd, lens_ref, mixed_last, mixed_ref, mixed_peer, tokens_ref, tokens_peer, middle_ref, last_ref, conv_ref,
     mixed_out, tokens_out, gain1_out, gain2_out, query_out, key_out, value_out, out_out, kconv_out, vconv_out,
     up_out, down_out, natural_mixed, natural_tokens,
 ):
     longest_here = lax.rem(lax.axis_index("tensor"), 2) == 0
-    place_rows(lens_ref, longest_here, mixed_ref, mixed_peer, natural_mixed, mixed_out)
-    place_rows(lens_ref, longest_here, tokens_ref, tokens_peer, natural_tokens, tokens_out)
+    place_rows(lens_ref, longest_here, mixed_ref, mixed_peer, mixed_last, natural_mixed, mixed_out)
+    place_rows(lens_ref, longest_here, tokens_ref, tokens_peer, None, natural_tokens, tokens_out)
 
     @pl.when(pl.program_id(0) == 0)
     def _():
         units, own = up_out.shape[1], query_out.shape[1]
         up_out[...] = middle_ref[:, 0:units]
-        down_out[...] = middle_ref[:, units : 2 * units].T
-        out_out[...] = middle_ref[:, 2 * units : 2 * units + own].T
+        down_out[...] = middle_ref[:, units : 2 * units]
+        out_out[...] = middle_ref[:, 2 * units : 2 * units + own]
         gain2_out[...] = middle_ref[:, 2 * units + own :].T[0:1]
         for n, out in enumerate((query_out, key_out, value_out)):
             out[...] = last_ref[:, n * own : (n + 1) * own]
         gain1_out[...] = last_ref[:, 3 * own :].T[0:1]
         for n, out in enumerate((kconv_out, vconv_out)):
             for h in range(out.shape[0]):
-                out[h] = conv_ref[:, n * own + h * hd : n * own + (h + 1) * hd].T
+                out[h] = conv_ref[:, n * own + h * hd : n * own + (h + 1) * hd]
 
 
 def whole(shape):
@@ -706,12 +731,13 @@
             grid=(blocks,),
             in_specs=[inside, inside, whole((1, dim))] + [inside] * 6 + [anywhere] * 3,
             out_specs=[
-                rows_spec, rows_spec, cols_spec, cols_spec, cols_spec, cols_spec, lse_spec,
+                whole((rows, dim)), whole((rows, dim)), cols_spec, cols_spec, cols_spec, cols_spec, lse_spec,
                 whole((heads, groups, hd)), whole((width, groups)), whole((heads, groups, hd)),
                 anywhere, anywhere, anywhere, anywhere, anywhere,
             ],
             scratch_shapes=[
                 pltpu.VMEM((dim // 128 + 1, 2 * rows, 128), F32), pltpu.VMEM((dim // 128, 2 * rows, 128), F32),
+                pltpu.VMEM((blocks, TB, dim), BF16), pltpu.VMEM((blocks, 8, TB), F32),
                 pltpu.VMEM((peers, 3 * own, dim), BF16), pltpu.VMEM((peers, own, 2 * conv_cols), BF16),
                 pltpu.VMEM((width, groups), BF16), pltpu.VMEM((groups, GB), F32),
                 pltpu.SemaphoreType.DMA((2, 2, 5, peers - 1)), pltpu.SemaphoreType.DMA((2, 3, 5, peers - 1)),
@@ -784,7 +810,7 @@
     two = 2 * own_heads
     last_cols = 6 * own + GB
     out_dims = [(dim // count, slot_cols + GB), (dim // count, 3 * own + GB), (taps // count, 2 * own)]
-    grad_rows, grad_peer, middle_share, last_share, conv_share = pl.pallas_call(
+    grad_rows, grad_peer, mixed_last, middle_share, last_share, conv_share = pl.pallas_call(
         functools.partial(backward_kernel, heads, hd, two),
         grid_spec=pltpu.PrefetchScalarGridSpec(
             num_scalar_prefetch=1,
@@ -793,9 +819,9 @@
                 back_rows, whole((1, dim)), whole((peers, 3 * own, dim)), whole((peers, own, 2 * conv_cols)),
                 back_cols, back_cols, back_cols, back_lse,
                 back_cols, back_stat, back_rows, whole((heads, groups, hd)), whole((width, groups)),
-                whole((heads, groups, hd)), anywhere,
+                whole((heads, groups, hd)), anywhere, anywhere,
             ],
-            out_specs=[anywhere, anywhere] + [whole(d) for d in out_dims],
+            out_specs=[anywhere] * 3 + [whole(d) for d in out_dims],
             scratch_shapes=[
                 pltpu.VMEM((2, TB, dim), BF16), pltpu.VMEM((groups, GB), F32),
                 pltpu.VMEM((2, heads, taps, hd), BF16), pltpu.VMEM((heads, groups, hd), F32),
@@ -815,40 +841,44 @@
             + [
                 pltpu.SemaphoreType.DMA((2, blocks)), pltpu.SemaphoreType.DMA((blocks,)),
                 pltpu.SemaphoreType.DMA((2, count)), pltpu.SemaphoreType.DMA((2, count)),
-                pltpu.SemaphoreType.DMA((2, count)), pltpu.SemaphoreType.DMA((2, 3)), pltpu.SemaphoreType.DMA((3,)),
+                pltpu.SemaphoreType.DMA((2, count)), pltpu.SemaphoreType.DMA((2, 4)), pltpu.SemaphoreType.DMA((3,)),
             ],
         ),
-        out_shape=[jax.ShapeDtypeStruct((rows, dim), BF16)] * 2 + [jax.ShapeDtypeStruct(d, F32) for d in out_dims],
+        out_shape=[jax.ShapeDtypeStruct((rows, dim), BF16)] * 2
+        + [jax.ShapeDtypeStruct((TB, dim), BF16)]
+        + [jax.ShapeDtypeStruct(d, F32) for d in out_dims],
         compiler_params=pltpu.CompilerParams(
             vmem_limit_bytes=VMEM, dimension_semantics=("arbitrary",), collective_id=2, has_side_effects=True
         ),
         cost_estimate=cost(60),
         name="attention_backward",
-    )(lens, x, gain1, w_all, conv_all, q, k, v, lse, dctx, delta, resid_grad, ck, ckt, cv, middle_grads)
+    )(lens, x, gain1, w_all, conv_all, q, k, v, lse, dctx, delta, resid_grad, ck, ckt, cv, middle_grads, mixed)
 
     share = dim // count
-    own_conv = (own_heads, hd, taps // count)
+    own_conv = (own_heads, taps // count, hd)
     shapes = [
         ((1, share), F32), ((1, share), F32), ((share, own), F32), ((share, own), F32), ((share, own), F32),
-        ((own, share), F32), (own_conv, F32), (own_conv, F32), ((share, units), F32), ((units, share), F32),
+        ((share, own), F32), (own_conv, F32), (own_conv, F32), ((share, units), F32), ((share, units), F32),
     ]
     lane_half = pl.BlockSpec((rows, 128), lambda c: (0, c))
     lane_all = pl.BlockSpec((2 * rows, 128), lambda c: (0, c))
     outs = pl.pallas_call(
         functools.partial(last_kernel, hd),
         grid=(dim // 128,),
-        in_specs=[pl.BlockSpec(memory_space=pltpu.SMEM)] + [lane_half] * 4 + [whole(d) for d in out_dims],
+        in_specs=[pl.BlockSpec(memory_space=pltpu.SMEM), pl.BlockSpec((TB, 128), lambda c: (0, c))]
+        + [lane_half] * 4
+        + [whole(d) for d in out_dims],
         out_specs=[lane_all] * 2 + [whole(d) for d, _ in shapes],
         out_shape=[jax.ShapeDtypeStruct((2 * rows, dim), BF16)] * 2 + [jax.ShapeDtypeStruct(d, t) for d, t in shapes],
         scratch_shapes=[pltpu.VMEM((2 * rows, 128), F32)] * 2,
         compiler_params=params(),
         cost_estimate=cost(15),
         name="in_order",
-    )(lens, mixed, mixed_peer, grad_rows, grad_peer, middle_share, last_share, conv_share)
+    )(lens, mixed_last, mixed, mixed_peer, grad_rows, grad_peer, middle_share, last_share, conv_share)
     mixed, grad_tokens, gain1, gain2, query, key, value, out, kconv, vconv, up, down = outs
     return (
-        mixed, grad_tokens, gain1.reshape(share), gain2.reshape(share), query, key, value, out,
-        kconv.transpose(0, 2, 1), vconv.transpose(0, 2, 1), up, down,
+        mixed, grad_tokens, gain1.reshape(share), gain2.reshape(share), query, key, value, out.T,
+        kconv, vconv, up, down.T,
     )
 
 

time: 235 us -> 201 us (0.86); the launches traced: 231 us -> 201 us
  Pallas kernels: 224 us -> 200 us
  local copies, waits for them, and re-layouts: 6.3 us -> 0 us
    pallas_call x1, Pallas kernels: 86.3 us -> 74.5 us  [on_device(): pl.pallas_call(functools.partial(backward_kernel, heads, hd, two), grid_s...]
    pallas_call x1, Pallas kernels: 62.9 us -> 53.6 us  [on_device(): pl.pallas_call(functools.partial(middle_kernel, heads, hd), grid=(blocks,...]
    unnamed x4 -> x0, local copies, waits for them, and re-layouts: 6.3 us -> none
    pallas_call x1, Pallas kernels: 65.4 us -> 62.2 us  [on_device(): pl.pallas_call(functools.partial(forward_kernel, heads, hd), grid_spec=pl...]
where the time goes in v5:
time: 201 us
  Pallas kernels  200 us (100%)
    pallas_call x1, Pallas kernels, on_device(): pl.pallas_call(functools.partial(backward_kernel, heads, hd, two), grid_s...  74.5 us
    pallas_call x1, Pallas kernels, on_device(): pl.pallas_call(functools.partial(forward_kernel, heads, hd), grid_spec=pl...  62.2 us
    pallas_call x1, Pallas kernels, on_device(): pl.pallas_call(functools.partial(middle_kernel, heads, hd), grid=(blocks,...  53.6 us
    pallas_call x1, Pallas kernels, on_device(): pl.pallas_call(functools.partial(last_kernel, hd), grid=(dim // 128,), in...  9.74 us

profile of v5, /device:TPU:0, one launch (start us, length us, event | category | flops | bytes accessed | tf_op | source)
XLA Modules:
  0.0 200.9 jit_solution(5061331275708162280)
XLA Ops:
  0.6 62.2 %attention_forward.1 = (bf16[2304,512]{1,0:T(8,128)(2,1)}, bf16[2304,512]{1,0:T(8,128)(2,1)}, bf16[512,2304]{1,0:T(8,128)(2,1)}, bf16[512,2304]{1,0:T(8,128)(2,1...) custom-call(s32[6]{0:T(128)} %bitcast.17, ...), custom_call_target="tpu_custom_call" | custom-call | flops 54999998464 | bytes 1048576 | tf_op jit(solution)/shard_map/attention_forward/pallas_call | solution.py:727
  62.9 53.6 %feed_forward.1 = (bf16[2304,512]{1,0:T(8,128)(2,1)}, bf16[2304,512]{1,0:T(8,128)(2,1)}, bf16[2304,512]{1,0:T(8,128)(2,1)}, bf16[512,2304]{1,0:T(8,128)(2,1)}, f...) custom-call(bf16[2304,512]{1,0:T(8,128)(2,1)} %get-tuple-element.51.x_ref, bf16[2304,512]{1,0:T(8,128)(2,1)} %get-tuple-element.58.g_ref, ...), custom_call_target="tpu_custom_call" | custom-call | flops 54999998464 | bytes 1048576 | tf_op jit(solution)/shard_map/feed_forward/pallas_call | solution.py:774
  116.5 74.5 %attention_backward.1 = (bf16[2304,512]{1,0:T(8,128)(2,1)}, bf16[2304,512]{1,0:T(8,128)(2,1)}, bf16[384,512]{1,0:T(8,128)(2,1)}, f32[64,1280]{1,0:T(8,128)}, f32[64,512]{1,0:T(8,128)}, /*index=5*/f32[24,256]{1,0:T(8,128)}) custom-call(s32[6]{0:T(128)} %bitcast.18, bf16[2304,512]{1,0:T(8,128)(2,1)} %get-tuple-element.51.x_ref, f32[1,512]{1,0:T(1,128)} %bitcast.16, ...), custom_call_target="tpu_custom_call" | custom-call | flops 60000002048 | bytes 1048576 | tf_op jit(solution)/shard_map/attention_backward/pallas_call | solution.py:813
  191.0 9.7 %in_order.1 = (bf16[4608,512]{1,0:T(8,128)(2,1)}, bf16[4608,512]{1,0:T(8,128)(2,1)}, f32[1,64]{1,0:T(1,128)}, f32[1,64]{1,0:T(1,128)}, f32[64,128]{1,0:T(8,128)}...) custom-call(s32[6]{0:T(128)} %bitcast.19, ...), custom_call_target="tpu_custom_call" | custom-call | flops 15000000512 | bytes 1048576 | tf_op jit(solution)/shard_map/in_order/pallas_call | solution.py:865

commit v6 on v5

v6 whole, which is shorter than its diff:
```python
import functools
import math

import jax
import jax.numpy as jnp
from jax import lax
from jax.experimental import pallas as pl
from jax.experimental.pallas import tpu as pltpu
from jax.sharding import PartitionSpec as P

F32 = jnp.float32
BF16 = jnp.bfloat16
GB = 128
TB = 3 * GB
NEG = -1e30
LOG2E = 1.0 / math.log(2.0)
VMEM = 60 * 1024 * 1024

ERF_P = 0.43
ERF_C = (
    0.24255178053871013,
    0.24376598744271377,
    0.2089868288055898,
    0.23281685899157548,
    -0.05797941172752005,
    0.3523368029188165,
    -0.2915198548110903,
    0.06904073943922798,
)


def nn(a, b):
    return lax.dot_general(a, b, (((1,), (0,)), ((), ())), preferred_element_type=F32)


def nt(a, b):
    return lax.dot_general(a, b, (((1,), (1,)), ((), ())), preferred_element_type=F32)


def tn(a, b):
    return lax.dot_general(a, b, (((0,), (0,)), ((), ())), preferred_element_type=F32)


def norm_rows(values):
    centred = values - jnp.mean(values, -1, keepdims=True)
    inv_std = lax.rsqrt(jnp.mean(centred * centred, -1, keepdims=True) + 1e-05)
    return centred * inv_std, inv_std


def norm_back(grad_out, gains, normed, inv_std):
    scaled = grad_out * gains
    return inv_std * (
        scaled
        - jnp.mean(scaled, -1, keepdims=True)
        - normed * jnp.mean(scaled * normed, -1, keepdims=True)
    )


def gelu_and_slope(h):
    t = 1.0 / (1.0 + (ERF_P * math.sqrt(0.5)) * jnp.abs(h))
    poly = t * (0.5 * ERF_C[-1]) + 0.5 * ERF_C[-2]
    for c in ERF_C[-3::-1]:
        poly = poly * t + 0.5 * c
    e = jnp.exp2((h * h) * (-0.5 * LOG2E))
    tail = e * (poly * t)
    cdf = jnp.where(h >= 0, 1.0 - tail, tail)
    return h * cdf, cdf + h * (e * (1.0 / math.sqrt(2.0 * math.pi)))


def item_starts(lens_ref, block, longest_here, half):
    places = block * GB + lax.broadcasted_iota(jnp.int32, (1, GB), 1)
    starts = jnp.zeros((1, GB), jnp.int32)
    end = jnp.int32(0)
    for i in range(lens_ref.shape[0] - 1):
        end = end + jnp.where((lens_ref[i] == half) == longest_here, lens_ref[i], 0)
        starts = jnp.where(places >= end, end, starts)
    return places, starts


def longest_first(lens_ref, half):
    first, ahead = jnp.int32(0), jnp.int32(1)
    for i in range(lens_ref.shape[0]):
        ahead = jnp.where(lens_ref[i] == half, 0, ahead)
        first = first + ahead * lens_ref[i]
    return 3 * first


def own_taps(source, block, first, longest_here):
    half = source.shape[1] // 2
    base = block * TB
    parts = []
    for c in range(source.shape[0]):
        for r in range(3):
            inside = source[c, pl.ds(first + base + r, GB, stride=3), :]
            low = source[c, pl.ds(base + r, GB, stride=3), :]
            high = source[c, pl.ds(half + base + r, GB, stride=3), :]
            place = base + r + 3 * lax.broadcasted_iota(jnp.int32, (GB, 1), 0)
            parts.append(jnp.where(longest_here, inside, jnp.where(place < first, low, high)))
    return jnp.concatenate(
        [jnp.concatenate(parts[3 * c : 3 * c + 3], axis=0) for c in range(source.shape[0])], axis=1
    )


def put_bias(bias_ref, places, starts, count):
    for kb in range(count):
        keys = kb * GB + lax.broadcasted_iota(jnp.int32, (GB, GB), 0)
        bias_ref[kb * GB : (kb + 1) * GB, :] = jnp.where((keys >= starts) & (keys < places), 0.0, NEG)


def each_head(heads, hd, work):
    def some(i, carry):
        for n in range(2):
            h = 2 * i + n
            work(h, pl.ds(pl.multiple_of(h * hd, hd), hd), pl.ds(h, 1))
        return carry

    lax.fori_loop(0, heads // 2, some, 0)


def key_rows(kb):
    return pl.ds(pl.multiple_of(kb * GB, GB), GB)


def remote(src, dst, sems, at, device):
    return pltpu.make_async_remote_copy(
        src_ref=src, dst_ref=dst, send_sem=sems.at[(0, *at)], recv_sem=sems.at[(1, *at)],
        device_id=device, device_id_type=pl.DeviceIdType.MESH,
    )


def meet(devices):
    barrier = pltpu.get_barrier_semaphore()
    for device in devices:
        pl.semaphore_signal(barrier, inc=1, device_id=device, device_id_type=pl.DeviceIdType.MESH)
    pl.semaphore_wait(barrier, len(devices))


def put_rows(ref, pieces, at=0):
    parities, count, rows, _ = ref.shape
    for piece in pieces:
        cols = piece.shape[1]
        for d in range(parities * count):
            ref[d % 2, d // 2, :, at : at + cols] = piece[d * rows : (d + 1) * rows].astype(ref.dtype)
        at += cols


class Swap:
    def __init__(self, staged, mine, theirs, sems, local_sems):
        self.staged, self.mine, self.theirs, self.sems, self.local_sems = staged, mine, theirs, sems, local_sems
        self.device = (lax.axis_index("dp"), lax.axis_index("tensor") ^ 1)
        self.blocks = mine.shape[0] // TB

    def rows(self, block):
        return pl.ds(pl.multiple_of(block * TB, TB), TB)

    def local(self, block):
        return pltpu.make_async_copy(
            self.staged.at[block], self.mine.at[self.rows(block)], self.local_sems.at[block]
        )

    def far(self, block):
        return remote(
            self.staged.at[block], self.theirs.at[self.rows(block)], self.sems, (block,), self.device
        )

    def send(self, block, values):
        self.staged[block] = values
        self.local(block).start()
        self.far(block).start()

    def finish(self):
        for block in range(self.blocks):
            self.local(block).wait()
            self.far(block).wait()


class Spread:
    def __init__(self, source, paired, landed, sums, sems):
        self.source, self.paired, self.landed, self.sums, self.sems = source, paired, landed, sums, sems
        self.me, self.peer = lax.axis_index("dp"), lax.axis_index("tensor")
        self.parity = lax.rem(self.me, 2)
        self.count = lax.axis_size("dp")

    def beside(self):
        return remote(
            self.source.at[1 - self.parity], self.paired, self.sems, (0,), (self.me ^ 1, self.peer)
        )

    def copy(self, s):
        there = lax.rem(self.me + 2 * s, self.count)
        return remote(self.paired.at[there // 2], self.landed.at[s], self.sems, (s,), (there, self.peer))

    def start(self):
        self.beside().start()

    def pass_on(self):
        self.beside().wait()

        def add(n, carry):
            pair = self.paired[n].astype(F32) + self.source[self.parity, n].astype(F32)
            self.paired[n] = pair.astype(BF16)
            return carry

        lax.fori_loop(0, self.count // 2, add, 0)

        def step(s, carry):
            self.copy(s).start()
            return carry

        lax.fori_loop(1, self.count // 2, step, 0)

    def total(self):
        def step(s, carry):
            self.copy(s).wait()
            return carry

        lax.fori_loop(1, self.count // 2, step, 0)
        self.sums[...] = self.paired[self.me // 2].astype(F32)

        def add(s, carry):
            self.sums[...] += self.landed[s].astype(F32)
            return carry

        lax.fori_loop(1, self.count // 2, add, 0)
        return self.sums


class Gather:
    def __init__(self, own, far, sems):
        self.own, self.far, self.sems = own, far, sems
        self.dp, self.tensor = lax.axis_index("dp"), lax.axis_index("tensor")
        self.peers = lax.axis_size("tensor")

    def devices(self):
        return [(self.dp, self.tensor ^ s) for s in range(1, self.peers)] + [
            (self.dp ^ m, self.tensor) for m in (1, 2, 4, 6)
        ]

    def eighth(self, array):
        rows = array.shape[0] // 8
        place = lax.rem(self.dp, 2) * 4 + lax.rem(self.dp, 8) // 2
        return array.at[pl.ds(pl.multiple_of(place * rows, rows), rows)]

    def half(self, array):
        rows = array.shape[0] // 2
        return array.at[pl.ds(pl.multiple_of(lax.rem(self.dp, 2) * rows, rows), rows)]

    def across(self, n, s):
        device = (self.dp, self.tensor ^ s)
        return remote(
            self.eighth(self.own[n]), self.eighth(self.far[n].at[s - 1]), self.sems, (n, 0, s - 1), device
        )

    def around(self, n, s, m):
        part = self.eighth(self.far[n].at[s - 1])
        return remote(part, part, self.sems, (n, m // 2, s - 1), (self.dp ^ m, self.tensor))

    def beside(self, n, s):
        part = self.half(self.far[n].at[s - 1])
        return remote(part, part, self.sems, (n, 4, s - 1), (self.dp ^ 1, self.tensor))

    def each(self, s=None):
        peers = range(1, self.peers) if s is None else (s,)
        return [(n, s) for s in peers for n in range(len(self.far))]

    def start(self):
        for n, s in self.each():
            self.across(n, s).start()

    def pass_around(self, s=None):
        for n, s in self.each(s):
            self.across(n, s).wait_recv()
            for m in (6, 4, 2):
                self.around(n, s, m).start()

    def pass_beside(self, s=None):
        for n, s in self.each(s):
            for m in (2, 4, 6):
                self.around(n, s, m).wait_recv()
            self.beside(n, s).start()

    def arrive(self):
        for n, s in self.each():
            self.beside(n, s).wait_recv()

    def finish(self):
        for n, s in self.each():
            self.across(n, s).wait_send()
            for m in (2, 4, 6):
                self.around(n, s, m).wait_send()
            self.beside(n, s).wait_send()


def attend_forward(
    heads, hd, count, places, starts, bias_ref, ck_ref, cvt_ref, q_ref, k_ref, v_ref, ctx_ref, put_lse
):
    scale = LOG2E / math.sqrt(hd)
    keys = slice(0, count * GB)
    put_bias(bias_ref, places, starts, count)

    def head(h, band, one):
        q = q_ref[band, :]
        own_score = jnp.sum(q.astype(F32) * k_ref[band, :].astype(F32), axis=0, keepdims=True) * scale
        s = nn(ck_ref[h, keys, :], q) * scale + jnp.concatenate([bias_ref[keys, :]] * 3, axis=1)
        top = jnp.maximum(own_score, jnp.max(s, axis=0, keepdims=True))
        p = jnp.exp2(s - top)
        own_prob = jnp.exp2(own_score - top)
        total = own_prob + jnp.sum(p, axis=0, keepdims=True)
        mixed = own_prob * v_ref[band, :].astype(F32) + nn(cvt_ref[band, keys], p.astype(BF16))
        ctx_ref[band, :] = (mixed * (1.0 / total)).astype(BF16)
        put_lse(one, top + jnp.log(total) * LOG2E)

    each_head(heads, hd, head)


def forward_kernel(
    heads, hd, lens_ref, x_ref, g_ref, gain_ref, pad_ref, query_ref, key_ref, value_ref, kconv_ref, vconv_ref,
    out_ref, up_ref, down_ref,
    x_own, g_own, q_ref, k_ref, v_ref, ctx_ref, lse_ref, ck_ref, ckt_ref, cv_ref, cvt_ref, w_all, conv_all,
    out_far, up_far, down_far,
    xs, gs, first_all, mask_rows, w_ref, conv_ref, bias_ref, first_sems, last_sems, local_sems,
):
    block = pl.program_id(0)
    blocks = pl.num_programs(0)
    own_heads, _, taps = kconv_ref.shape
    own = own_heads * hd
    dim = x_ref.shape[1]
    conv_cols = conv_ref.shape[2] // 2
    first_gather = Gather((w_ref.at[0], conv_ref.at[0]), (w_ref.at[1:], conv_ref.at[1:]), first_sems)
    last_gather = Gather((out_ref, up_ref, down_ref), (out_far, up_far, down_far), last_sems)
    keep_copies = [
        pltpu.make_async_copy(w_ref, w_all, local_sems.at[0]), pltpu.make_async_copy(conv_ref, conv_all, local_sems.at[1])
    ]

    half = x_ref.shape[0] // 2
    blocks_there = half // TB
    longest_here = lax.rem(lax.axis_index("tensor"), 2) == 0
    first = longest_first(lens_ref, half // 3)

    @pl.when(block == 0)
    def _():
        for n, src in enumerate((query_ref, key_ref, value_ref)):
            w_ref[0, n * own : (n + 1) * own, :] = src[...].T
        conv_ref[0] = jnp.zeros_like(conv_ref[0])
        for n, src in enumerate((kconv_ref, vconv_ref)):
            for h in range(own_heads):
                conv_ref[0, h * hd : (h + 1) * hd, n * conv_cols : n * conv_cols + taps] = src[h]
        meet(first_gather.devices())
        first_gather.start()
        for src, dst in ((x_ref, xs), (g_ref, gs)):
            for c in range(dim // 128):
                dst[c] = src[:, c * 128 : (c + 1) * 128].astype(F32)
        pads = pad_ref[...].astype(F32).T
        for c in range(pads.shape[1]):
            xs[dim // 128, c * 128 : (c + 1) * 128, :] = jnp.broadcast_to(pads[:, c : c + 1], (128, 128))
        first_gather.pass_around()
        last_gather.start()

        def prepare(n, carry):
            x = own_taps(xs, n, first, longest_here)
            mask_rows[n] = jnp.broadcast_to(x[:, dim:].T[0:1], mask_rows.shape[1:])
            x = x[:, :dim]
            normed, _ = norm_rows(x)
            first_all[n] = (normed * gain_ref[...]).astype(BF16)
            rows = pl.ds(pl.multiple_of(n * TB, TB), TB)
            x_own[rows, :] = x.astype(BF16)
            g_own[rows, :] = own_taps(gs, n, first, longest_here).astype(BF16)
            return carry

        lax.fori_loop(0, half // TB // 2, prepare, 0)
        first_gather.pass_beside()
        lax.fori_loop(half // TB // 2, half // TB, prepare, 0)
        first_gather.arrive()
        first_gather.finish()
        for copy in keep_copies:
            copy.start()

    mask = mask_rows[block, 0:1]
    first_in = first_all[block]
    for slot in range(w_ref.shape[0]):
        at = slice(slot * own, (slot + 1) * own)
        part = nt(w_ref[slot], first_in)
        q_ref[at, :] = part[0:own].astype(BF16)
        k_ref[at, :] = (part[own : 2 * own] * mask).astype(BF16)
        v_ref[at, :] = (part[2 * own : 3 * own] * mask).astype(BF16)
    rows = key_rows(block)
    for h in range(heads):
        band = slice(h * hd, (h + 1) * hd)
        slot, i = divmod(h, own_heads)
        for n, src, plain, trans in ((0, k_ref, ck_ref, ckt_ref), (1, v_ref, cv_ref, cvt_ref)):
            grouped = jnp.concatenate([src[band, r * GB : (r + 1) * GB] for r in range(3)], axis=0)
            comp = nn(conv_ref[slot, i * hd : (i + 1) * hd, n * conv_cols : n * conv_cols + taps], grouped)
            trans[band, rows] = comp.astype(BF16)
            plain[h, rows, :] = comp.T.astype(BF16)
    places, starts = item_starts(lens_ref, block, longest_here, half // 3)
    lse_ref[heads:, :] = jnp.broadcast_to(mask, (lse_ref.shape[0] - heads, TB))

    peers = w_ref.shape[0]
    for s in range(1, peers):
        pl.when(block == s - 1)(functools.partial(last_gather.pass_around, s))
        if s < peers - 1:
            pl.when(block == blocks_there - peers + 1 + s)(functools.partial(last_gather.pass_beside, s))

    @pl.when(block < blocks // 2)
    def _():
        lse_ref[0:heads, :] = jnp.zeros_like(lse_ref[0:heads, :])

    def put_lse(one, values):
        lse_ref[one, :] = values

    for n in range(blocks_there // 2, blocks_there):
        pl.when(block == n)(
            functools.partial(
                attend_forward, heads, hd, n + 1, places, starts, bias_ref, ck_ref, cvt_ref, q_ref, k_ref, v_ref,
                ctx_ref, put_lse,
            )
        )

    @pl.when(block == blocks - 1)
    def _():
        last_gather.pass_beside(w_ref.shape[0] - 1)

    @pl.when(block == blocks - 1)
    def _():
        last_gather.arrive()
        last_gather.finish()
        for copy in keep_copies:
            copy.wait()


def feed_forward(
    heads, hd, block, swap, x_ref, g_ref, gain_ref, ctx_ref, out_ref, up_ref, down_ref,
    out_far, up_far, down_far, resid_all, dctx_all, delta_all, grads_ref,
    acts, hidden_grads, pre, act_grads, ff_sum, out_sum, gain_sum,
):
    own, two = out_ref.shape[0], out_sum.shape[0]
    units = up_ref.shape[1]
    step = pre.shape[2]
    slots = up_far.shape[0] + 1
    gain = gain_ref[...]
    g_low = g_ref[...]
    resid = x_ref[...].astype(F32) + tn(ctx_ref[0:own, :], out_ref[...]) + tn(ctx_ref[own:, :], out_far[...])
    hat, inv_std = norm_rows(resid)
    second_in = (hat * gain).astype(BF16)

    def up(slot, cols=slice(None)):
        return up_ref[:, cols] if slot == 0 else up_far[slot - 1, :, cols]

    def down(slot, rows=slice(None)):
        return down_ref[rows, :] if slot == 0 else down_far[slot - 1, rows, :]

    def products(c):
        slot, at = divmod(c * step, units)
        part = slice(at, at + step)
        pre[c % 2] = nn(second_in, up(slot, part))
        act_grads[c % 2] = nt(g_low, down(slot, part))

    count = slots * units // step
    products(0)
    for c in range(count):
        if c + 1 < count:
            products(c + 1)
        act, slope = gelu_and_slope(pre[c % 2])
        act = act.astype(BF16)
        hidden_grad = (act_grads[c % 2] * slope).astype(BF16)
        part = slice(c * step, (c + 1) * step)
        acts[:, part] = act
        hidden_grads[:, part] = hidden_grad
        slot, at = divmod(c * step, units)
        if slot < 2:
            ff_sum[slot, 0, :, at : at + step] += tn(second_in, hidden_grad)
            ff_sum[slot, 1, :, at : at + step] += tn(g_low, act)
    parts = [slice(slot * units, (slot + 1) * units) for slot in range(slots)]
    ffn = sum(nn(acts[:, part], down(slot)) for slot, part in enumerate(parts))
    swap.send(block, (resid + ffn).astype(BF16))
    back = sum(nt(hidden_grads[:, part], up(slot)) for slot, part in enumerate(parts))
    gain_sum[...] += jnp.sum(back * hat, axis=0, keepdims=True)
    resid_grad = g_low.astype(F32) + norm_back(back, gain, hat, inv_std)
    attn_grad = resid_grad.astype(BF16)
    resid_all[block] = attn_grad
    out_sum[...] += nn(ctx_ref[0:two, :], attn_grad)
    dctx = jnp.concatenate([nt(out_ref[...], attn_grad), nt(out_far[...], attn_grad)], axis=0).astype(BF16)
    dctx_all[block] = dctx
    dots = dctx.astype(F32) * ctx_ref[...].astype(F32)
    for h in range(heads):
        delta_all[block, h : h + 1, :] = jnp.sum(dots[h * hd : (h + 1) * hd], axis=0, keepdims=True)

    @pl.when(block == 0)
    def _():
        pieces = []
        for slot in range(2):
            pieces += [ff_sum[slot, 0], ff_sum[slot, 1], out_sum[slot * own : (slot + 1) * own].T]
        put_rows(grads_ref, pieces + [jnp.broadcast_to(gain_sum[...], (GB, gain.shape[1])).T])


def attention_back(
    heads, hd, own_heads, lens_ref, block, swap, x_ref, gain_ref, w_ref, q_ref, k_ref, v_ref, stats_ref,
    lse_all, dctx_all, delta_all, resid_all, ck_ref, ckt_ref, cv_ref,
    bias_ref, convs_ref, dck_sum, dcv_sum, dq_sum, dqkv, weight_sum, kconv_sum, vconv_sum, gain_sum,
):
    own = own_heads * hd
    slots, _, dim = w_ref.shape
    slot_heads = heads // slots
    lanes = slot_heads * hd
    factor = 1.0 / math.sqrt(hd)
    scale = LOG2E * factor
    longest_here = lax.rem(lax.axis_index("tensor"), 2) == 0
    places, starts = item_starts(lens_ref, block, longest_here, ck_ref.shape[1])

    def attend(count):
        keys = slice(0, count * GB)
        put_bias(bias_ref, places, starts, count)

        def head(h, band, one):
            q, dctx = q_ref[band, :], dctx_all[block, band, :]
            s = nn(ck_ref[h, keys, :], q) * scale + jnp.concatenate([bias_ref[keys, :]] * 3, axis=1)
            p = jnp.exp2(s - lse_all[block, one, :])
            dp = nn(cv_ref[h, keys, :], dctx)
            ds = (p * (dp - delta_all[block, one, :])).astype(BF16)
            dcv_sum[h, keys, :] += nt(p.astype(BF16), dctx)
            dck_sum[h, keys, :] += nt(ds, q)
            dq_sum[band, :] = nn(ckt_ref[band, keys], ds)

        each_head(heads, hd, head)

    for n in range(ck_ref.shape[1] // GB):
        pl.when(block == n)(functools.partial(attend, n + 1))
    mask = stats_ref[heads : heads + 1, :]
    rows = key_rows(block)
    for h in range(heads):
        band = slice(h * hd, (h + 1) * hd)
        one = slice(h, h + 1)
        q, k = q_ref[band, :].astype(F32), k_ref[band, :].astype(F32)
        v, dctx = v_ref[band, :].astype(F32), dctx_all[block, band, :].astype(F32)
        own_prob = jnp.exp2(jnp.sum(q * k, axis=0, keepdims=True) * scale - lse_all[block, one, :])
        own_dprob = jnp.sum(dctx * v, axis=0, keepdims=True)
        own_dscore = own_prob * (own_dprob - delta_all[block, one, :]) * factor
        slot, i = divmod(h, slot_heads)
        base = slot * 3 * lanes + i * hd
        dqkv[base : base + hd, :] = (dq_sum[band, :] * factor + own_dscore * k).astype(BF16)
        dck = (dck_sum[h, rows, :] * factor).astype(BF16)
        dcv = dcv_sum[h, rows, :].astype(BF16)
        for n, src, total, grad, beside in (
            (0, k_ref, kconv_sum, dck, own_dscore * q),
            (1, v_ref, vconv_sum, dcv, own_prob * dctx),
        ):
            spread = nt(convs_ref[n, h], grad)
            spread = jnp.concatenate([spread[r * hd : (r + 1) * hd] for r in range(3)], axis=1)
            at = base + (n + 1) * lanes
            dqkv[at : at + hd, :] = ((spread + beside) * mask).astype(BF16)
            if h < own_heads:
                grouped = jnp.concatenate([src[band, r * GB : (r + 1) * GB] for r in range(3)], axis=0)
                total[h] += nn(grouped, grad)
    hat, inv_std = norm_rows(x_ref[...].astype(F32))
    gain = gain_ref[...]
    first_in = (hat * gain).astype(BF16)
    weight_sum[...] += nn(dqkv[0 : 3 * own, :], first_in)
    back = tn(dqkv[...], w_ref[...].reshape(slots * 3 * lanes, dim))
    gain_sum[...] += jnp.sum(back * hat, axis=0, keepdims=True)
    total = resid_all[block].astype(F32) + norm_back(back, gain, hat, inv_std)
    swap.send(block, total.astype(BF16))


def schedule(step, blocks):
    late = (step + 3) // (2 * blocks)
    started = (step + 2 * blocks - 1) // (2 * blocks)
    last = (step + 4) // (2 * blocks)
    forward = started * (1 - last) * (blocks - 1 - (step + 1) // 2)
    forward = forward + (1 - started) * (blocks - 1)
    backward = started * ((1 - late) * (blocks - step // 2) + late * (2 * blocks - 1 - step))
    backward = backward + (1 - started) * (blocks - 1)
    backward = jnp.minimum(backward, blocks - 1)
    is_forward = (1 - started) + started * (1 - late) * ((step % 2) * (1 - last) + last * (1 - late))
    return forward, backward, is_forward


def later_kernel(
    heads, hd, own_heads, lens_ref,
    x_ref, g_ref, gain2_ref, ctx_ref, out_ref, up_ref, down_ref, out_far, up_far, down_far,
    q_front, k_front, v_front,
    x_back, gain1_ref, q_ref, k_ref, v_ref, lse_ref, w_hbm, conv_hbm, ck_hbm, ckt_hbm, cv_hbm, cvt_hbm,
    mixed_ref, mixed_peer, tokens_ref, tokens_peer, middle_out, last_out, conv_out,
    w_ref, conv_ref, ck_ref, ckt_ref, cv_ref, cvt_ref,
    mixed_staged, acts, hidden_grads, pre, act_grads, ff_sum, out_sum, gain2_sum,
    ctx_block, lse_all, dctx_all, resid_all, delta_all,
    bias_ref, convs_ref, dck_sum, dcv_sum, dq_sum, dqkv, weight_sum, kconv_sum, vconv_sum, gain1_sum,
    middle_parts, middle_pair, middle_in, last_parts, last_pair, last_in, conv_parts, conv_pair, conv_in,
    middle_turn, last_turn, conv_turn, middle_sum, last_sum, conv_sum,
    mixed_sems, mixed_local, swap_sems, swap_local, middle_sems, last_sems, conv_sems, turn_sems, load_sems,
):
    step_id = pl.program_id(0)
    blocks = dctx_all.shape[0]
    forward_block, backward_block, is_forward = schedule(step_id, blocks)
    mixed_swap = Swap(mixed_staged, mixed_ref, mixed_peer, mixed_sems, mixed_local)
    swap = Swap(resid_all, tokens_ref, tokens_peer, swap_sems, swap_local)
    middle = Spread(middle_parts, middle_pair, middle_in, middle_sum, middle_sems)
    last = Spread(last_parts, last_pair, last_in, last_sum, last_sems)
    convs = Spread(conv_parts, conv_pair, conv_in, conv_sum, conv_sems)
    slots, _, dim = w_ref.shape
    taps = convs_ref.shape[2]
    conv_cols = conv_ref.shape[2] // 2
    slot_heads = heads // slots

    loads = [
        pltpu.make_async_copy(src, dst, load_sems.at[n])
        for n, (src, dst) in enumerate(
            (
                (w_hbm, w_ref), (conv_hbm, conv_ref), (ck_hbm, ck_ref), (ckt_hbm, ckt_ref), (cv_hbm, cv_ref),
                (cvt_hbm, cvt_ref),
            )
        )
    ]

    @pl.when(step_id == 0)
    def _():
        for load in loads:
            load.start()
        count = lax.axis_size("dp")
        me, peer = lax.axis_index("dp"), lax.axis_index("tensor")
        meet([swap.device, (me ^ 1, peer)] + [(lax.rem(me + 2 * s, count), peer) for s in range(1, count // 2)])
        for ref in (
            ff_sum, out_sum, gain2_sum, dck_sum, dcv_sum, weight_sum, kconv_sum, vconv_sum, gain1_sum,
        ):
            ref[...] = jnp.zeros_like(ref)

    @pl.when(step_id == 2)
    def _():
        for load in loads:
            load.wait()
        for h in range(heads):
            slot, i = divmod(h, slot_heads)
            for n in range(2):
                conv = conv_ref[slot, i * hd : (i + 1) * hd, n * conv_cols : n * conv_cols + taps]
                convs_ref[n, h] = conv.astype(F32).T.astype(BF16)

    longest_here = lax.rem(lax.axis_index("tensor"), 2) == 0

    @pl.when(is_forward == 1)
    def _():
        places, starts = item_starts(lens_ref, forward_block, longest_here, ck_ref.shape[1])

        def put_lse(one, values):
            lse_all[forward_block, one, :] = values

        @pl.when(forward_block >= blocks // 2)
        def _():
            ctx_block[...] = ctx_ref[...]

        for n in range(blocks // 2):
            pl.when(forward_block == n)(
                functools.partial(
                    attend_forward, heads, hd, n + 1, places, starts, bias_ref, ck_ref, cvt_ref, q_front, k_front,
                    v_front, ctx_block, put_lse,
                )
            )
        feed_forward(
            heads, hd, forward_block, mixed_swap, x_ref, g_ref, gain2_ref, ctx_block, out_ref, up_ref, down_ref,
            out_far, up_far, down_far, resid_all, dctx_all, delta_all, middle_parts,
            acts, hidden_grads, pre, act_grads, ff_sum, out_sum, gain2_sum,
        )

        @pl.when(forward_block == 0)
        def _():
            middle.start()

    @pl.when(is_forward == 0)
    def _():
        @pl.when(backward_block >= blocks // 2)
        def _():
            lse_all[backward_block] = lse_ref[0:heads, :]

        attention_back(
            heads, hd, own_heads, lens_ref, backward_block, swap, x_back, gain1_ref, w_ref, q_ref, k_ref, v_ref, lse_ref,
            lse_all, dctx_all, delta_all, resid_all, ck_ref, ckt_ref, cv_ref,
            bias_ref, convs_ref, dck_sum, dcv_sum, dq_sum, dqkv, weight_sum, kconv_sum, vconv_sum, gain1_sum,
        )

    @pl.when((is_forward == 0) & (backward_block == blocks // 2 - 1))
    def _():
        middle.pass_on()

    def turned(n, ref):
        return remote(ref.at[0], ref.at[1], turn_sems, (n,), swap.device)

    def turn(n, ref, total):
        ref[0] = total[:, total.shape[1] - ref.shape[2] :].astype(BF16)
        turned(n, ref).start()

    @pl.when(step_id == 2 * blocks - 1)
    def _():
        put_rows(last_parts, [weight_sum[...].T, jnp.broadcast_to(gain1_sum[...], (GB, dim)).T])
        last.start()
        put_rows(
            conv_parts,
            [
                total[h]
                for slot in range(2)
                for total in (kconv_sum, vconv_sum)
                for h in range(slot * slot_heads, (slot + 1) * slot_heads)
            ],
        )
        convs.start()
        last.pass_on()
        convs.pass_on()
        sums = ((middle_out, middle_turn, middle), (last_out, last_turn, last), (conv_out, conv_turn, convs))
        for n, (_, ref, spread) in enumerate(sums):
            turn(n, ref, spread.total())
        for n, (out, ref, spread) in enumerate(sums):
            turned(n, ref).wait()
            total, cols = spread.sums, out.shape[1]
            split = total.shape[1] - cols
            kept = [total[:, :split]] + ([total[:, 2 * split :]] if cols > split else [])
            out[...] = ref[1].astype(F32) + jnp.concatenate(kept, axis=1)
        mixed_swap.finish()
        swap.finish()


def place_rows(lens_ref, longest_here, mine, theirs, natural, out_ref):
    half = mine.shape[0]
    first = longest_first(lens_ref, half // 3)

    def taps(block, r, other):
        rows = slice(block * TB + r * GB, block * TB + (r + 1) * GB)
        a, b = mine[rows, :].astype(F32), theirs[rows, :].astype(F32)
        return jnp.where(longest_here == other, b, a)

    for block in range(half // TB):
        for r in range(3):
            others = taps(block, r, True)
            for base in (0, half):
                natural[pl.ds(base + block * TB + r, GB, stride=3), :] = others
    for block in range(half // TB):
        for r in range(3):
            natural[pl.ds(first + block * TB + r, GB, stride=3), :] = taps(block, r, False)
    out_ref[...] = natural[...].astype(BF16)


def last_kernel(
    hd, lens_ref, mixed_ref, mixed_peer, tokens_ref, tokens_peer, middle_ref, last_ref, conv_ref,
    mixed_out, tokens_out, gain1_out, gain2_out, query_out, key_out, value_out, out_out, kconv_out, vconv_out,
    up_out, down_out, natural_mixed, natural_tokens,
):
    longest_here = lax.rem(lax.axis_index("tensor"), 2) == 0
    place_rows(lens_ref, longest_here, mixed_ref, mixed_peer, natural_mixed, mixed_out)
    place_rows(lens_ref, longest_here, tokens_ref, tokens_peer, natural_tokens, tokens_out)

    @pl.when(pl.program_id(0) == 0)
    def _():
        units, own = up_out.shape[1], query_out.shape[1]
        up_out[...] = middle_ref[:, 0:units]
        down_out[...] = middle_ref[:, units : 2 * units]
        out_out[...] = middle_ref[:, 2 * units : 2 * units + own]
        gain2_out[...] = middle_ref[:, 2 * units + own :].T[0:1]
        for n, out in enumerate((query_out, key_out, value_out)):
            out[...] = last_ref[:, n * own : (n + 1) * own]
        gain1_out[...] = last_ref[:, 3 * own :].T[0:1]
        for n, out in enumerate((kconv_out, vconv_out)):
            for h in range(out.shape[0]):
                out[h] = conv_ref[:, n * own + h * hd : n * own + (h + 1) * hd]


def whole(shape):
    return pl.BlockSpec(shape, lambda *_: (0,) * len(shape))


def cost(micros):
    return pl.CostEstimate(flops=int(micros * 1e9), bytes_accessed=1 << 20, transcendentals=0)


def params():
    return pltpu.CompilerParams(vmem_limit_bytes=VMEM, dimension_semantics=("arbitrary",))


def on_device(
    tokens, first_gain, second_gain, query_weight, key_weight, value_weight, out_weight,
    key_conv, value_conv, up_weight, down_weight, pad_mask, item_lengths, cotangent,
):
    dim = tokens.shape[1]
    own_heads, taps, hd = key_conv.shape
    peers = lax.axis_size("tensor")
    heads = own_heads * peers
    width = heads * hd
    own = own_heads * hd
    units = up_weight.shape[1]
    lens = item_lengths[0]
    rows = tokens.shape[0] // 2
    blocks = rows // TB
    groups = rows // 3
    pads = pad_mask.reshape(-1, 128)
    key_conv, value_conv = key_conv.transpose(0, 2, 1), value_conv.transpose(0, 2, 1)
    conv_cols = -(-taps // 128) * 128
    stats = heads + 8
    gain1, gain2 = first_gain[None], second_gain[None]

    rows_spec = pl.BlockSpec((TB, dim), lambda b, *_: (b, 0))
    cols_spec = pl.BlockSpec((width, TB), lambda b, *_: (0, b))
    stat_spec = pl.BlockSpec((heads, TB), lambda b, *_: (0, b))
    lse_spec = pl.BlockSpec((stats, TB), lambda b, *_: (0, b))
    early = blocks // 2
    late_cols = pl.BlockSpec((width, TB), lambda b, *_: (0, jnp.maximum(b - early, 0)))
    anywhere = pl.BlockSpec(memory_space=pl.ANY)
    inside = pl.BlockSpec(memory_space=pltpu.VMEM)
    x, g, q, k, v, ctx, lse, ck, ckt, cv, cvt, w_all, conv_all, out_far, up_far, down_far = pl.pallas_call(
        functools.partial(forward_kernel, heads, hd),
        grid_spec=pltpu.PrefetchScalarGridSpec(
            num_scalar_prefetch=1,
            grid=(blocks,),
            in_specs=[inside, inside, whole((1, dim))] + [inside] * 6 + [anywhere] * 3,
            out_specs=[
                whole((rows, dim)), whole((rows, dim)), cols_spec, cols_spec, cols_spec, late_cols, lse_spec,
                whole((heads, groups, hd)), whole((width, groups)), whole((heads, groups, hd)), whole((width, groups)),
                anywhere, anywhere, anywhere, anywhere, anywhere,
            ],
            scratch_shapes=[
                pltpu.VMEM((dim // 128 + 1, 2 * rows, 128), F32), pltpu.VMEM((dim // 128, 2 * rows, 128), F32),
                pltpu.VMEM((blocks, TB, dim), BF16), pltpu.VMEM((blocks, 8, TB), F32),
                pltpu.VMEM((peers, 3 * own, dim), BF16), pltpu.VMEM((peers, own, 2 * conv_cols), BF16),
                pltpu.VMEM((groups, GB), F32),
                pltpu.SemaphoreType.DMA((2, 2, 5, peers - 1)), pltpu.SemaphoreType.DMA((2, 3, 5, peers - 1)),
                pltpu.SemaphoreType.DMA((2,)),
            ],
        ),
        out_shape=[jax.ShapeDtypeStruct((rows, dim), BF16)] * 2
        + [jax.ShapeDtypeStruct((width, rows), BF16)] * 3
        + [jax.ShapeDtypeStruct((width, (blocks - early) * TB), BF16)]
        + [
            jax.ShapeDtypeStruct((stats, rows), F32),
            jax.ShapeDtypeStruct((heads, groups, hd), BF16),
            jax.ShapeDtypeStruct((width, groups), BF16),
            jax.ShapeDtypeStruct((heads, groups, hd), BF16),
            jax.ShapeDtypeStruct((width, groups), BF16),
            jax.ShapeDtypeStruct((peers, 3 * own, dim), BF16),
            jax.ShapeDtypeStruct((peers, own, 2 * conv_cols), BF16),
            jax.ShapeDtypeStruct((peers - 1, own, dim), BF16),
            jax.ShapeDtypeStruct((peers - 1, dim, units), BF16),
            jax.ShapeDtypeStruct((peers - 1, units, dim), BF16),
        ],
        compiler_params=pltpu.CompilerParams(
            vmem_limit_bytes=VMEM, dimension_semantics=("arbitrary",), collective_id=0, has_side_effects=True
        ),
        cost_estimate=cost(55),
        name="attention_forward",
    )(
        lens, tokens, cotangent, gain1, pads, query_weight, key_weight, value_weight, key_conv, value_conv,
        out_weight, up_weight, down_weight,
    )

    count = lax.axis_size("dp")
    slot_cols = 2 * units + own
    mid_cols = 2 * slot_cols + GB
    last_cols = 6 * own + GB
    two = 2 * own_heads
    step = 256

    def forward_at(n):
        return schedule(n, blocks)[0]

    def backward_at(n):
        return schedule(n, blocks)[1]

    def left_at(n):
        return jnp.minimum(forward_at(n), early - 1)

    left_cols = pl.BlockSpec((width, TB), lambda n, *_: (0, left_at(n)))
    front_rows = pl.BlockSpec((TB, dim), lambda n, *_: (forward_at(n), 0))
    front_cols = pl.BlockSpec((width, TB), lambda n, *_: (0, jnp.maximum(forward_at(n) - early, 0)))
    back_rows = pl.BlockSpec((TB, dim), lambda n, *_: (backward_at(n), 0))
    back_cols = pl.BlockSpec((width, TB), lambda n, *_: (0, backward_at(n)))
    back_lse = pl.BlockSpec((stats, TB), lambda n, *_: (0, backward_at(n)))
    out_dims = [(dim // count, slot_cols + GB), (dim // count, 3 * own + GB), (taps // count, 2 * own)]
    swap_sems = [pltpu.SemaphoreType.DMA((2, blocks)), pltpu.SemaphoreType.DMA((blocks,))]
    spread_sems = pltpu.SemaphoreType.DMA((2, count // 2))
    split = [(dim // count, mid_cols), (dim // count, last_cols), (taps // count, 4 * own)]
    mixed, mixed_peer, grad_rows, grad_peer, middle_share, last_share, conv_share = pl.pallas_call(
        functools.partial(later_kernel, heads, hd, two),
        grid_spec=pltpu.PrefetchScalarGridSpec(
            num_scalar_prefetch=1,
            grid=(2 * blocks,),
            in_specs=[front_rows, front_rows, inside, front_cols]
            + [inside] * 6
            + [left_cols] * 3
            + [back_rows, inside, back_cols, back_cols, back_cols, back_lse]
            + [anywhere] * 6,
            out_specs=[anywhere] * 4 + [whole(d) for d in out_dims],
            scratch_shapes=[
                pltpu.VMEM((peers, 3 * own, dim), BF16), pltpu.VMEM((peers, own, 2 * conv_cols), BF16),
                pltpu.VMEM((heads, groups, hd), BF16), pltpu.VMEM((width, groups), BF16),
                pltpu.VMEM((heads, groups, hd), BF16), pltpu.VMEM((width, groups), BF16),
                pltpu.VMEM((blocks, TB, dim), BF16),
                pltpu.VMEM((TB, peers * units), BF16), pltpu.VMEM((TB, peers * units), BF16),
                pltpu.VMEM((2, TB, step), F32), pltpu.VMEM((2, TB, step), F32),
                pltpu.VMEM((2, 2, dim, units), F32), pltpu.VMEM((2 * own, dim), F32), pltpu.VMEM((1, dim), F32),
                pltpu.VMEM((width, TB), BF16), pltpu.VMEM((blocks, heads, TB), F32),
                pltpu.VMEM((blocks, width, TB), BF16), pltpu.VMEM((blocks, TB, dim), BF16),
                pltpu.VMEM((blocks, heads, TB), F32),
                pltpu.VMEM((groups, GB), F32),
                pltpu.VMEM((2, heads, taps, hd), BF16), pltpu.VMEM((heads, groups, hd), F32),
                pltpu.VMEM((heads, groups, hd), F32), pltpu.VMEM((width, TB), F32),
                pltpu.VMEM((3 * width, TB), BF16), pltpu.VMEM((6 * own, dim), F32),
                pltpu.VMEM((two, taps, hd), F32), pltpu.VMEM((two, taps, hd), F32),
                pltpu.VMEM((1, dim), F32),
            ]
            + [pltpu.VMEM((*lead, *d), BF16) for d in split for lead in ((2, count // 2), (count // 2,), (count // 2,))]
            + [pltpu.VMEM((2, *d), BF16) for d in out_dims]
            + [pltpu.VMEM(d, F32) for d in split]
            + swap_sems * 2
            + [spread_sems] * 3
            + [pltpu.SemaphoreType.DMA((2, 3)), pltpu.SemaphoreType.DMA((6,))],
        ),
        out_shape=[jax.ShapeDtypeStruct((rows, dim), BF16)] * 4 + [jax.ShapeDtypeStruct(d, F32) for d in out_dims],
        compiler_params=pltpu.CompilerParams(
            vmem_limit_bytes=VMEM, dimension_semantics=("arbitrary",), collective_id=1, has_side_effects=True
        ),
        cost_estimate=cost(110),
        name="feed_forward_and_backward",
    )(
        lens, x, g, gain2, ctx, out_weight, up_weight, down_weight, out_far.reshape(width - own, dim), up_far, down_far,
        q, k, v, x, gain1, q, k, v, lse, w_all, conv_all, ck, ckt, cv, cvt,
    )

    share = dim // count
    own_conv = (own_heads, taps // count, hd)
    shapes = [
        ((1, share), F32), ((1, share), F32), ((share, own), F32), ((share, own), F32), ((share, own), F32),
        ((share, own), F32), (own_conv, F32), (own_conv, F32), ((share, units), F32), ((share, units), F32),
    ]
    lane_half = pl.BlockSpec((rows, 128), lambda c: (0, c))
    lane_all = pl.BlockSpec((2 * rows, 128), lambda c: (0, c))
    outs = pl.pallas_call(
        functools.partial(last_kernel, hd),
        grid=(dim // 128,),
        in_specs=[pl.BlockSpec(memory_space=pltpu.SMEM)] + [lane_half] * 4 + [whole(d) for d in out_dims],
        out_specs=[lane_all] * 2 + [whole(d) for d, _ in shapes],
        out_shape=[jax.ShapeDtypeStruct((2 * rows, dim), BF16)] * 2 + [jax.ShapeDtypeStruct(d, t) for d, t in shapes],
        scratch_shapes=[pltpu.VMEM((2 * rows, 128), F32)] * 2,
        compiler_params=params(),
        cost_estimate=cost(15),
        name="in_order",
    )(lens, mixed, mixed_peer, grad_rows, grad_peer, middle_share, last_share, conv_share)
    mixed, grad_tokens, gain1, gain2, query, key, value, out, kconv, vconv, up, down = outs
    return (
        mixed, grad_tokens, gain1.reshape(share), gain2.reshape(share), query, key, value, out.T,
        kconv, vconv, up, down.T,
    )


def solution(mesh):
    in_specs = (
        P("dp", None),
        P(),
        P(),
        P(None, "tensor"),
        P(None, "tensor"),
        P(None, "tensor"),
        P("tensor", None),
        P("tensor", None, None),
        P("tensor", None, None),
        P(None, "tensor"),
        P("tensor", None),
        P("dp"),
        P("dp", None),
        P("dp", None),
    )
    out_specs = (
        P("dp", None),
        P("dp", None),
        P("dp"),
        P("dp"),
        P("dp", "tensor"),
        P("dp", "tensor"),
        P("dp", "tensor"),
        P("tensor", "dp"),
        P("tensor", "dp", None),
        P("tensor", "dp", None),
        P("dp", "tensor"),
        P("tensor", "dp"),
    )
    return jax.shard_map(
        on_device, mesh=mesh, in_specs=in_specs, out_specs=out_specs, check_vma=False
    )
```

time: 201 us -> 189 us (0.940)
  Pallas kernels: 200 us -> 188 us
    pallas_call x1, Pallas kernels: 62.2 us -> 55.4 us  [on_device(): pl.pallas_call(functools.partial(forward_kernel, heads, hd), grid_spec=pl...]
    pallas_call x2 -> x1, Pallas kernels: 128 us -> 123 us  [on_device(): pl.pallas_call(functools.partial(later_kernel, heads, hd, two), grid_spec...]
where the time goes in v6:
time: 189 us
  Pallas kernels  188 us (99%)
    pallas_call x1, Pallas kernels, on_device(): pl.pallas_call(functools.partial(later_kernel, heads, hd, two), grid_spec...  123 us
    pallas_call x1, Pallas kernels, on_device(): pl.pallas_call(functools.partial(forward_kernel, heads, hd), grid_spec=pl...  55.4 us
    pallas_call x1, Pallas kernels, on_device(): pl.pallas_call(functools.partial(last_kernel, hd), grid=(dim // 128,), in...  9.45 us

profile of v6, /device:TPU:0, one launch (start us, length us, event | category | flops | bytes accessed | tf_op | source)
XLA Modules:
  0.0 188.8 jit_solution(8859026911801225332)
XLA Ops:
  0.6 55.4 %attention_forward.1 = (bf16[2304,512]{1,0:T(8,128)(2,1)}, bf16[2304,512]{1,0:T(8,128)(2,1)}, bf16[512,2304]{1,0:T(8,128)(2,1)}, bf16[512,2304]{1,0:T(8,128)(2,1...) custom-call(s32[6]{0:T(128)} %bitcast.17, ...), custom_call_target="tpu_custom_call" | custom-call | flops 54999998464 | bytes 1048576 | tf_op jit(solution)/shard_map/attention_forward/pallas_call | solution.py:803
  56.0 123.2 %feed_forward_and_backward.1 = (bf16[2304,512]{1,0:T(8,128)(2,1)}, bf16[2304,512]{1,0:T(8,128)(2,1)}, bf16[2304,512]{1,0:T(8,128)(2,1)}, bf16[2304,512]{1,0:T(8,...) custom-call(s32[6]{0:T(128)} %bitcast.18, bf16[2304,512]{1,0:T(8,128)(2,1)} %get-tuple-element.47.x_ref.x_back, ...), custom_call_target="tpu_custom_call" | custom-call | flops 109999996928 | bytes 1048576 | tf_op jit(solution)/shard_map/feed_forward_and_backward/pallas_call | solution.py:874
  179.2 9.4 %in_order.1 = (bf16[4608,512]{1,0:T(8,128)(2,1)}, bf16[4608,512]{1,0:T(8,128)(2,1)}, f32[1,64]{1,0:T(1,128)}, f32[1,64]{1,0:T(1,128)}, f32[64,128]{1,0:T(8,128)}...) custom-call(s32[6]{0:T(128)} %bitcast.19, ...), custom_call_target="tpu_custom_call" | custom-call | flops 15000000512 | bytes 1048576 | tf_op jit(solution)/shard_map/in_order/pallas_call | solution.py:929

commit v7 on v6

--- a/solution.py
+++ b/solution.py
@@ -128,11 +128,14 @@
     )
 
 
-def meet(devices):
+def greet(devices):
     barrier = pltpu.get_barrier_semaphore()
     for device in devices:
         pl.semaphore_signal(barrier, inc=1, device_id=device, device_id_type=pl.DeviceIdType.MESH)
-    pl.semaphore_wait(barrier, len(devices))
+
+
+def greeted(devices):
+    pl.semaphore_wait(pltpu.get_barrier_semaphore(), len(devices))
 
 
 def put_rows(ref, pieces, at=0):
@@ -316,9 +319,9 @@
 def forward_kernel(
     heads, hd, lens_ref, x_ref, g_ref, gain_ref, pad_ref, query_ref, key_ref, value_ref, kconv_ref, vconv_ref,
     out_ref, up_ref, down_ref,
-    x_own, g_own, q_ref, k_ref, v_ref, ctx_ref, lse_ref, ck_ref, ckt_ref, cv_ref, cvt_ref, w_all, conv_all,
+    q_ref, k_ref, v_ref, ctx_ref, lse_ref, x_all, g_all, ck_all, ckt_all, cv_all, cvt_all, w_all, conv_all,
     out_far, up_far, down_far,
-    xs, gs, first_all, mask_rows, w_ref, conv_ref, bias_ref, first_sems, last_sems, local_sems,
+    xs, gs, x_own, g_own, ck_ref, ckt_ref, cv_ref, cvt_ref, first_all, mask_rows, w_ref, conv_ref, bias_ref, first_sems, last_sems, local_sems,
 ):
     block = pl.program_id(0)
     blocks = pl.num_programs(0)
@@ -328,10 +331,9 @@
     conv_cols = conv_ref.shape[2] // 2
     first_gather = Gather((w_ref.at[0], conv_ref.at[0]), (w_ref.at[1:], conv_ref.at[1:]), first_sems)
     last_gather = Gather((out_ref, up_ref, down_ref), (out_far, up_far, down_far), last_sems)
-    keep_copies = [
-        pltpu.make_async_copy(w_ref, w_all, local_sems.at[0]), pltpu.make_async_copy(conv_ref, conv_all, local_sems.at[1])
-    ]
-
+    kept = ((w_ref, w_all), (conv_ref, conv_all), (x_own, x_all), (g_own, g_all))
+    kept += ((ck_ref, ck_all), (ckt_ref, ckt_all), (cv_ref, cv_all), (cvt_ref, cvt_all))
+    keep_copies = [pltpu.make_async_copy(src, dst, local_sems.at[n]) for n, (src, dst) in enumerate(kept)]
     half = x_ref.shape[0] // 2
     blocks_there = half // TB
     longest_here = lax.rem(lax.axis_index("tensor"), 2) == 0
@@ -339,13 +341,14 @@
 
     @pl.when(block == 0)
     def _():
+        greet(first_gather.devices())
         for n, src in enumerate((query_ref, key_ref, value_ref)):
             w_ref[0, n * own : (n + 1) * own, :] = src[...].T
         conv_ref[0] = jnp.zeros_like(conv_ref[0])
         for n, src in enumerate((kconv_ref, vconv_ref)):
             for h in range(own_heads):
                 conv_ref[0, h * hd : (h + 1) * hd, n * conv_cols : n * conv_cols + taps] = src[h]
-        meet(first_gather.devices())
+        greeted(first_gather.devices())
         first_gather.start()
         for src, dst in ((x_ref, xs), (g_ref, gs)):
             for c in range(dim // 128):
@@ -372,7 +375,7 @@
         lax.fori_loop(half // TB // 2, half // TB, prepare, 0)
         first_gather.arrive()
         first_gather.finish()
-        for copy in keep_copies:
+        for copy in keep_copies[:4]:
             copy.start()
 
     mask = mask_rows[block, 0:1]
@@ -394,6 +397,11 @@
             plain[h, rows, :] = comp.T.astype(BF16)
     places, starts = item_starts(lens_ref, block, longest_here, half // 3)
     lse_ref[heads:, :] = jnp.broadcast_to(mask, (lse_ref.shape[0] - heads, TB))
+
+    @pl.when(block == blocks - 1)
+    def _():
+        for copy in keep_copies[4:]:
+            copy.start()
 
     peers = w_ref.shape[0]
     for s in range(1, peers):
@@ -576,11 +584,11 @@
 
 def later_kernel(
     heads, hd, own_heads, lens_ref,
-    x_ref, g_ref, gain2_ref, ctx_ref, out_ref, up_ref, down_ref, out_far, up_far, down_far,
+    x_ref, g_ref, gain2_ref, ctx_ref, out_ref, up_ref, down_ref, out_far, up_hbm, down_hbm,
     q_front, k_front, v_front,
     x_back, gain1_ref, q_ref, k_ref, v_ref, lse_ref, w_hbm, conv_hbm, ck_hbm, ckt_hbm, cv_hbm, cvt_hbm,
     mixed_ref, mixed_peer, tokens_ref, tokens_peer, middle_out, last_out, conv_out,
-    w_ref, conv_ref, ck_ref, ckt_ref, cv_ref, cvt_ref,
+    up_far, down_far, w_ref, conv_ref, ck_ref, ckt_ref, cv_ref, cvt_ref,
     mixed_staged, acts, hidden_grads, pre, act_grads, ff_sum, out_sum, gain2_sum,
     ctx_block, lse_all, dctx_all, resid_all, delta_all,
     bias_ref, convs_ref, dck_sum, dcv_sum, dq_sum, dqkv, weight_sum, kconv_sum, vconv_sum, gain1_sum,
@@ -605,7 +613,7 @@
         pltpu.make_async_copy(src, dst, load_sems.at[n])
         for n, (src, dst) in enumerate(
             (
-                (w_hbm, w_ref), (conv_hbm, conv_ref), (ck_hbm, ck_ref), (ckt_hbm, ckt_ref), (cv_hbm, cv_ref),
+                (up_hbm, up_far), (down_hbm, down_far), (w_hbm, w_ref), (conv_hbm, conv_ref), (ck_hbm, ck_ref), (ckt_hbm, ckt_ref), (cv_hbm, cv_ref),
                 (cvt_hbm, cvt_ref),
             )
         )
@@ -617,16 +625,20 @@
             load.start()
         count = lax.axis_size("dp")
         me, peer = lax.axis_index("dp"), lax.axis_index("tensor")
-        meet([swap.device, (me ^ 1, peer)] + [(lax.rem(me + 2 * s, count), peer) for s in range(1, count // 2)])
-        for ref in (
-            ff_sum, out_sum, gain2_sum, dck_sum, dcv_sum, weight_sum, kconv_sum, vconv_sum, gain1_sum,
-        ):
+        devices = [swap.device, (me ^ 1, peer)] + [(lax.rem(me + 2 * s, count), peer) for s in range(1, count // 2)]
+        greet(devices)
+        for ref in (ff_sum, out_sum, gain2_sum):
             ref[...] = jnp.zeros_like(ref)
+        for load in loads[:2]:
+            load.wait()
+        greeted(devices)
 
     @pl.when(step_id == 2)
     def _():
-        for load in loads:
+        for load in loads[2:]:
             load.wait()
+        for ref in (dck_sum, dcv_sum, weight_sum, kconv_sum, vconv_sum, gain1_sum):
+            ref[...] = jnp.zeros_like(ref)
         for h in range(heads):
             slot, i = divmod(h, slot_heads)
             for n in range(2):
@@ -724,15 +736,20 @@
         a, b = mine[rows, :].astype(F32), theirs[rows, :].astype(F32)
         return jnp.where(longest_here == other, b, a)
 
+    parts = natural.shape[0]
     for block in range(half // TB):
         for r in range(3):
             others = taps(block, r, True)
-            for base in (0, half):
-                natural[pl.ds(base + block * TB + r, GB, stride=3), :] = others
+            for c in range(parts):
+                for base in (0, half):
+                    natural[c, pl.ds(base + block * TB + r, GB, stride=3), :] = others[:, c * 128 : (c + 1) * 128]
     for block in range(half // TB):
         for r in range(3):
-            natural[pl.ds(first + block * TB + r, GB, stride=3), :] = taps(block, r, False)
-    out_ref[...] = natural[...].astype(BF16)
+            longest = taps(block, r, False)
+            for c in range(parts):
+                natural[c, pl.ds(first + block * TB + r, GB, stride=3), :] = longest[:, c * 128 : (c + 1) * 128]
+    for c in range(parts):
+        out_ref[:, c * 128 : (c + 1) * 128] = natural[c].astype(BF16)
 
 
 def last_kernel(
@@ -800,31 +817,34 @@
     late_cols = pl.BlockSpec((width, TB), lambda b, *_: (0, jnp.maximum(b - early, 0)))
     anywhere = pl.BlockSpec(memory_space=pl.ANY)
     inside = pl.BlockSpec(memory_space=pltpu.VMEM)
-    x, g, q, k, v, ctx, lse, ck, ckt, cv, cvt, w_all, conv_all, out_far, up_far, down_far = pl.pallas_call(
+    q, k, v, ctx, lse, x, g, ck, ckt, cv, cvt, w_all, conv_all, out_far, up_far, down_far = pl.pallas_call(
         functools.partial(forward_kernel, heads, hd),
         grid_spec=pltpu.PrefetchScalarGridSpec(
             num_scalar_prefetch=1,
             grid=(blocks,),
             in_specs=[inside, inside, whole((1, dim))] + [inside] * 6 + [anywhere] * 3,
             out_specs=[
-                whole((rows, dim)), whole((rows, dim)), cols_spec, cols_spec, cols_spec, late_cols, lse_spec,
-                whole((heads, groups, hd)), whole((width, groups)), whole((heads, groups, hd)), whole((width, groups)),
-                anywhere, anywhere, anywhere, anywhere, anywhere,
-            ],
+                cols_spec, cols_spec, cols_spec, late_cols, lse_spec,
+            ]
+            + [anywhere] * 11,
             scratch_shapes=[
                 pltpu.VMEM((dim // 128 + 1, 2 * rows, 128), F32), pltpu.VMEM((dim // 128, 2 * rows, 128), F32),
+                pltpu.VMEM((rows, dim), BF16), pltpu.VMEM((rows, dim), BF16),
+                pltpu.VMEM((heads, groups, hd), BF16), pltpu.VMEM((width, groups), BF16),
+                pltpu.VMEM((heads, groups, hd), BF16), pltpu.VMEM((width, groups), BF16),
                 pltpu.VMEM((blocks, TB, dim), BF16), pltpu.VMEM((blocks, 8, TB), F32),
                 pltpu.VMEM((peers, 3 * own, dim), BF16), pltpu.VMEM((peers, own, 2 * conv_cols), BF16),
                 pltpu.VMEM((groups, GB), F32),
                 pltpu.SemaphoreType.DMA((2, 2, 5, peers - 1)), pltpu.SemaphoreType.DMA((2, 3, 5, peers - 1)),
-                pltpu.SemaphoreType.DMA((2,)),
+                pltpu.SemaphoreType.DMA((8,)),
             ],
         ),
-        out_shape=[jax.ShapeDtypeStruct((rows, dim), BF16)] * 2
-        + [jax.ShapeDtypeStruct((width, rows), BF16)] * 3
-        + [jax.ShapeDtypeStruct((width, (blocks - early) * TB), BF16)]
+        out_shape=[jax.ShapeDtypeStruct((width, rows), BF16)] * 3
         + [
+            jax.ShapeDtypeStruct((width, (blocks - early) * TB), BF16),
             jax.ShapeDtypeStruct((stats, rows), F32),
+            jax.ShapeDtypeStruct((rows, dim), BF16),
+            jax.ShapeDtypeStruct((rows, dim), BF16),
             jax.ShapeDtypeStruct((heads, groups, hd), BF16),
             jax.ShapeDtypeStruct((width, groups), BF16),
             jax.ShapeDtypeStruct((heads, groups, hd), BF16),
@@ -877,12 +897,14 @@
             num_scalar_prefetch=1,
             grid=(2 * blocks,),
             in_specs=[front_rows, front_rows, inside, front_cols]
-            + [inside] * 6
+            + [inside] * 4
+            + [anywhere] * 2
             + [left_cols] * 3
             + [back_rows, inside, back_cols, back_cols, back_cols, back_lse]
             + [anywhere] * 6,
             out_specs=[anywhere] * 4 + [whole(d) for d in out_dims],
             scratch_shapes=[
+                pltpu.VMEM((peers - 1, dim, units), BF16), pltpu.VMEM((peers - 1, units, dim), BF16),
                 pltpu.VMEM((peers, 3 * own, dim), BF16), pltpu.VMEM((peers, own, 2 * conv_cols), BF16),
                 pltpu.VMEM((heads, groups, hd), BF16), pltpu.VMEM((width, groups), BF16),
                 pltpu.VMEM((heads, groups, hd), BF16), pltpu.VMEM((width, groups), BF16),
@@ -905,7 +927,7 @@
             + [pltpu.VMEM(d, F32) for d in split]
             + swap_sems * 2
             + [spread_sems] * 3
-            + [pltpu.SemaphoreType.DMA((2, 3)), pltpu.SemaphoreType.DMA((6,))],
+            + [pltpu.SemaphoreType.DMA((2, 3)), pltpu.SemaphoreType.DMA((8,))],
         ),
         out_shape=[jax.ShapeDtypeStruct((rows, dim), BF16)] * 4 + [jax.ShapeDtypeStruct(d, F32) for d in out_dims],
         compiler_params=pltpu.CompilerParams(
@@ -924,15 +946,16 @@
         ((1, share), F32), ((1, share), F32), ((share, own), F32), ((share, own), F32), ((share, own), F32),
         ((share, own), F32), (own_conv, F32), (own_conv, F32), ((share, units), F32), ((share, units), F32),
     ]
-    lane_half = pl.BlockSpec((rows, 128), lambda c: (0, c))
-    lane_all = pl.BlockSpec((2 * rows, 128), lambda c: (0, c))
+    lanes = 256
+    lane_half = pl.BlockSpec((rows, lanes), lambda c: (0, c))
+    lane_all = pl.BlockSpec((2 * rows, lanes), lambda c: (0, c))
     outs = pl.pallas_call(
         functools.partial(last_kernel, hd),
-        grid=(dim // 128,),
+        grid=(dim // lanes,),
         in_specs=[pl.BlockSpec(memory_space=pltpu.SMEM)] + [lane_half] * 4 + [whole(d) for d in out_dims],
         out_specs=[lane_all] * 2 + [whole(d) for d, _ in shapes],
         out_shape=[jax.ShapeDtypeStruct((2 * rows, dim), BF16)] * 2 + [jax.ShapeDtypeStruct(d, t) for d, t in shapes],
-        scratch_shapes=[pltpu.VMEM((2 * rows, 128), F32)] * 2,
+        scratch_shapes=[pltpu.VMEM((lanes // 128, 2 * rows, 128), F32)] * 2,
         compiler_params=params(),
         cost_estimate=cost(15),
         name="in_order",

time: 189 us -> 185 us (0.979)
  Pallas kernels: 188 us -> 184 us
    pallas_call x1, Pallas kernels: 55.4 us -> 52.6 us  [on_device(): pl.pallas_call(functools.partial(forward_kernel, heads, hd), grid_spec=pl...]
where the time goes in v7:
time: 185 us; the launch traced here: 184 us
  Pallas kernels  184 us (99%)
    pallas_call x1, Pallas kernels, on_device(): pl.pallas_call(functools.partial(later_kernel, heads, hd, two), grid_spec...  122 us
    pallas_call x1, Pallas kernels, on_device(): pl.pallas_call(functools.partial(forward_kernel, heads, hd), grid_spec=pl...  52.6 us
    pallas_call x1, Pallas kernels, on_device(): pl.pallas_call(functools.partial(last_kernel, hd), grid=(dim // lanes,),...  8.51 us

profile of v7, /device:TPU:0, one launch (start us, length us, event | category | flops | bytes accessed | tf_op | source)
XLA Modules:
  0.0 184.4 jit_solution(1953860357262885726)
XLA Ops:
  0.6 52.6 %attention_forward.1 = (bf16[512,2304]{1,0:T(8,128)(2,1)}, bf16[512,2304]{1,0:T(8,128)(2,1)}, bf16[512,2304]{1,0:T(8,128)(2,1)}, bf16[512,1152]{1,0:T(8,128)(2,1...) custom-call(s32[6]{0:T(128)} %bitcast.17, ...), custom_call_target="tpu_custom_call" | custom-call | flops 54999998464 | bytes 1048576 | tf_op jit(solution)/shard_map/attention_forward/pallas_call | solution.py:820
  53.2 122.5 %feed_forward_and_backward.1 = (bf16[2304,512]{1,0:T(8,128)(2,1)}, bf16[2304,512]{1,0:T(8,128)(2,1)}, bf16[2304,512]{1,0:T(8,128)(2,1)}, bf16[2304,512]{1,0:T(8,...) custom-call(s32[6]{0:T(128)} %bitcast.18, bf16[2304,512]{1,0:T(8,128)(2,1)} %get-tuple-element.47.x_ref.x_back, ...), custom_call_target="tpu_custom_call" | custom-call | flops 109999996928 | bytes 1048576 | tf_op jit(solution)/shard_map/feed_forward_and_backward/pallas_call | solution.py:894
  175.7 8.5 %in_order.1 = (bf16[4608,512]{1,0:T(8,128)(2,1)}, bf16[4608,512]{1,0:T(8,128)(2,1)}, f32[1,64]{1,0:T(1,128)}, f32[1,64]{1,0:T(1,128)}, f32[64,128]{1,0:T(8,128)}...) custom-call(s32[6]{0:T(128)} %bitcast.19, ...), custom_call_target="tpu_custom_call" | custom-call | flops 15000000512 | bytes 1048576 | tf_op jit(solution)/shard_map/in_order/pallas_call | solution.py:952

commit v8 on v7

--- a/solution.py
+++ b/solution.py
@@ -85,8 +85,7 @@
     return 3 * first
 
 
-def own_taps(source, block, first, longest_here):
-    half = source.shape[1] // 2
+def own_taps(source, half, block, first, longest_here):
     base = block * TB
     parts = []
     for c in range(source.shape[0]):
@@ -352,7 +351,7 @@
         first_gather.start()
         for src, dst in ((x_ref, xs), (g_ref, gs)):
             for c in range(dim // 128):
-                dst[c] = src[:, c * 128 : (c + 1) * 128].astype(F32)
+                dst[c, 0 : 2 * half, :] = src[:, c * 128 : (c + 1) * 128].astype(F32)
         pads = pad_ref[...].astype(F32).T
         for c in range(pads.shape[1]):
             xs[dim // 128, c * 128 : (c + 1) * 128, :] = jnp.broadcast_to(pads[:, c : c + 1], (128, 128))
@@ -360,14 +359,14 @@
         last_gather.start()
 
         def prepare(n, carry):
-            x = own_taps(xs, n, first, longest_here)
+            x = own_taps(xs, half, n, first, longest_here)
             mask_rows[n] = jnp.broadcast_to(x[:, dim:].T[0:1], mask_rows.shape[1:])
             x = x[:, :dim]
             normed, _ = norm_rows(x)
             first_all[n] = (normed * gain_ref[...]).astype(BF16)
             rows = pl.ds(pl.multiple_of(n * TB, TB), TB)
             x_own[rows, :] = x.astype(BF16)
-            g_own[rows, :] = own_taps(gs, n, first, longest_here).astype(BF16)
+            g_own[rows, :] = own_taps(gs, half, n, first, longest_here).astype(BF16)
             return carry
 
         lax.fori_loop(0, half // TB // 2, prepare, 0)
@@ -712,11 +711,13 @@
             ],
         )
         convs.start()
+        turn(0, middle_turn, middle.total())
         last.pass_on()
         convs.pass_on()
         sums = ((middle_out, middle_turn, middle), (last_out, last_turn, last), (conv_out, conv_turn, convs))
         for n, (_, ref, spread) in enumerate(sums):
-            turn(n, ref, spread.total())
+            if n > 0:
+                turn(n, ref, spread.total())
         for n, (out, ref, spread) in enumerate(sums):
             turned(n, ref).wait()
             total, cols = spread.sums, out.shape[1]
@@ -749,7 +750,7 @@
             for c in range(parts):
                 natural[c, pl.ds(first + block * TB + r, GB, stride=3), :] = longest[:, c * 128 : (c + 1) * 128]
     for c in range(parts):
-        out_ref[:, c * 128 : (c + 1) * 128] = natural[c].astype(BF16)
+        out_ref[:, c * 128 : (c + 1) * 128] = natural[c, 0 : 2 * half, :].astype(BF16)
 
 
 def last_kernel(
@@ -828,7 +829,7 @@
             ]
             + [anywhere] * 11,
             scratch_shapes=[
-                pltpu.VMEM((dim // 128 + 1, 2 * rows, 128), F32), pltpu.VMEM((dim // 128, 2 * rows, 128), F32),
+                pltpu.VMEM((dim // 128 + 1, 2 * rows + 8, 128), F32), pltpu.VMEM((dim // 128, 2 * rows + 8, 128), F32),
                 pltpu.VMEM((rows, dim), BF16), pltpu.VMEM((rows, dim), BF16),
                 pltpu.VMEM((heads, groups, hd), BF16), pltpu.VMEM((width, groups), BF16),
                 pltpu.VMEM((heads, groups, hd), BF16), pltpu.VMEM((width, groups), BF16),
@@ -955,7 +956,7 @@
         in_specs=[pl.BlockSpec(memory_space=pltpu.SMEM)] + [lane_half] * 4 + [whole(d) for d in out_dims],
         out_specs=[lane_all] * 2 + [whole(d) for d, _ in shapes],
         out_shape=[jax.ShapeDtypeStruct((2 * rows, dim), BF16)] * 2 + [jax.ShapeDtypeStruct(d, t) for d, t in shapes],
-        scratch_shapes=[pltpu.VMEM((lanes // 128, 2 * rows, 128), F32)] * 2,
+        scratch_shapes=[pltpu.VMEM((lanes // 128, 2 * rows + 8, 128), F32)] * 2,
         compiler_params=params(),
         cost_estimate=cost(15),
         name="in_order",

time: 185 us -> 184 us (level)
  no operation moved by 1% of the time
where the time goes in v8:
time: 184 us
  Pallas kernels  183 us (99%)
    pallas_call x1, Pallas kernels, on_device(): pl.pallas_call(functools.partial(later_kernel, heads, hd, two), grid_spec...  122 us
    pallas_call x1, Pallas kernels, on_device(): pl.pallas_call(functools.partial(forward_kernel, heads, hd), grid_spec=pl...  52.4 us
    pallas_call x1, Pallas kernels, on_device(): pl.pallas_call(functools.partial(last_kernel, hd), grid=(dim // lanes,),...  8.51 us

profile of v8, /device:TPU:0, one launch (start us, length us, event | category | flops | bytes accessed | tf_op | source)
XLA Modules:
  0.0 184.2 jit_solution(14475982384864916852)
XLA Ops:
  0.6 52.4 %attention_forward.1 = (bf16[512,2304]{1,0:T(8,128)(2,1)}, bf16[512,2304]{1,0:T(8,128)(2,1)}, bf16[512,2304]{1,0:T(8,128)(2,1)}, bf16[512,1152]{1,0:T(8,128)(2,1...) custom-call(s32[6]{0:T(128)} %bitcast.17, ...), custom_call_target="tpu_custom_call" | custom-call | flops 54999998464 | bytes 1048576 | tf_op jit(solution)/shard_map/attention_forward/pallas_call | solution.py:821
  53.1 122.5 %feed_forward_and_backward.1 = (bf16[2304,512]{1,0:T(8,128)(2,1)}, bf16[2304,512]{1,0:T(8,128)(2,1)}, bf16[2304,512]{1,0:T(8,128)(2,1)}, bf16[2304,512]{1,0:T(8,...) custom-call(s32[6]{0:T(128)} %bitcast.18, bf16[2304,512]{1,0:T(8,128)(2,1)} %get-tuple-element.47.x_ref.x_back, ...), custom_call_target="tpu_custom_call" | custom-call | flops 109999996928 | bytes 1048576 | tf_op jit(solution)/shard_map/feed_forward_and_backward/pallas_call | solution.py:895
  175.5 8.5 %in_order.1 = (bf16[4608,512]{1,0:T(8,128)(2,1)}, bf16[4608,512]{1,0:T(8,128)(2,1)}, f32[1,64]{1,0:T(1,128)}, f32[1,64]{1,0:T(1,128)}, f32[64,128]{1,0:T(8,128)}...) custom-call(s32[6]{0:T(128)} %bitcast.19, ...), custom_call_target="tpu_custom_call" | custom-call | flops 15000000512 | bytes 1048576 | tf_op jit(solution)/shard_map/in_order/pallas_call | solution.py:953

commit v9 on v8

--- a/solution.py
+++ b/solution.py
@@ -534,6 +534,7 @@
         pl.when(block == n)(functools.partial(attend, n + 1))
     mask = stats_ref[heads : heads + 1, :]
     rows = key_rows(block)
+    later = []
     for h in range(heads):
         band = slice(h * hd, (h + 1) * hd)
         one = slice(h, h + 1)
@@ -557,15 +558,17 @@
             dqkv[at : at + hd, :] = ((spread + beside) * mask).astype(BF16)
             if h < own_heads:
                 grouped = jnp.concatenate([src[band, r * GB : (r + 1) * GB] for r in range(3)], axis=0)
-                total[h] += nn(grouped, grad)
+                later.append((total, h, grouped, grad))
     hat, inv_std = norm_rows(x_ref[...].astype(F32))
     gain = gain_ref[...]
     first_in = (hat * gain).astype(BF16)
-    weight_sum[...] += nn(dqkv[0 : 3 * own, :], first_in)
     back = tn(dqkv[...], w_ref[...].reshape(slots * 3 * lanes, dim))
-    gain_sum[...] += jnp.sum(back * hat, axis=0, keepdims=True)
     total = resid_all[block].astype(F32) + norm_back(back, gain, hat, inv_std)
     swap.send(block, total.astype(BF16))
+    gain_sum[...] += jnp.sum(back * hat, axis=0, keepdims=True)
+    weight_sum[...] += nn(dqkv[0 : 3 * own, :], first_in)
+    for into, h, grouped, grad in later:
+        into[h] += nn(grouped, grad)
 
 
 def schedule(step, blocks):

time: 184 us -> 184 us (level)
  no operation moved by 1% of the time
where the time goes in v9:
time: 184 us
  Pallas kernels  183 us (99%)
    pallas_call x1, Pallas kernels, on_device(): pl.pallas_call(functools.partial(later_kernel, heads, hd, two), grid_spec...  122 us
    pallas_call x1, Pallas kernels, on_device(): pl.pallas_call(functools.partial(forward_kernel, heads, hd), grid_spec=pl...  52.4 us
    pallas_call x1, Pallas kernels, on_device(): pl.pallas_call(functools.partial(last_kernel, hd), grid=(dim // lanes,),...  8.51 us

profile of v9, /device:TPU:0, one launch (start us, length us, event | category | flops | bytes accessed | tf_op | source)
XLA Modules:
  0.0 184.1 jit_solution(17003505143494873316)
XLA Ops:
  0.6 52.4 %attention_forward.1 = (bf16[512,2304]{1,0:T(8,128)(2,1)}, bf16[512,2304]{1,0:T(8,128)(2,1)}, bf16[512,2304]{1,0:T(8,128)(2,1)}, bf16[512,1152]{1,0:T(8,128)(2,1...) custom-call(s32[6]{0:T(128)} %bitcast.17, ...), custom_call_target="tpu_custom_call" | custom-call | flops 54999998464 | bytes 1048576 | tf_op jit(solution)/shard_map/attention_forward/pallas_call | solution.py:824
  53.1 122.4 %feed_forward_and_backward.1 = (bf16[2304,512]{1,0:T(8,128)(2,1)}, bf16[2304,512]{1,0:T(8,128)(2,1)}, bf16[2304,512]{1,0:T(8,128)(2,1)}, bf16[2304,512]{1,0:T(8,...) custom-call(s32[6]{0:T(128)} %bitcast.18, bf16[2304,512]{1,0:T(8,128)(2,1)} %get-tuple-element.47.x_ref.x_back, ...), custom_call_target="tpu_custom_call" | custom-call | flops 109999996928 | bytes 1048576 | tf_op jit(solution)/shard_map/feed_forward_and_backward/pallas_call | solution.py:898
  175.5 8.5 %in_order.1 = (bf16[4608,512]{1,0:T(8,128)(2,1)}, bf16[4608,512]{1,0:T(8,128)(2,1)}, f32[1,64]{1,0:T(1,128)}, f32[1,64]{1,0:T(1,128)}, f32[64,128]{1,0:T(8,128)}...) custom-call(s32[6]{0:T(128)} %bitcast.19, ...), custom_call_target="tpu_custom_call" | custom-call | flops 15000000512 | bytes 1048576 | tf_op jit(solution)/shard_map/in_order/pallas_call | solution.py:956
